TPU v7x, 32 devices: a whole 2x2x4 slice. The times are simulated.
32 devices in a mesh: lists: 4 (over z), seq: 8 (over y, x, core).
Axes of the slice: x: 2, y: 2, z: 4, core: 2. Of those that a mesh axis runs over, the one named last changes fastest.
Arguments:
- queries: bfloat16 [24576, 2048], P(('lists', 'seq')), parts along dimension 0, may hold values from -6 to 6
- key_rows: bfloat16 [24576, 2048], P(('lists', 'seq')), parts along dimension 0, may hold values from -6 to 6
- value_rows: bfloat16 [24576, 2048], P(('lists', 'seq')), parts along dimension 0, may hold values from -6 to 6
- out_grad: bfloat16 [24576, 2048], P(('lists', 'seq')), parts along dimension 0, may hold values from -6 to 6
Outputs:
- query_grad: bfloat16 [24576, 2048], P(('lists', 'seq')), parts along dimension 0
- key_grad: bfloat16 [24576, 2048], P(('lists', 'seq')), parts along dimension 0
- content_derivative: bfloat16 [24576, 2048], P(('lists', 'seq')), parts along dimension 0
There are 4 independent parts, one for each index of `lists`. A program takes and returns all parts, laid end to end along the dimension named above; each array names one. Nothing has to cross between parts.
All inputs are finite; a program needn't handle non-finite values.
Results may differ from a plain program's by a relative error of at most 0.0049.
Values sent between devices are 32-bit elements; how exact they have to be, the bound alone decides.
No kernel may reach another device: no remote copies, remote signals or barrier semaphores. Data moves between devices by JAX's collectives and lax.ppermute only.
A program may use at most 192 MiB of HBM per device.

v0:
```python
import jax
import jax.numpy as jnp
from jax import lax
from jax.sharding import PartitionSpec as P

HEADS = 16
HEAD_DIM = 128


def carried_in(part, axis, combine, identity, reverse):
    count = lax.axis_size(axis)
    place = lax.axis_index(axis)
    ahead = count - 1 - place if reverse else place
    gathered = lax.all_gather(part, axis)
    state = jnp.zeros_like(part) + jnp.asarray(identity, part.dtype)

    def one(turn, state):
        source = count - 1 - turn if reverse else turn
        return combine(state, lax.dynamic_index_in_dim(gathered, source, 0, False))

    return lax.fori_loop(0, ahead, one, state)


def add_states(earlier, later_state):
    return earlier + later_state


def on_device(queries, key_rows, value_rows, out_grad):
    rows = queries.shape[0]
    length = rows * lax.axis_size("seq")
    scale_factor = (HEAD_DIM * length) ** (-0.5)
    shape3 = (rows, HEADS, HEAD_DIM)
    query_token_rows = queries.reshape(shape3)
    lookup_per_position = key_rows.reshape(shape3)
    content_per_position = value_rows.reshape(shape3)
    gradient_token_rows = out_grad.reshape(shape3)
    key_value_sum = jnp.einsum(
        "mjw,mjf->jwf",
        lookup_per_position,
        content_per_position,
        preferred_element_type=jnp.float32,
    )
    query_output_sum = jnp.einsum(
        "axo,axu->xou", query_token_rows, gradient_token_rows, preferred_element_type=jnp.float32
    )
    zero_state = jnp.zeros((HEADS, HEAD_DIM, HEAD_DIM), jnp.float32)
    cumulative_leading = carried_in(key_value_sum, "seq", add_states, zero_state, False)
    suffix = carried_in(query_output_sum, "seq", add_states, zero_state, True)
    prefix_halves = cumulative_leading.astype(jnp.bfloat16)
    suffix_halves = suffix.astype(jnp.bfloat16)
    counter = jnp.arange(rows, dtype=jnp.int32)
    causal = (counter[:, None] >= counter[None, :])[None]
    scores = jnp.einsum(
        "thk,shk->hts", query_token_rows, lookup_per_position, preferred_element_type=jnp.float32
    )
    forward_weight_matrix = jnp.where(causal, scale_factor * scores, 0.0).astype(jnp.bfloat16)
    products = jnp.einsum(
        "thv,shv->hts",
        gradient_token_rows,
        content_per_position,
        preferred_element_type=jnp.float32,
    )
    weight_gradients = jnp.where(causal, scale_factor * products, 0.0).astype(jnp.bfloat16)
    query_portion = jnp.einsum(
        "ynv,vyq->nyq", weight_gradients, lookup_per_position, preferred_element_type=jnp.float32
    )
    query_portion = query_portion + scale_factor * jnp.einsum(
        "aro,rbo->arb", gradient_token_rows, prefix_halves, preferred_element_type=jnp.float32
    )
    key_portion = jnp.einsum(
        "eca,ceo->aeo", weight_gradients, query_token_rows, preferred_element_type=jnp.float32
    )
    key_portion = key_portion + scale_factor * jnp.einsum(
        "jan,aon->jao", content_per_position, suffix_halves, preferred_element_type=jnp.float32
    )
    value_portion = jnp.einsum(
        "uno,nud->oud",
        forward_weight_matrix,
        gradient_token_rows,
        preferred_element_type=jnp.float32,
    )
    value_portion = value_portion + scale_factor * jnp.einsum(
        "nam,amx->nax", lookup_per_position, suffix_halves, preferred_element_type=jnp.float32
    )
    flat = (rows, HEADS * HEAD_DIM)
    return (
        query_portion.astype(jnp.bfloat16).reshape(flat),
        key_portion.astype(jnp.bfloat16).reshape(flat),
        value_portion.astype(jnp.bfloat16).reshape(flat),
    )


def solution(mesh):
    placed = (
        P(("lists", "seq"), None),
        P(("lists", "seq"), None),
        P(("lists", "seq"), None),
        P(("lists", "seq"), None),
    )
    return jax.shard_map(
        on_device,
        mesh=mesh,
        in_specs=placed,
        out_specs=(P(("lists", "seq"), None), P(("lists", "seq"), None), P(("lists", "seq"), None)),
        check_vma=False,
    )
```

profile of v0, /device:TPU:0, one launch (start us, length us, event | category | flops | bytes accessed | tf_op | source)
XLA Modules:
  0.0 175.5 jit_solution(18369785466371770407)
XLA Ops:
  7.2 0.0 copy-start
  7.2 0.0 all-gather.5.cloned.1.call-start
  7.2 1.8 %copy-done = bf16[768,2048]{1,0:T(8,128)(2,1)S(1)} copy-done((bf16[768,2048]{1,0:T(8,128)(2,1)S(1)}, bf16[768,2048]{1,0:T(8,128)(2,1)}, u32[]{:S(2)}) %copy-start) | copy-done | bytes 3145752
  9.1 4.2 %fusion.17 = f32[16,128,128]{2,1,0:T(8,128)} fusion(bf16[768,2048]{1,0:T(8,128)(2,1)S(1)} %copy-done, bf16[768,2048]{1,0:T(8,128)(2,1)} %param.9), kind=kOutput, calls=%fused_computation.21 | convolution fusion | flops 402653184 | bytes 7340032 | tf_op jit(solution)/shard_map/mjw,mjf->jwf/dot_general | solution.py:37
  13.3 0.0 all-gather.5.cloned.1.call-update
  13.3 0.0 all-gather.7.cloned.1.call-start
  13.4 4.6 %copy.41 = bf16[768,2048]{0,1:T(8,128)(2,1)} copy(bf16[768,2048]{1,0:T(8,128)(2,1)} %param.11) | data formatting | bytes 6291456 | tf_op jit(solution)/shard_map/reshape | solution.py:36
  18.0 4.9 %fusion.9 = f32[16,128,128]{2,1,0:T(8,128)} fusion(bf16[768,16,128]{0,2,1:T(8,128)(2,1)} %bitcast.102, bf16[768,2048]{1,0:T(8,128)(2,1)} %param.8), kind=kOutput, calls=%fused_computation.15 | convolution fusion | flops 402653184 | bytes 7340032 | tf_op jit(solution)/shard_map/axo,axu->xou/dot_general | solution.py:43
  22.9 0.0 all-gather.7.cloned.1.call-update
  22.9 1.0 iota_compare_fusion
  23.9 12.1 %select_convert_fusion.1 = bf16[16,768,768]{2,1,0:T(8,128)(2,1)} fusion(pred[768,768]{1,0:T(8,128)(4,1)} %iota_compare_fusion, bf16[768,16,128]{0,2,1:T(8,128)(2,1)} %bitcast.103, bf16[768,2048]{1,0:T(8,128)(2,1)S(1)} %copy-done), kind=kOutput, calls=%fused_computation.3 | convolution fusion | flops 2444230656 | bytes 25755648 | tf_op jit(solution)/shard_map/thv,shv->hts/dot_general | solution.py:57
  36.0 12.7 %fusion.11 = f32[16,768,128]{1,2,0:T(8,128)} fusion(bf16[16,768,768]{2,1,0:T(8,128)(2,1)} %select_convert_fusion.1, bf16[768,2048]{1,0:T(8,128)(2,1)} %param.8), kind=kOutput, calls=%fused_computation.17 | convolution fusion | flops 2415919104 | bytes 28311552 | tf_op jit(solution)/shard_map/eca,ceo->aeo/dot_general | solution.py:70
  48.7 12.8 %fusion.19 = f32[16,768,128]{1,2,0:T(8,128)} fusion(bf16[16,768,768]{2,1,0:T(8,128)(2,1)} %select_convert_fusion.1, bf16[768,2048]{1,0:T(8,128)(2,1)} %param.9), kind=kOutput, calls=%fused_computation.23 | convolution fusion | flops 2415919104 | bytes 28311552 | tf_op jit(solution)/shard_map/ynv,vyq->nyq/dot_general | solution.py:64
  61.5 12.4 %fusion = f32[16,768,128]{1,2,0:T(8,128)} fusion(bf16[768,16,128]{0,2,1:T(8,128)(2,1)} %bitcast.104, pred[768,768]{1,0:T(8,128)(4,1)} %iota_compare_fusion, bf16[768,2048]{1,0:T(8,128)(2,1)} %param.8, bf16[768,2048]{1,0:T(8,128)(2,1)} %param.9), kind=kOutput, calls=%fused_computation.4 | convolution fusion | flops 4860149760 | bytes 16318464 | tf_op jit(solution)/shard_map/uno,nud->oud/dot_general | solution.py:76
  73.9 0.0 all-gather.5.cloned.1.call-done
  73.9 1.1 broadcast_in_dim.26.clone
  75.0 6.8 %fusion.8 = bf16[768,16,128]{0,2,1:T(8,128)(2,1)} fusion(f32[16,768,128]{1,2,0:T(8,128)} %fusion.19, bf16[768,16,128]{0,2,1:T(8,128)(2,1)} %bitcast.105, f32[16,128,128]{2,1,0:T(8,128)} %get-tuple-element.82), kind=kOutput, calls=%fused_computation.14 | convolution fusion | flops 407633920 | bytes 13631488 | tf_op jit(solution)/shard_map/aro,rbo->arb/dot_general | solution.py:67
  81.7 4.7 %copy.36 = bf16[768,2048]{1,0:T(8,128)(2,1)} copy(bf16[768,2048]{0,1:T(8,128)(2,1)} %bitcast.106) | data formatting | bytes 6291456
  86.4 40.5 %all-gather.7.cloned.1.call-done = f32[128,128,128]{2,1,0:T(8,128)} async-done(((f32[16,128,128]{2,1,0:T(8,128)}), f32[128,128,128]{2,1,0:T(8,128)}) %all-gather.7.cloned.1.call-update) | async-done | bytes 8388624 | tf_op jit(solution)/shard_map/all_gather | solution.py:14
  126.9 1.1 broadcast_in_dim.26.clone.1
  128.0 18.6 %while.23 = (s32[]{:T(128)}, f32[16,128,128]{2,1,0:T(8,128)}, s32[]{:T(128)}, f32[8,16,128,128]{3,2,1,0:T(8,128)}, s32[]{:T(128)}, /*index=5*/s32[]{:T(128)}, s32[]{:T(128)}, s32[]{:T(128)}) while((s32[]{:T(128)}, f32[16,128,128]{2,1,0:T(8,128)}, s32[]{:T(128)}, f32[8,16,128,128]{3,2,1,0:T(8,128)}, s32[]{:T(128)}, /*index=5*/s32[]{:T(128)}, ...), condition=%wide.region_3.4_spmd, body=%wide.region_2.3_spmd.sunk | while | flops 262150 | bytes 3145871 | solution.py:21
  128.0 2.7 %bitcast_add_fusion.8 = f32[16,128,128]{2,1,0:T(8,128)} fusion(f32[16,128,128]{2,1,0:T(8,128)} %get-tuple-element.188, f32[8,16,128,128]{3,2,1,0:T(8,128)} %get-tuple-element.198, s32[]{:T(128)S(6)} %select_n.26), kind=kLoop, calls=%fused_computation.1.clone.1 | loop fusion | flops 262144 | bytes 3145732 | tf_op jit(solution)/shard_map/while/body/add | solution.py:25
  130.6 2.7 %bitcast_add_fusion.8 = f32[16,128,128]{2,1,0:T(8,128)} fusion(f32[16,128,128]{2,1,0:T(8,128)} %get-tuple-element.188, f32[8,16,128,128]{3,2,1,0:T(8,128)} %get-tuple-element.198, s32[]{:T(128)S(6)} %select_n.26), kind=kLoop, calls=%fused_computation.1.clone.1 | loop fusion | flops 262144 | bytes 3145732 | tf_op jit(solution)/shard_map/while/body/add | solution.py:25
  133.3 2.7 %bitcast_add_fusion.8 = f32[16,128,128]{2,1,0:T(8,128)} fusion(f32[16,128,128]{2,1,0:T(8,128)} %get-tuple-element.188, f32[8,16,128,128]{3,2,1,0:T(8,128)} %get-tuple-element.198, s32[]{:T(128)S(6)} %select_n.26), kind=kLoop, calls=%fused_computation.1.clone.1 | loop fusion | flops 262144 | bytes 3145732 | tf_op jit(solution)/shard_map/while/body/add | solution.py:25
  135.9 2.7 %bitcast_add_fusion.8 = f32[16,128,128]{2,1,0:T(8,128)} fusion(f32[16,128,128]{2,1,0:T(8,128)} %get-tuple-element.188, f32[8,16,128,128]{3,2,1,0:T(8,128)} %get-tuple-element.198, s32[]{:T(128)S(6)} %select_n.26), kind=kLoop, calls=%fused_computation.1.clone.1 | loop fusion | flops 262144 | bytes 3145732 | tf_op jit(solution)/shard_map/while/body/add | solution.py:25
  138.6 2.7 %bitcast_add_fusion.8 = f32[16,128,128]{2,1,0:T(8,128)} fusion(f32[16,128,128]{2,1,0:T(8,128)} %get-tuple-element.188, f32[8,16,128,128]{3,2,1,0:T(8,128)} %get-tuple-element.198, s32[]{:T(128)S(6)} %select_n.26), kind=kLoop, calls=%fused_computation.1.clone.1 | loop fusion | flops 262144 | bytes 3145732 | tf_op jit(solution)/shard_map/while/body/add | solution.py:25
  141.3 2.7 %bitcast_add_fusion.8 = f32[16,128,128]{2,1,0:T(8,128)} fusion(f32[16,128,128]{2,1,0:T(8,128)} %get-tuple-element.188, f32[8,16,128,128]{3,2,1,0:T(8,128)} %get-tuple-element.198, s32[]{:T(128)S(6)} %select_n.26), kind=kLoop, calls=%fused_computation.1.clone.1 | loop fusion | flops 262144 | bytes 3145732 | tf_op jit(solution)/shard_map/while/body/add | solution.py:25
  143.9 2.7 %bitcast_add_fusion.8 = f32[16,128,128]{2,1,0:T(8,128)} fusion(f32[16,128,128]{2,1,0:T(8,128)} %get-tuple-element.188, f32[8,16,128,128]{3,2,1,0:T(8,128)} %get-tuple-element.198, s32[]{:T(128)S(6)} %select_n.26), kind=kLoop, calls=%fused_computation.1.clone.1 | loop fusion | flops 262144 | bytes 3145732 | tf_op jit(solution)/shard_map/while/body/add | solution.py:25
  146.6 5.9 %fusion.7 = bf16[768,16,128]{0,2,1:T(8,128)(2,1)} fusion(f32[16,768,128]{1,2,0:T(8,128)} %fusion.11, f32[16,128,128]{2,1,0:T(8,128)} %get-tuple-element.83, bf16[768,2048]{1,0:T(8,128)(2,1)S(1)} %copy-done), kind=kOutput, calls=%fused_computation.12 | convolution fusion | flops 407633920 | bytes 13631488 | tf_op jit(solution)/shard_map/jan,aon->jao/dot_general | solution.py:73
  152.4 4.6 %copy.37 = bf16[768,2048]{1,0:T(8,128)(2,1)} copy(bf16[768,2048]{0,1:T(8,128)(2,1)} %bitcast.108) | data formatting | bytes 6291456
  157.1 7.0 %fusion.6 = bf16[768,16,128]{0,2,1:T(8,128)(2,1)} fusion(f32[16,768,128]{1,2,0:T(8,128)} %fusion, f32[16,128,128]{2,1,0:T(8,128)} %get-tuple-element.83, bf16[768,2048]{1,0:T(8,128)(2,1)} %param.9), kind=kOutput, calls=%fused_computation.10 | convolution fusion | flops 407633920 | bytes 13631488 | tf_op jit(solution)/shard_map/nam,amx->nax/dot_general | solution.py:82
  164.0 4.6 %copy.38 = bf16[768,2048]{1,0:T(8,128)(2,1)} copy(bf16[768,2048]{0,1:T(8,128)(2,1)} %bitcast.107) | data formatting | bytes 6291456
  (1 shorter events, 0.0 us)
Async XLA Ops:
  7.2 1.9 %copy-start = (bf16[768,2048]{1,0:T(8,128)(2,1)S(1)}, bf16[768,2048]{1,0:T(8,128)(2,1)}, u32[]{:S(2)}) copy-start(bf16[768,2048]{1,0:T(8,128)(2,1)} %param.10) | copy-start | bytes 9437188
  7.2 66.7 %all-gather.5.cloned.1.call-start = ((), (), s32[]{:S(2)}) async-start(), calls=%async_computation | async-start | bytes 9437184 | tf_op jit(solution)/shard_map/all_gather | solution.py:14
  13.3 113.6 %all-gather.7.cloned.1.call-start = ((), (), s32[]{:S(2)}) async-start(), calls=%async_computation.1 | async-start | bytes 9437184 | tf_op jit(solution)/shard_map/all_gather | solution.py:14
Sparse Core Ops, SparseCore 0:
  13.5 57.0 all-gather.4
  72.5 54.3 all-gather.6
where the time goes:
time: 176 us; the launch traced here: 175 us
  matrix products  78.7 us (45%)
  waiting for transfers between devices  40.6 us (23%)
  local copies, waits for them, and re-layouts  22.6 us (13%)
  other arithmetic  19.6 us (11%)
  between operations  14.1 us (8%)
    all_gather x2, waiting for transfers between devices, carried_in(): gathered = lax.all_gather(part, axis)  40.5 us
    add x7, other arithmetic, add_states(): return earlier + later_state  18.6 us
    unnamed x5, local copies, waits for them, and re-layouts  15.8 us
    dot_general x1, matrix products, on_device(): jnp.einsum('ynv,vyq->nyq', weight_gradients, lookup_per_position, preferr...  12.8 us
    dot_general x1, matrix products, on_device(): jnp.einsum('eca,ceo->aeo', weight_gradients, query_token_rows, preferred_...  12.7 us
    dot_general x1, matrix products, on_device(): jnp.einsum('uno,nud->oud', forward_weight_matrix, gradient_token_rows, pr...  12.4 us
    dot_general x1, matrix products, on_device(): jnp.einsum('thv,shv->hts', gradient_token_rows, content_per_position, pre...  12.1 us
    dot_general x1, matrix products, on_device(): jnp.einsum('nam,amx->nax', lookup_per_position, suffix_halves, preferred_...  6.96 us
  transfers between devices with their start and end apart: 2, of which 1 were waited for; matrix products, arithmetic and copies ran while one was open for 42% of the time, Pallas kernels for 0%

commit v1 on v0

v1 whole, which is shorter than its diff:
```python
import functools

import jax
import jax.numpy as jnp
from jax import lax
from jax.experimental import pallas as pl
from jax.experimental.pallas import tpu as pltpu
from jax.sharding import PartitionSpec as P

HEADS = 16
HEAD_DIM = 128
HALF = HEADS // 2
COLUMNS = HALF * HEAD_DIM
CHUNKS = ((0, 4), (4, 8))
READS = 4
SUB = 256
PARTIAL = jnp.float32

TN = (((0,), (0,)), ((), ()))
NT = (((1,), (1,)), ((), ()))
NN = (((1,), (0,)), ((), ()))

IN_VMEM = pl.BlockSpec(memory_space=pltpu.VMEM)
ANYWHERE = pl.BlockSpec(memory_space=pl.ANY)
CHEAP = pl.CostEstimate(flops=1000, bytes_accessed=1000, transcendentals=0)
LONG = pl.CostEstimate(flops=2 * 10**10, bytes_accessed=1000, transcendentals=0)


def dot(left, right, dims):
    return lax.dot_general(left, right, dims, preferred_element_type=jnp.float32)


def state_of(heads):
    return pltpu.VMEM((2, heads, HEAD_DIM, HEAD_DIM), jnp.float32)


def my_core():
    return lax.rem(lax.axis_index("seq"), 2)


def comes_earlier(turn):
    pair = lax.div(lax.axis_index("seq"), 2)
    return jnp.bitwise_xor(pair, turn) < pair


def half_start(mine):
    half = my_core() if mine else 1 - my_core()
    return half * COLUMNS


def states_kernel(mine, *refs):
    sources, local, (sums, early, late, sems) = refs[:4], refs[-8:-4], refs[-4:]
    rows = local[0].shape[0]
    subs = rows // SUB
    width = READS * HEAD_DIM
    base = half_start(mine)
    copies = []
    for group in range(HALF // READS):
        for i in (1, 2, 0, 3):
            copy = pltpu.make_async_copy(
                sources[i].at[:, pl.ds(pl.multiple_of(base + group * width, width), width)],
                local[i].at[:, pl.ds(group * width, width)],
                sems.at[group, i],
            )
            copy.start()
            copies.append(copy)
    q, k, v, o = local
    for group in range(HALF // READS):
        for kind, (left, right) in enumerate(((k, v), (q, o))):
            copies[4 * group + 2 * kind].wait()
            copies[4 * group + 2 * kind + 1].wait()
            order = list(range(subs)) if kind == 0 else list(range(subs - 1, -1, -1))
            for head in range(group * READS, (group + 1) * READS):
                at = pl.ds(head * HEAD_DIM, HEAD_DIM)
                total = None
                for sub in order:
                    span = pl.ds(sub * SUB, SUB)
                    part = dot(left[span, at], right[span, at], TN)
                    total = part if total is None else total + part
                    if sub != order[-1]:
                        if kind == 0:
                            early[head, sub] = total
                        else:
                            late[head, sub - 1] = total
                sums[kind, head] = total


def states(mine, sources, after):
    rows = sources[0].shape[0]
    partial = pltpu.VMEM((HALF, rows // SUB - 1, HEAD_DIM, HEAD_DIM), jnp.float32)
    out = [pltpu.VMEM((rows, COLUMNS), jnp.bfloat16)] * 4 + [state_of(HALF), partial, partial]
    *local, sums, early, late = pl.pallas_call(
        functools.partial(states_kernel, mine),
        out_shape=out,
        in_specs=[ANYWHERE] * (4 + len(after)),
        out_specs=[IN_VMEM] * len(out),
        scratch_shapes=[pltpu.SemaphoreType.DMA((HALF // READS, 4))],
        compiler_params=pltpu.CompilerParams(vmem_limit_bytes=2 << 20),
        cost_estimate=CHEAP,
        name="states",
    )(*sources, *after)
    return local, sums, (early, late)


def within_kernel(scale, q, k, v, o, *rest):
    dq, dk, dv = rest[-3:]
    rows = q.shape[0]
    at_row = lax.broadcasted_iota(jnp.int32, (SUB, SUB), 0)
    at_column = lax.broadcasted_iota(jnp.int32, (SUB, SUB), 1)
    lower = at_row >= at_column
    upper = at_row <= at_column
    for head in range(HALF):
        at = pl.ds(head * HEAD_DIM, HEAD_DIM)
        for sub in range(rows // SUB):
            span = pl.ds(sub * SUB, SUB)
            q_one, k_one, v_one, o_one = q[span, at], k[span, at], v[span, at], o[span, at]
            weights = jnp.where(upper, scale * dot(k_one, q_one, NT), 0.0).astype(jnp.bfloat16)
            grads = jnp.where(lower, scale * dot(o_one, v_one, NT), 0.0).astype(jnp.bfloat16)
            grads_t = jnp.where(upper, scale * dot(v_one, o_one, NT), 0.0).astype(jnp.bfloat16)
            dq[span, at] = dot(grads, k_one, NN).astype(PARTIAL)
            dk[span, at] = dot(grads_t, q_one, NN).astype(PARTIAL)
            dv[span, at] = dot(weights, o_one, NN).astype(PARTIAL)


def within(scale, local, after):
    rows = local[0].shape[0]
    return pl.pallas_call(
        functools.partial(within_kernel, scale),
        out_shape=[pltpu.VMEM((rows, COLUMNS), PARTIAL)] * 3,
        in_specs=[IN_VMEM] * 4 + [ANYWHERE] * len(after),
        out_specs=[IN_VMEM] * 3,
        compiler_params=pltpu.CompilerParams(vmem_limit_bytes=2 << 20),
        cost_estimate=CHEAP,
        name="within",
    )(*local, *after)


def join_kernel(turns, sums, sums_in, *sent):
    earlier = [comes_earlier(turn) for turn in turns]
    for index, (start, stop) in enumerate(CHUNKS):
        for head in range(start, stop):
            forward = sums[0, head] + sums_in[0, head]
            backward = sums[1, head] + sums_in[1, head]
            for i in range(len(turns)):
                sent[index * len(turns) + i][head - start] = jnp.where(earlier[i], backward, forward)


def join(turns, sums, sums_in):
    out = [
        pltpu.VMEM((stop - start, HEAD_DIM, HEAD_DIM), jnp.float32) for start, stop in CHUNKS for _ in turns
    ]
    return pl.pallas_call(
        functools.partial(join_kernel, turns),
        out_shape=out,
        in_specs=[IN_VMEM] * 2,
        out_specs=[IN_VMEM] * len(out),
        compiler_params=pltpu.CompilerParams(vmem_limit_bytes=2 << 20),
        cost_estimate=CHEAP,
        name="join",
    )(sums, sums_in)


def combine_kernel(turns, start, *refs):
    received, (sums, sums_in) = refs[: len(turns)], refs[len(turns) : len(turns) + 2]
    own, other = refs[-2:]
    second = my_core() == 1
    earlier = [comes_earlier(turn) for turn in turns]
    for head in range(own.shape[1]):
        prefix = jnp.zeros((HEAD_DIM, HEAD_DIM), jnp.float32)
        suffix = jnp.zeros((HEAD_DIM, HEAD_DIM), jnp.float32)
        for i in range(len(turns)):
            value = received[i][head]
            prefix = prefix + jnp.where(earlier[i], value, 0.0)
            suffix = suffix + jnp.where(earlier[i], 0.0, value)
        own[0, head] = prefix + jnp.where(second, sums_in[0, start + head], 0.0)
        own[1, head] = suffix + jnp.where(second, 0.0, sums_in[1, start + head])
        other[0, head] = prefix + jnp.where(second, 0.0, sums[0, start + head])
        other[1, head] = suffix + jnp.where(second, sums[1, start + head], 0.0)


def combine(turns, chunk, received, sums, sums_in, after):
    start, stop = chunk
    return pl.pallas_call(
        functools.partial(combine_kernel, turns, start),
        out_shape=[state_of(stop - start)] * 2,
        in_specs=[IN_VMEM] * (len(received) + 2) + [ANYWHERE] * len(after),
        out_specs=[IN_VMEM] * 2,
        compiler_params=pltpu.CompilerParams(vmem_limit_bytes=3 << 20),
        cost_estimate=CHEAP,
        name="combine",
    )(*received, sums, sums_in, *after)


def finish_kernel(scale, mine, chunk, k, v, o, dq, dk, dv, state, early, late, *rest):
    *targets, dq_out, dk_out, dv_out, sems = rest[-7:]
    rows = k.shape[0]
    subs = rows // SUB
    first, stop = chunk
    base = half_start(mine)
    width = 2 * HEAD_DIM
    copies = []
    for head in range(first, stop):
        at = pl.ds(head * HEAD_DIM, HEAD_DIM)
        to = pl.ds((head - first) * HEAD_DIM, HEAD_DIM)
        for sub in range(subs):
            span = pl.ds(sub * SUB, SUB)
            before, later = state[0, head - first], state[1, head - first]
            if sub > 0:
                before = before + early[head, sub - 1]
            if sub < subs - 1:
                later = later + late[head, sub]
            before, later = before.astype(jnp.bfloat16), later.astype(jnp.bfloat16)
            dq_out[span, to] = (dq[span, at] + scale * dot(o[span, at], before, NT)).astype(jnp.bfloat16)
            dk_out[span, to] = (dk[span, at] + scale * dot(v[span, at], later, NT)).astype(jnp.bfloat16)
            dv_out[span, to] = (dv[span, at] + scale * dot(k[span, at], later, NN)).astype(jnp.bfloat16)
        if (head - first) % 2 == 1:
            done = (head - 1) * HEAD_DIM
            for i, (source, target) in enumerate(zip((dq_out, dk_out, dv_out), targets, strict=True)):
                copy = pltpu.make_async_copy(
                    source.at[:, pl.ds(done - first * HEAD_DIM, width)],
                    target.at[:, pl.ds(pl.multiple_of(base + done, width), width)],
                    sems.at[(head - first) // 2, i],
                )
                copy.start()
                copies.append(copy)
    for copy in copies:
        copy.wait()


def finish(scale, mine, chunk, local, partials, state, inner, before):
    rows = local[0].shape[0]
    heads = chunk[1] - chunk[0]
    out = [jax.ShapeDtypeStruct((rows, HEADS * HEAD_DIM), jnp.bfloat16)] * 3
    operands = [*local[1:], *partials, state, *inner, *before]
    return pl.pallas_call(
        functools.partial(finish_kernel, scale, mine, chunk),
        out_shape=out,
        in_specs=[IN_VMEM] * 9 + [ANYWHERE] * len(before),
        out_specs=[ANYWHERE] * 3,
        scratch_shapes=[pltpu.VMEM((rows, heads * HEAD_DIM), jnp.bfloat16)] * 3
        + [pltpu.SemaphoreType.DMA((heads // 2, 3))],
        input_output_aliases={9 + i: i for i in range(len(before))},
        compiler_params=pltpu.CompilerParams(vmem_limit_bytes=5 << 20),
        cost_estimate=LONG,
        name="finish",
    )(*operands)


def on_device(queries, key_rows, value_rows, out_grad):
    count = lax.axis_size("seq")
    scale = (HEAD_DIM * queries.shape[0] * count) ** -0.5
    turns = range(1, count // 2)
    sources = [
        pltpu.with_memory_space_constraint(array, pltpu.HBM) for array in (queries, key_rows, value_rows, out_grad)
    ]

    def swap(value):
        return lax.ppermute(value, "seq", [(i, i ^ 1) for i in range(count)])

    local_b, sums_b, inner_b = states(False, sources, ())
    sums_in = swap(sums_b)
    local_a, sums_a, inner_a = states(True, sources, (sums_b,))
    sent = join(turns, sums_a, sums_in)
    received = [
        lax.ppermute(value, "seq", [(i, i ^ (2 * turns[n % len(turns)])) for i in range(count)])
        for n, value in enumerate(sent)
    ]
    partials_b = within(scale, local_b, sent)
    partials_a = within(scale, local_a, (partials_b[0],))
    done = ()
    after = (partials_a[0],)
    for index, chunk in enumerate(CHUNKS):
        values = received[index * len(turns) : (index + 1) * len(turns)]
        own, other = combine(turns, chunk, values, sums_a, sums_in, after)
        other = swap(other)
        done = finish(scale, True, chunk, local_a, partials_a, own, inner_a, done)
        done = finish(scale, False, chunk, local_b, partials_b, other, inner_b, done)
        after = (pltpu.with_memory_space_constraint(done[0], pltpu.HBM),)
    return tuple(done)


def solution(mesh):
    placed = P(("lists", "seq"), None)
    return jax.shard_map(
        on_device,
        mesh=mesh,
        in_specs=(placed,) * 4,
        out_specs=(placed,) * 3,
        check_vma=False,
    )
```

time: 176 us -> 41.6 us (0.24)
  matrix products: 78.7 us -> 0 us
  waiting for transfers between devices: 40.6 us -> 3.46 us
  Pallas kernels: 0 us -> 28.7 us
  local copies, waits for them, and re-layouts: 22.6 us -> 0 us
  other arithmetic: 19.6 us -> 0 us
  between operations: 14.1 us -> 0.94 us
  starting transfers between devices: 0.08 us -> 8.33 us
    dot_general x9 -> x0, matrix products: 78.7 us -> none  [the longest x1 12.8 us: on_device(): jnp.einsum('ynv,vyq->nyq', weight_gradients, lookup_per_position, preferr...]
    all_gather x2 -> x0, waiting for transfers between devices: 40.5 us -> none  [carried_in(): gathered = lax.all_gather(part, axis)]
    pallas_call x0 -> x11, Pallas kernels: none -> 28.7 us  [the longest x2 13 us: within(): pl.pallas_call(functools.partial(within_kernel, scale), out_shape=[pltpu....]
    add x7 -> x0, other arithmetic: 18.6 us -> none  [add_states(): return earlier + later_state]
    unnamed x5 -> x0, local copies, waits for them, and re-layouts: 15.8 us -> none
    ppermute x0 -> x9, starting transfers between devices: none -> 8.33 us  [the longest x6 7.67 us: on_device(): lax.ppermute(value, 'seq', [(i, i ^ 2 * turns[n % len(turns)]) for i in r...]
    reshape x1 -> x0, local copies, waits for them, and re-layouts: 4.64 us -> none  [on_device(): gradient_token_rows = out_grad.reshape(shape3)]
    ppermute x0 -> x9, waiting for transfers between devices: none -> 3.46 us  [the longest x6 3.45 us: on_device(): lax.ppermute(value, 'seq', [(i, i ^ 2 * turns[n % len(turns)]) for i in r...]
  transfers between devices with their start and end apart: 2 -> 9, of which waited for: 1 -> 1; matrix products, arithmetic and copies ran while one was open for 42% -> 0% of each run, Pallas kernels for 0% -> 56%
where the time goes in v1:
time: 41.6 us; the launch traced here: 41.5 us
  Pallas kernels  28.7 us (69%)
  starting transfers between devices  8.33 us (20%)
  waiting for transfers between devices  3.46 us (8%)
  between operations  0.94 us (2%)
    pallas_call x2, Pallas kernels, within(): pl.pallas_call(functools.partial(within_kernel, scale), out_shape=[pltpu....  13 us
    pallas_call x4, Pallas kernels, finish(): pl.pallas_call(functools.partial(finish_kernel, scale, mine, chunk), out_...  8.5 us
    ppermute x6, starting transfers between devices, on_device(): lax.ppermute(value, 'seq', [(i, i ^ 2 * turns[n % len(turns)]) for i in r...  7.67 us
    pallas_call x2, Pallas kernels, states(): pl.pallas_call(functools.partial(states_kernel, mine), out_shape=out, in_...  6.75 us
    ppermute x6, waiting for transfers between devices, on_device(): lax.ppermute(value, 'seq', [(i, i ^ 2 * turns[n % len(turns)]) for i in r...  3.45 us
  transfers between devices with their start and end apart: 9, of which 1 were waited for; matrix products, arithmetic and copies ran while one was open for 0% of the time, Pallas kernels for 56%

profile of v1, /device:TPU:0, one launch (start us, length us, event | category | flops | bytes accessed | tf_op | source)
XLA Modules:
  0.0 41.5 jit_solution(5562956936413609214)
XLA Ops:
  0.6 3.4 %states.2 = (bf16[768,1024]{1,0:T(8,128)(2,1)S(1)}, bf16[768,1024]{1,0:T(8,128)(2,1)S(1)}, bf16[768,1024]{1,0:T(8,128)(2,1)S(1)}, bf16[768,1024]{1,0:T(8,128)(2,...) custom-call(bf16[768,2048]{1,0:T(8,128)(2,1)} %refs_0_.3, ...), custom_call_target="tpu_custom_call" | custom-call | flops 1000 | bytes 1000 | tf_op jit(solution)/shard_map/states/pallas_call | solution.py:92
  4.0 0.5 %collective-permute-start = (f32[2,8,128,128]{3,2,1,0:T(8,128)S(1)}, f32[2,8,128,128]{3,2,1,0:T(8,128)S(1)}, u32[]{:S(2)}, u32[]{:S(2)}) collective-permute-start(f32[2,8,128,128]{3,2,1,0:T(8,128)S(1)} %get-tuple-element.46.refs_4_), channel_id=1, source_target_pairs={{0,1},{1,0},{2,3},{3,2},{4,5},{5,4},{6,7},{7,6},{8,9},{9,8},{10,11... | collective-permute-start | bytes 3145736 | tf_op jit(solution)/shard_map/ppermute | solution.py:258
  4.5 3.4 %states.3 = (bf16[768,1024]{1,0:T(8,128)(2,1)S(1)}, bf16[768,1024]{1,0:T(8,128)(2,1)S(1)}, bf16[768,1024]{1,0:T(8,128)(2,1)S(1)}, bf16[768,1024]{1,0:T(8,128)(2,...) custom-call(bf16[768,2048]{1,0:T(8,128)(2,1)} %refs_0_.3, ...), custom_call_target="tpu_custom_call" | custom-call | flops 1000 | bytes 1000 | tf_op jit(solution)/shard_map/states/pallas_call | solution.py:92
  7.9 0.0 collective-permute-done.sums_in.refs_4_
  7.9 0.1 join.1
  8.1 2.6 %collective-permute-start.4 = (f32[4,128,128]{2,1,0:T(8,128)S(1)}, f32[4,128,128]{2,1,0:T(8,128)S(1)}, u32[]{:S(2)}, u32[]{:S(2)}) collective-permute-start(f32[4,128,128]{2,1,0:T(8,128)S(1)} %get-tuple-element.48.rest_0_), channel_id=1, source_target_pairs={{0,2},{1,3},{2,0},{3,1},{4,6},{5,7},{6,4},{7,5},{8,10},{9,11},{10,... | collective-permute-start | bytes 786440 | tf_op jit(solution)/shard_map/ppermute | solution.py:265
  10.6 1.5 %collective-permute-start.5 = (f32[4,128,128]{2,1,0:T(8,128)S(1)}, f32[4,128,128]{2,1,0:T(8,128)S(1)}, u32[]{:S(2)}, u32[]{:S(2)}) collective-permute-start(f32[4,128,128]{2,1,0:T(8,128)S(1)} %get-tuple-element.49.rest_1_), channel_id=1, source_target_pairs={{0,4},{1,5},{2,6},{3,7},{4,0},{5,1},{6,2},{7,3},{8,12},{9,13},{10,... | collective-permute-start | bytes 786440 | tf_op jit(solution)/shard_map/ppermute | solution.py:265
  12.2 0.0 collective-permute-start.6
  12.2 1.9 %collective-permute-start.1 = (f32[4,128,128]{2,1,0:T(8,128)S(1)}, f32[4,128,128]{2,1,0:T(8,128)S(1)}, u32[]{:S(2)}, u32[]{:S(2)}) collective-permute-start(f32[4,128,128]{2,1,0:T(8,128)S(1)} %get-tuple-element.51.rest_3_), channel_id=1, source_target_pairs={{0,2},{1,3},{2,0},{3,1},{4,6},{5,7},{6,4},{7,5},{8,10},{9,11},{10,... | collective-permute-start | bytes 786440 | tf_op jit(solution)/shard_map/ppermute | solution.py:265
  14.1 1.5 %collective-permute-start.2 = (f32[4,128,128]{2,1,0:T(8,128)S(1)}, f32[4,128,128]{2,1,0:T(8,128)S(1)}, u32[]{:S(2)}, u32[]{:S(2)}) collective-permute-start(f32[4,128,128]{2,1,0:T(8,128)S(1)} %get-tuple-element.52.rest_4_), channel_id=1, source_target_pairs={{0,4},{1,5},{2,6},{3,7},{4,0},{5,1},{6,2},{7,3},{8,12},{9,13},{10,... | collective-permute-start | bytes 786440 | tf_op jit(solution)/shard_map/ppermute | solution.py:265
  15.7 6.4 %within.2 = (f32[768,1024]{1,0:T(8,128)S(1)}, f32[768,1024]{1,0:T(8,128)S(1)}, f32[768,1024]{1,0:T(8,128)S(1)}) custom-call(bf16[768,1024]{1,0:T(8,128)(2,1)S(1)} %get-tuple-element.45.q, bf16[768,1024]{1,0:T(8,128)(2,1)S(1)} %get-tuple-element.42.k, bf16[768,1024]{1,0:T(8,128)(2,1)S(1)} %get-tuple-element.43.v, bf16[768,1024]{1,0:T(8,128)(2,1)S(1)} %get-tuple-element.44.o, ...), custom_call_target="tpu_custom_call" | custom-call | flops 1000 | bytes 1000 | tf_op jit(solution)/shard_map/within/pallas_call | solution.py:127
  22.1 6.6 %within.3 = (f32[768,1024]{1,0:T(8,128)S(1)}, f32[768,1024]{1,0:T(8,128)S(1)}, f32[768,1024]{1,0:T(8,128)S(1)}) custom-call(bf16[768,1024]{1,0:T(8,128)(2,1)S(1)} %get-tuple-element.57.q, bf16[768,1024]{1,0:T(8,128)(2,1)S(1)} %get-tuple-element.58.k, bf16[768,1024]{1,0:T(8,128)(2,1)S(1)} %get-tuple-element.59.v, bf16[768,1024]{1,0:T(8,128)(2,1)S(1)} %get-tuple-element.60.o, ...), custom_call_target="tpu_custom_call" | custom-call | flops 1000 | bytes 1000 | tf_op jit(solution)/shard_map/within/pallas_call | solution.py:127
  28.7 0.0 collective-permute-done.4.refs_0_
  28.7 0.1 collective-permute-start.3
  28.8 0.0 collective-permute-done.5.refs_1_
  28.8 0.0 collective-permute-done.6.refs_2_
  28.8 0.2 combine.2
  29.0 0.1 collective-permute-start.7
  29.0 2.2 %finish.4 = (bf16[768,2048]{1,0:T(8,128)(2,1)}, bf16[768,2048]{1,0:T(8,128)(2,1)}, bf16[768,2048]{1,0:T(8,128)(2,1)}) custom-call(bf16[768,1024]{1,0:T(8,128)(2,1)S(1)} %get-tuple-element.58.k, bf16[768,1024]{1,0:T(8,128)(2,1)S(1)} %get-tuple-element.59.v, bf16[768,1024]{1,0:T(8,128)(2,1)S(1)} %get-tuple-element.60.o, ...), custom_call_target="tpu_custom_call" | custom-call | flops 20000000000 | bytes 1000 | tf_op jit(solution)/shard_map/finish/pallas_call | solution.py:235
  31.3 0.0 collective-permute-done.7.state
  31.3 2.2 %finish.5 = (bf16[768,2048]{1,0:T(8,128)(2,1)}, bf16[768,2048]{1,0:T(8,128)(2,1)}, bf16[768,2048]{1,0:T(8,128)(2,1)}) custom-call(bf16[768,1024]{1,0:T(8,128)(2,1)S(1)} %get-tuple-element.42.k, bf16[768,1024]{1,0:T(8,128)(2,1)S(1)} %get-tuple-element.43.v, ...), custom_call_target="tpu_custom_call", output_to_operand_aliasing={{0}: (9, {}), {1}: (10, {}), {2}: (11, {})} | custom-call | flops 20000000000 | bytes 1000 | tf_op jit(solution)/shard_map/finish/pallas_call | solution.py:235
  33.5 0.0 collective-permute-done.1.refs_0_
  33.5 0.0 collective-permute-done.2.refs_1_
  33.5 3.4 %collective-permute-done.3.refs_2_ = f32[4,128,128]{2,1,0:T(8,128)S(1)} collective-permute-done((f32[4,128,128]{2,1,0:T(8,128)S(1)}, f32[4,128,128]{2,1,0:T(8,128)S(1)}, u32[]{:S(2)}, u32[]{:S(2)}) %collective-permute-start.3) | collective-permute-done | bytes 262176 | tf_op jit(solution)/shard_map/ppermute | solution.py:265
  36.9 0.2 combine.3
  37.1 0.1 collective-permute-start.8
  37.2 2.0 %finish.6 = (bf16[768,2048]{1,0:T(8,128)(2,1)}, bf16[768,2048]{1,0:T(8,128)(2,1)}, bf16[768,2048]{1,0:T(8,128)(2,1)}) custom-call(bf16[768,1024]{1,0:T(8,128)(2,1)S(1)} %get-tuple-element.58.k, bf16[768,1024]{1,0:T(8,128)(2,1)S(1)} %get-tuple-element.59.v, ...), custom_call_target="tpu_custom_call", output_to_operand_aliasing={{0}: (9, {}), {1}: (10, {}), {2}: (11, {})} | custom-call | flops 20000000000 | bytes 1000 | tf_op jit(solution)/shard_map/finish/pallas_call | solution.py:235
  39.2 0.0 collective-permute-done.8.state
  39.2 2.0 %finish.7 = (bf16[768,2048]{1,0:T(8,128)(2,1)}, bf16[768,2048]{1,0:T(8,128)(2,1)}, bf16[768,2048]{1,0:T(8,128)(2,1)}) custom-call(bf16[768,1024]{1,0:T(8,128)(2,1)S(1)} %get-tuple-element.42.k, bf16[768,1024]{1,0:T(8,128)(2,1)S(1)} %get-tuple-element.43.v, ...), custom_call_target="tpu_custom_call", output_to_operand_aliasing={{0}: (9, {}), {1}: (10, {}), {2}: (11, {})} | custom-call | flops 20000000000 | bytes 1000 | tf_op jit(solution)/shard_map/finish/pallas_call | solution.py:235
Async XLA Ops:
  4.0 3.9 %collective-permute-start = (f32[2,8,128,128]{3,2,1,0:T(8,128)S(1)}, f32[2,8,128,128]{3,2,1,0:T(8,128)S(1)}, u32[]{:S(2)}, u32[]{:S(2)}) collective-permute-start(f32[2,8,128,128]{3,2,1,0:T(8,128)S(1)} %get-tuple-element.46.refs_4_), channel_id=1, source_target_pairs={{0,1},{1,0},{2,3},{3,2},{4,5},{5,4},{6,7},{7,6},{8,9},{9,8},{10,11... | collective-permute-start | bytes 3145736 | tf_op jit(solution)/shard_map/ppermute | solution.py:258
  8.1 20.6 %collective-permute-start.4 = (f32[4,128,128]{2,1,0:T(8,128)S(1)}, f32[4,128,128]{2,1,0:T(8,128)S(1)}, u32[]{:S(2)}, u32[]{:S(2)}) collective-permute-start(f32[4,128,128]{2,1,0:T(8,128)S(1)} %get-tuple-element.48.rest_0_), channel_id=1, source_target_pairs={{0,2},{1,3},{2,0},{3,1},{4,6},{5,7},{6,4},{7,5},{8,10},{9,11},{10,... | collective-permute-start | bytes 786440 | tf_op jit(solution)/shard_map/ppermute | solution.py:265
  10.6 18.1 %collective-permute-start.5 = (f32[4,128,128]{2,1,0:T(8,128)S(1)}, f32[4,128,128]{2,1,0:T(8,128)S(1)}, u32[]{:S(2)}, u32[]{:S(2)}) collective-permute-start(f32[4,128,128]{2,1,0:T(8,128)S(1)} %get-tuple-element.49.rest_1_), channel_id=1, source_target_pairs={{0,4},{1,5},{2,6},{3,7},{4,0},{5,1},{6,2},{7,3},{8,12},{9,13},{10,... | collective-permute-start | bytes 786440 | tf_op jit(solution)/shard_map/ppermute | solution.py:265
  12.2 16.6 %collective-permute-start.6 = (f32[4,128,128]{2,1,0:T(8,128)S(1)}, f32[4,128,128]{2,1,0:T(8,128)S(1)}, u32[]{:S(2)}, u32[]{:S(2)}) collective-permute-start(f32[4,128,128]{2,1,0:T(8,128)S(1)} %get-tuple-element.50.rest_2_), channel_id=1, source_target_pairs={{0,6},{1,7},{2,4},{3,5},{4,2},{5,3},{6,0},{7,1},{8,14},{9,15},{10,... | collective-permute-start | bytes 786440 | tf_op jit(solution)/shard_map/ppermute | solution.py:265
  12.2 21.3 %collective-permute-start.1 = (f32[4,128,128]{2,1,0:T(8,128)S(1)}, f32[4,128,128]{2,1,0:T(8,128)S(1)}, u32[]{:S(2)}, u32[]{:S(2)}) collective-permute-start(f32[4,128,128]{2,1,0:T(8,128)S(1)} %get-tuple-element.51.rest_3_), channel_id=1, source_target_pairs={{0,2},{1,3},{2,0},{3,1},{4,6},{5,7},{6,4},{7,5},{8,10},{9,11},{10,... | collective-permute-start | bytes 786440 | tf_op jit(solution)/shard_map/ppermute | solution.py:265
  14.1 19.3 %collective-permute-start.2 = (f32[4,128,128]{2,1,0:T(8,128)S(1)}, f32[4,128,128]{2,1,0:T(8,128)S(1)}, u32[]{:S(2)}, u32[]{:S(2)}) collective-permute-start(f32[4,128,128]{2,1,0:T(8,128)S(1)} %get-tuple-element.52.rest_4_), channel_id=1, source_target_pairs={{0,4},{1,5},{2,6},{3,7},{4,0},{5,1},{6,2},{7,3},{8,12},{9,13},{10,... | collective-permute-start | bytes 786440 | tf_op jit(solution)/shard_map/ppermute | solution.py:265
  28.7 8.3 %collective-permute-start.3 = (f32[4,128,128]{2,1,0:T(8,128)S(1)}, f32[4,128,128]{2,1,0:T(8,128)S(1)}, u32[]{:S(2)}, u32[]{:S(2)}) collective-permute-start(f32[4,128,128]{2,1,0:T(8,128)S(1)} %get-tuple-element.53.rest_5_), channel_id=1, source_target_pairs={{0,6},{1,7},{2,4},{3,5},{4,2},{5,3},{6,0},{7,1},{8,14},{9,15},{10,... | collective-permute-start | bytes 786440 | tf_op jit(solution)/shard_map/ppermute | solution.py:265
  29.0 2.3 %collective-permute-start.7 = (f32[2,4,128,128]{3,2,1,0:T(8,128)S(1)}, f32[2,4,128,128]{3,2,1,0:T(8,128)S(1)}, u32[]{:S(2)}, u32[]{:S(2)}) collective-permute-start(f32[2,4,128,128]{3,2,1,0:T(8,128)S(1)} %get-tuple-element.62), channel_id=1, source_target_pairs={{0,1},{1,0},{2,3},{3,2},{4,5},{5,4},{6,7},{7,6},{8,9},{9,8},{10,11... | collective-permute-start | bytes 1572872 | tf_op jit(solution)/shard_map/ppermute | solution.py:258
  37.1 2.1 %collective-permute-start.8 = (f32[2,4,128,128]{3,2,1,0:T(8,128)S(1)}, f32[2,4,128,128]{3,2,1,0:T(8,128)S(1)}, u32[]{:S(2)}, u32[]{:S(2)}) collective-permute-start(f32[2,4,128,128]{3,2,1,0:T(8,128)S(1)} %get-tuple-element.74), channel_id=1, source_target_pairs={{0,1},{1,0},{2,3},{3,2},{4,5},{5,4},{6,7},{7,6},{8,9},{9,8},{10,11... | collective-permute-start | bytes 1572872 | tf_op jit(solution)/shard_map/ppermute | solution.py:258

commit v2 on v0

v2 whole, which is shorter than its diff:
```python
import functools

import jax
import jax.numpy as jnp
from jax import lax
from jax.experimental import pallas as pl
from jax.experimental.pallas import tpu as pltpu
from jax.sharding import PartitionSpec as P

HEADS = 16
HEAD_DIM = 128
HALF = HEADS // 2
COLUMNS = HALF * HEAD_DIM
CHUNKS = ((0, 4), (4, 8))
SUB = 256
PARTIAL = jnp.float32

TN = (((0,), (0,)), ((), ()))
NT = (((1,), (1,)), ((), ()))
NN = (((1,), (0,)), ((), ()))

IN_VMEM = pl.BlockSpec(memory_space=pltpu.VMEM)
ANYWHERE = pl.BlockSpec(memory_space=pl.ANY)
SHORT = pl.CostEstimate(flops=1000, bytes_accessed=1000, transcendentals=0)
LONG = pl.CostEstimate(flops=2 * 10**10, bytes_accessed=1000, transcendentals=0)


def dot(left, right, dims):
    return lax.dot_general(left, right, dims, preferred_element_type=jnp.float32)


def heads_of(chunk):
    return chunk[1] - chunk[0]


def state_of(heads):
    return pltpu.VMEM((2, heads, HEAD_DIM, HEAD_DIM), jnp.float32)


def head_columns(head):
    return pl.ds(head * HEAD_DIM, HEAD_DIM)


def my_core():
    return lax.rem(lax.axis_index("seq"), 2)


def comes_earlier(turn):
    pair = lax.div(lax.axis_index("seq"), 2)
    return jnp.bitwise_xor(pair, turn) < pair


def first_column(mine, chunk):
    half = my_core() if mine else 1 - my_core()
    return half * COLUMNS + chunk[0] * HEAD_DIM


def call(kernel, out, operands, after=(), scratch=(), cost=SHORT, limit=3, name=None):
    return pl.pallas_call(
        kernel,
        out_shape=out,
        in_specs=[IN_VMEM] * len(operands) + [ANYWHERE] * len(after),
        out_specs=[IN_VMEM] * len(out),
        scratch_shapes=list(scratch),
        compiler_params=pltpu.CompilerParams(vmem_limit_bytes=limit << 20),
        cost_estimate=cost,
        name=name,
    )(*operands, *after)


def read(mine, chunk, sources, local, sems):
    width = heads_of(chunk) * HEAD_DIM
    at = pl.ds(pl.multiple_of(first_column(mine, chunk), HEAD_DIM), width)
    copies = []
    for i in (1, 2, 0, 3):
        copy = pltpu.make_async_copy(sources[i].at[:, at], local[i], sems.at[i])
        copy.start()
        copies.append(copy)
    return copies


def sum_up(copies, local, sums, early, late):
    q, k, v, o = local
    subs = q.shape[0] // SUB
    for kind, (left, right) in enumerate(((k, v), (q, o))):
        copies[2 * kind].wait()
        copies[2 * kind + 1].wait()
        order = list(range(subs)) if kind == 0 else list(range(subs - 1, -1, -1))
        for head in range(sums.shape[1]):
            at = head_columns(head)
            total = None
            for sub in order:
                span = pl.ds(sub * SUB, SUB)
                part = dot(left[span, at], right[span, at], TN)
                total = part if total is None else total + part
                if sub != order[-1]:
                    if kind == 0:
                        early[head, sub] = total
                    else:
                        late[head, sub - 1] = total
            sums[kind, head] = total


def work_inside(scale, local, outs):
    (q, k, v, o), (dq, dk, dv) = local, outs
    rows, columns = q.shape
    at_row = lax.broadcasted_iota(jnp.int32, (SUB, SUB), 0)
    at_column = lax.broadcasted_iota(jnp.int32, (SUB, SUB), 1)
    lower = at_row >= at_column
    upper = at_row <= at_column

    def weights_of(unit):
        head, sub = unit
        at, span = head_columns(head), pl.ds(sub * SUB, SUB)
        q_one, k_one, v_one, o_one = q[span, at], k[span, at], v[span, at], o[span, at]
        return (
            jnp.where(lower, scale * dot(o_one, v_one, NT), 0.0).astype(jnp.bfloat16),
            jnp.where(upper, scale * dot(v_one, o_one, NT), 0.0).astype(jnp.bfloat16),
            jnp.where(upper, scale * dot(k_one, q_one, NT), 0.0).astype(jnp.bfloat16),
        )

    units = [(head, sub) for head in range(columns // HEAD_DIM) for sub in range(rows // SUB)]
    ahead = weights_of(units[0])
    for number, (head, sub) in enumerate(units):
        grads, grads_t, weights = ahead
        if number + 1 < len(units):
            ahead = weights_of(units[number + 1])
        at, span = head_columns(head), pl.ds(sub * SUB, SUB)
        dq[span, at] = dot(grads, k[span, at], NN).astype(PARTIAL)
        dk[span, at] = dot(grads_t, q[span, at], NN).astype(PARTIAL)
        dv[span, at] = dot(weights, o[span, at], NN).astype(PARTIAL)


def shapes_of(rows, chunk):
    heads = heads_of(chunk)
    local = [pltpu.VMEM((rows, heads * HEAD_DIM), jnp.bfloat16)] * 4
    inner = pltpu.VMEM((heads, rows // SUB - 1, HEAD_DIM, HEAD_DIM), jnp.float32)
    partials = [pltpu.VMEM((rows, heads * HEAD_DIM), PARTIAL)] * 3
    return local, [state_of(heads), inner, inner], partials


def states_kernel(mine, chunk, *refs):
    sources, local, sums, sems = refs[:4], refs[-8:-4], refs[-4:-1], refs[-1]
    sum_up(read(mine, chunk, sources, local, sems), local, *sums)


def states(mine, chunk, sources, after):
    local, sums, _ = shapes_of(sources[0].shape[0], chunk)
    result = pl.pallas_call(
        functools.partial(states_kernel, mine, chunk),
        out_shape=local + sums,
        in_specs=[ANYWHERE] * (4 + len(after)),
        out_specs=[IN_VMEM] * 7,
        scratch_shapes=[pltpu.SemaphoreType.DMA((4,))],
        compiler_params=pltpu.CompilerParams(vmem_limit_bytes=2 << 20),
        cost_estimate=LONG,
        name="states",
    )(*sources, *after)
    return result[:4], result[4], result[5:]


def states_both_kernel(chunk, *refs):
    sources, parts, sems = refs[:4], (refs[-15:-8], refs[-8:-1]), refs[-1]
    copies = [read(bool(mine), chunk, sources, parts[mine][:4], sems.at[mine]) for mine in range(2)]
    for mine in range(2):
        sum_up(copies[mine], parts[mine][:4], *parts[mine][4:])


def states_both(chunk, sources, after):
    local, sums, _ = shapes_of(sources[0].shape[0], chunk)
    result = pl.pallas_call(
        functools.partial(states_both_kernel, chunk),
        out_shape=(local + sums) * 2,
        in_specs=[ANYWHERE] * (4 + len(after)),
        out_specs=[IN_VMEM] * 14,
        scratch_shapes=[pltpu.SemaphoreType.DMA((2, 4))],
        compiler_params=pltpu.CompilerParams(vmem_limit_bytes=2 << 20),
        cost_estimate=LONG,
        name="states_both",
    )(*sources, *after)
    return [(part[:4], part[4], part[5:]) for part in (result[:7], result[7:])]


def within_kernel(scale, *refs):
    work_inside(scale, refs[:4], refs[-3:])


def within(scale, chunk, local, after):
    partials = shapes_of(local[0].shape[0], chunk)[2]
    return call(functools.partial(within_kernel, scale), partials, local, after, cost=LONG, name="within")


def join_kernel(turns, sums, sums_in, *rest):
    sent = rest[-len(turns) :]
    for head in range(sums.shape[1]):
        forward = sums[0, head] + sums_in[0, head]
        backward = sums[1, head] + sums_in[1, head]
        for turn, out in zip(turns, sent, strict=True):
            out[head] = jnp.where(comes_earlier(turn), backward, forward)


def join(turns, sums, sums_in, after):
    out = [pltpu.VMEM(sums.shape[1:], jnp.float32)] * len(turns)
    return call(functools.partial(join_kernel, turns), out, (sums, sums_in), after, name="join")


def combine_kernel(turns, *refs):
    received, (sums, sums_in) = refs[: len(turns)], refs[len(turns) : len(turns) + 2]
    own, other = refs[-2:]
    second = my_core() == 1
    for head in range(sums.shape[1]):
        prefix = jnp.zeros((HEAD_DIM, HEAD_DIM), jnp.float32)
        suffix = jnp.zeros((HEAD_DIM, HEAD_DIM), jnp.float32)
        for turn, value in zip(turns, received, strict=True):
            earlier = comes_earlier(turn)
            prefix = prefix + jnp.where(earlier, value[head], 0.0)
            suffix = suffix + jnp.where(earlier, 0.0, value[head])
        own[0, head] = prefix + jnp.where(second, sums_in[0, head], 0.0)
        own[1, head] = suffix + jnp.where(second, 0.0, sums_in[1, head])
        other[0, head] = prefix + jnp.where(second, 0.0, sums[0, head])
        other[1, head] = suffix + jnp.where(second, sums[1, head], 0.0)


def combine(turns, received, sums, sums_in, after):
    out = [state_of(sums.shape[1])] * 2
    return call(functools.partial(combine_kernel, turns), out, (*received, sums, sums_in), after, name="combine")


def finish_kernel(scale, chunk, halves, *refs):
    targets, staged, sems = refs[-7:-4], refs[-4:-1], refs[-1]
    heads = heads_of(chunk)
    copies = []
    for number, mine in enumerate(halves):
        k, v, o, dq, dk, dv, state, early, late = refs[9 * number : 9 * number + 9]
        rows = k.shape[0]
        subs = rows // SUB
        base = first_column(mine, chunk)
        for head in range(heads):
            at = head_columns(head)
            to = head_columns(number * heads + head)
            for sub in range(subs):
                span = pl.ds(sub * SUB, SUB)
                before, later = state[0, head], state[1, head]
                if sub > 0:
                    before = before + early[head, sub - 1]
                if sub < subs - 1:
                    later = later + late[head, sub]
                before, later = before.astype(jnp.bfloat16), later.astype(jnp.bfloat16)
                pieces = (
                    dq[span, at] + scale * dot(o[span, at], before, NT),
                    dk[span, at] + scale * dot(v[span, at], later, NT),
                    dv[span, at] + scale * dot(k[span, at], later, NN),
                )
                for out, piece in zip(staged, pieces, strict=True):
                    out[span, to] = piece.astype(jnp.bfloat16)
            if head % 2 == 1 or head == heads - 1:
                first, width = (head - head % 2) * HEAD_DIM, (1 + head % 2) * HEAD_DIM
                for i in range(3):
                    copy = pltpu.make_async_copy(
                        staged[i].at[:, pl.ds(number * heads * HEAD_DIM + first, width)],
                        targets[i].at[:, pl.ds(pl.multiple_of(base + first, HEAD_DIM), width)],
                        sems.at[number, head // 2, i],
                    )
                    copy.start()
                    copies.append(copy)
    for copy in copies:
        copy.wait()


def finish(scale, chunk, parts, before):
    rows = parts[0][1][0].shape[0]
    out = [jax.ShapeDtypeStruct((rows, HEADS * HEAD_DIM), jnp.bfloat16)] * 3
    halves = tuple(part[0] for part in parts)
    operands = []
    for _, local, partials, state, inner in parts:
        operands += [*local[1:], *partials, state, *inner]
    width = len(parts) * heads_of(chunk) * HEAD_DIM
    return pl.pallas_call(
        functools.partial(finish_kernel, scale, chunk, halves),
        out_shape=out,
        in_specs=[IN_VMEM] * len(operands) + [ANYWHERE] * len(before),
        out_specs=[ANYWHERE] * 3,
        scratch_shapes=[pltpu.VMEM((rows, width), jnp.bfloat16)] * 3
        + [pltpu.SemaphoreType.DMA((len(parts), (heads_of(chunk) + 1) // 2, 3))],
        input_output_aliases={len(operands) + i: i for i in range(len(before))},
        compiler_params=pltpu.CompilerParams(vmem_limit_bytes=(2 + 3 * len(parts)) << 20),
        cost_estimate=LONG,
        name="finish",
    )(*operands, *before)


def on_device(queries, key_rows, value_rows, out_grad):
    count = lax.axis_size("seq")
    scale = (HEAD_DIM * queries.shape[0] * count) ** -0.5
    turns = range(1, count // 2)
    sources = [
        pltpu.with_memory_space_constraint(array, pltpu.HBM) for array in (queries, key_rows, value_rows, out_grad)
    ]
    early_chunk, late_chunk = CHUNKS

    def trade(value, distance):
        return lax.ppermute(value, "seq", [(i, i ^ distance) for i in range(count)])

    def trade_all(values):
        return [trade(value, 2 * turn) for turn, value in zip(turns, values, strict=True)]

    local_eo, sums_eo, inner_eo = states(False, early_chunk, sources, ())
    sums_e_in = trade(sums_eo, 1)
    local_em, sums_em, inner_em = states(True, early_chunk, sources, (sums_eo,))
    sent_e = join(turns, sums_em, sums_e_in, ())
    received_e = trade_all(sent_e)

    (local_lo, sums_lo, inner_lo), (local_lm, sums_lm, inner_lm) = states_both(late_chunk, sources, sent_e)
    sums_l_in = trade(sums_lo, 1)
    partials_eo = within(scale, early_chunk, local_eo, (sums_lo,))
    sent_l = join(turns, sums_lm, sums_l_in, (partials_eo[0],))
    received_l = trade_all(sent_l)
    partials_em = within(scale, early_chunk, local_em, (received_e[0], *sent_l))
    partials_lo = within(scale, late_chunk, local_lo, (partials_em[0],))

    own_e, other_e = combine(turns, received_e, sums_em, sums_e_in, (partials_lo[0],))
    other_e = trade(other_e, 1)
    partials_lm = within(scale, late_chunk, local_lm, (own_e,))
    done = finish(
        scale,
        early_chunk,
        [(True, local_em, partials_em, own_e, inner_em), (False, local_eo, partials_eo, other_e, inner_eo)],
        (),
    )

    held_back = (pltpu.with_memory_space_constraint(done[0], pltpu.HBM), partials_lm[0])
    own_l, other_l = combine(turns, received_l, sums_lm, sums_l_in, held_back)
    other_l = trade(other_l, 1)
    done = finish(scale, late_chunk, [(True, local_lm, partials_lm, own_l, inner_lm)], done)
    return tuple(finish(scale, late_chunk, [(False, local_lo, partials_lo, other_l, inner_lo)], done))


def solution(mesh):
    placed = P(("lists", "seq"), None)
    return jax.shard_map(
        on_device,
        mesh=mesh,
        in_specs=(placed,) * 4,
        out_specs=(placed,) * 3,
        check_vma=False,
    )
```

time: 176 us -> 38.5 us (0.22)
  matrix products: 78.7 us -> 0 us
  waiting for transfers between devices: 40.6 us -> 2.58 us
  Pallas kernels: 0 us -> 26.4 us
  local copies, waits for them, and re-layouts: 22.6 us -> 0 us
  other arithmetic: 19.6 us -> 0 us
  between operations: 14.1 us -> 0.97 us
  starting transfers between devices: 0.08 us -> 8.42 us
    dot_general x9 -> x0, matrix products: 78.7 us -> none  [the longest x1 12.8 us: on_device(): jnp.einsum('ynv,vyq->nyq', weight_gradients, lookup_per_position, preferr...]
    all_gather x2 -> x0, waiting for transfers between devices: 40.5 us -> none  [carried_in(): gathered = lax.all_gather(part, axis)]
    pallas_call x0 -> x14, Pallas kernels: none -> 26.4 us  [the longest x8 11.1 us: call(): pl.pallas_call(kernel, out_shape=out, in_specs=[IN_VMEM] * len(operands)...]
    add x7 -> x0, other arithmetic: 18.6 us -> none  [add_states(): return earlier + later_state]
    unnamed x5 -> x0, local copies, waits for them, and re-layouts: 15.8 us -> none
    ppermute x0 -> x10, starting transfers between devices: none -> 8.42 us  [trade(): return lax.ppermute(value, 'seq', [(i, i ^ distance) for i in range(count)])]
    reshape x1 -> x0, local copies, waits for them, and re-layouts: 4.64 us -> none  [on_device(): gradient_token_rows = out_grad.reshape(shape3)]
    ppermute x0 -> x10, waiting for transfers between devices: none -> 2.58 us  [trade(): return lax.ppermute(value, 'seq', [(i, i ^ distance) for i in range(count)])]
  transfers between devices with their start and end apart: 2 -> 10, of which waited for: 1 -> 1; matrix products, arithmetic and copies ran while one was open for 42% -> 0% of each run, Pallas kernels for 0% -> 57%
where the time goes in v2:
time: 38.5 us; the launch traced here: 38.3 us
  Pallas kernels  26.4 us (69%)
  starting transfers between devices  8.42 us (22%)
  waiting for transfers between devices  2.58 us (7%)
  between operations  0.97 us (3%)
    pallas_call x8, Pallas kernels, call(): pl.pallas_call(kernel, out_shape=out, in_specs=[IN_VMEM] * len(operands)...  11.1 us
    ppermute x10, starting transfers between devices, trade(): return lax.ppermute(value, 'seq', [(i, i ^ distance) for i in range(count)])  8.42 us
    pallas_call x3, Pallas kernels, finish(): pl.pallas_call(functools.partial(finish_kernel, scale, chunk, halves), ou...  7.22 us
    pallas_call x2, Pallas kernels, states(): pl.pallas_call(functools.partial(states_kernel, mine, chunk), out_shape=l...  4.63 us
    pallas_call x1, Pallas kernels, states_both(): pl.pallas_call(functools.partial(states_both_kernel, chunk), out_shape=(l...  3.39 us
    ppermute x10, waiting for transfers between devices, trade(): return lax.ppermute(value, 'seq', [(i, i ^ distance) for i in range(count)])  2.58 us
  transfers between devices with their start and end apart: 10, of which 1 were waited for; matrix products, arithmetic and copies ran while one was open for 0% of the time, Pallas kernels for 57%

profile of v2, /device:TPU:0, one launch (start us, length us, event | category | flops | bytes accessed | tf_op | source)
XLA Modules:
  0.0 38.3 jit_solution(17558802977955532598)
XLA Ops:
  0.6 2.3 %states.2 = (bf16[768,512]{1,0:T(8,128)(2,1)S(1)}, bf16[768,512]{1,0:T(8,128)(2,1)S(1)}, bf16[768,512]{1,0:T(8,128)(2,1)S(1)}, bf16[768,512]{1,0:T(8,128)(2,1)S(...) custom-call(bf16[768,2048]{1,0:T(8,128)(2,1)} %refs_0_.5, ...), custom_call_target="tpu_custom_call" | custom-call | flops 20000000000 | bytes 1000 | tf_op jit(solution)/shard_map/states/pallas_call | solution.py:149
  3.0 0.5 %collective-permute-start = (f32[2,4,128,128]{3,2,1,0:T(8,128)S(1)}, f32[2,4,128,128]{3,2,1,0:T(8,128)S(1)}, u32[]{:S(2)}, u32[]{:S(2)}) collective-permute-start(f32[2,4,128,128]{3,2,1,0:T(8,128)S(1)} %get-tuple-element.59.refs_4_), channel_id=1, source_target_pairs={{0,1},{1,0},{2,3},{3,2},{4,5},{5,4},{6,7},{7,6},{8,9},{9,8},{10,11... | collective-permute-start | bytes 1572872 | tf_op jit(solution)/shard_map/ppermute | solution.py:302
  3.5 2.3 %states.3 = (bf16[768,512]{1,0:T(8,128)(2,1)S(1)}, bf16[768,512]{1,0:T(8,128)(2,1)S(1)}, bf16[768,512]{1,0:T(8,128)(2,1)S(1)}, bf16[768,512]{1,0:T(8,128)(2,1)S(...) custom-call(bf16[768,2048]{1,0:T(8,128)(2,1)} %refs_0_.5, ...), custom_call_target="tpu_custom_call" | custom-call | flops 20000000000 | bytes 1000 | tf_op jit(solution)/shard_map/states/pallas_call | solution.py:149
  5.8 0.0 collective-permute-done.sums_in.refs_4_
  5.8 0.1 join.2
  5.9 2.6 %collective-permute-start.1 = (f32[4,128,128]{2,1,0:T(8,128)S(1)}, f32[4,128,128]{2,1,0:T(8,128)S(1)}, u32[]{:S(2)}, u32[]{:S(2)}) collective-permute-start(f32[4,128,128]{2,1,0:T(8,128)S(1)} %get-tuple-element.61.refs_4_), channel_id=1, source_target_pairs={{0,2},{1,3},{2,0},{3,1},{4,6},{5,7},{6,4},{7,5},{8,10},{9,11},{10,... | collective-permute-start | bytes 786440 | tf_op jit(solution)/shard_map/ppermute | solution.py:302
  8.5 1.5 %collective-permute-start.6 = (f32[4,128,128]{2,1,0:T(8,128)S(1)}, f32[4,128,128]{2,1,0:T(8,128)S(1)}, u32[]{:S(2)}, u32[]{:S(2)}) collective-permute-start(f32[4,128,128]{2,1,0:T(8,128)S(1)} %get-tuple-element.62.refs_5_), channel_id=1, source_target_pairs={{0,4},{1,5},{2,6},{3,7},{4,0},{5,1},{6,2},{7,3},{8,12},{9,13},{10,... | collective-permute-start | bytes 786440 | tf_op jit(solution)/shard_map/ppermute | solution.py:302
  10.0 0.0 collective-permute-start.7
  10.0 3.4 %states_both.1 = (bf16[768,512]{1,0:T(8,128)(2,1)S(1)}, bf16[768,512]{1,0:T(8,128)(2,1)S(1)}, bf16[768,512]{1,0:T(8,128)(2,1)S(1)}, bf16[768,512]{1,0:T(8,128)(2...) custom-call(bf16[768,2048]{1,0:T(8,128)(2,1)} %refs_0_.5, ...), custom_call_target="tpu_custom_call" | custom-call | flops 20000000000 | bytes 1000 | tf_op jit(solution)/shard_map/states_both/pallas_call | solution.py:171
  13.4 0.1 collective-permute-start.2
  13.5 2.6 %within.4 = (f32[768,512]{1,0:T(8,128)S(1)}, f32[768,512]{1,0:T(8,128)S(1)}, f32[768,512]{1,0:T(8,128)S(1)}) custom-call(bf16[768,512]{1,0:T(8,128)(2,1)S(1)} %get-tuple-element.74.refs_0_, bf16[768,512]{1,0:T(8,128)(2,1)S(1)} %get-tuple-element.75.refs_1_.refs_9_, bf16[768,512]{1,0:T(8,128)(2,1)S(1)} %get-tuple-element.76.refs_2_.refs_10_, ...), custom_call_target="tpu_custom_call" | custom-call | flops 20000000000 | bytes 1000 | tf_op jit(solution)/shard_map/within/pallas_call | solution.py:59
  16.1 0.0 collective-permute-done.2.sums_in.refs_4_
  16.1 0.1 join.3
  16.2 2.0 %collective-permute-start.3 = (f32[4,128,128]{2,1,0:T(8,128)S(1)}, f32[4,128,128]{2,1,0:T(8,128)S(1)}, u32[]{:S(2)}, u32[]{:S(2)}) collective-permute-start(f32[4,128,128]{2,1,0:T(8,128)S(1)} %get-tuple-element.79.refs_5_), channel_id=1, source_target_pairs={{0,2},{1,3},{2,0},{3,1},{4,6},{5,7},{6,4},{7,5},{8,10},{9,11},{10,... | collective-permute-start | bytes 786440 | tf_op jit(solution)/shard_map/ppermute | solution.py:302
  18.2 1.5 %collective-permute-start.4 = (f32[4,128,128]{2,1,0:T(8,128)S(1)}, f32[4,128,128]{2,1,0:T(8,128)S(1)}, u32[]{:S(2)}, u32[]{:S(2)}) collective-permute-start(f32[4,128,128]{2,1,0:T(8,128)S(1)} %get-tuple-element.80.refs_6_), channel_id=1, source_target_pairs={{0,4},{1,5},{2,6},{3,7},{4,0},{5,1},{6,2},{7,3},{8,12},{9,13},{10,... | collective-permute-start | bytes 786440 | tf_op jit(solution)/shard_map/ppermute | solution.py:302
  19.7 0.0 collective-permute-done.1.refs_4_.refs_0_
  19.7 0.0 collective-permute-start.5
  19.8 2.6 %within.5 = (f32[768,512]{1,0:T(8,128)S(1)}, f32[768,512]{1,0:T(8,128)S(1)}, f32[768,512]{1,0:T(8,128)S(1)}) custom-call(bf16[768,512]{1,0:T(8,128)(2,1)S(1)} %get-tuple-element.68.refs_0_, bf16[768,512]{1,0:T(8,128)(2,1)S(1)} %get-tuple-element.69.refs_1_.refs_0_, bf16[768,512]{1,0:T(8,128)(2,1)S(1)} %get-tuple-element.70.refs_2_.refs_1_, ...), custom_call_target="tpu_custom_call" | custom-call | flops 20000000000 | bytes 1000 | tf_op jit(solution)/shard_map/within/pallas_call | solution.py:59
  22.4 2.6 %within.6 = (f32[768,512]{1,0:T(8,128)S(1)}, f32[768,512]{1,0:T(8,128)S(1)}, f32[768,512]{1,0:T(8,128)S(1)}) custom-call(bf16[768,512]{1,0:T(8,128)(2,1)S(1)} %get-tuple-element.67.refs_0_, bf16[768,512]{1,0:T(8,128)(2,1)S(1)} %get-tuple-element.64.refs_1_.refs_0_, bf16[768,512]{1,0:T(8,128)(2,1)S(1)} %get-tuple-element.65.refs_2_.refs_1_, ...), custom_call_target="tpu_custom_call" | custom-call | flops 20000000000 | bytes 1000 | tf_op jit(solution)/shard_map/within/pallas_call | solution.py:59
  25.0 0.0 collective-permute-done.6.refs_1_
  25.0 0.0 collective-permute-done.7.refs_2_
  25.0 0.3 combine.2
  25.4 0.1 collective-permute-start.8
  25.5 2.6 %within.7 = (f32[768,512]{1,0:T(8,128)S(1)}, f32[768,512]{1,0:T(8,128)S(1)}, f32[768,512]{1,0:T(8,128)S(1)}) custom-call(bf16[768,512]{1,0:T(8,128)(2,1)S(1)} %get-tuple-element.97.refs_0_, bf16[768,512]{1,0:T(8,128)(2,1)S(1)} %get-tuple-element.98.refs_1_.refs_0_, bf16[768,512]{1,0:T(8,128)(2,1)S(1)} %get-tuple-element.99.refs_2_.refs_1_, ...), custom_call_target="tpu_custom_call" | custom-call | flops 20000000000 | bytes 1000 | tf_op jit(solution)/shard_map/within/pallas_call | solution.py:59
  28.1 0.0 collective-permute-done.8.refs_15_
  28.1 3.0 %finish.3 = (bf16[768,2048]{1,0:T(8,128)(2,1)}, bf16[768,2048]{1,0:T(8,128)(2,1)}, bf16[768,2048]{1,0:T(8,128)(2,1)}) custom-call(bf16[768,512]{1,0:T(8,128)(2,1)S(1)} %get-tuple-element.69.refs_1_.refs_0_, bf16[768,512]{1,0:T(8,128)(2,1)S(1)} %get-tuple-element.70.refs_2_.refs_1_, bf16[768,512]{1,0:T(8,128)(2,1)S(1)} %get-tuple-element.71.refs_3_.refs_2_, ...), custom_call_target="tpu_custom_call" | custom-call | flops 20000000000 | bytes 1000 | tf_op jit(solution)/shard_map/finish/pallas_call | solution.py:278
  31.2 0.0 collective-permute-done.3.refs_0_
  31.2 2.6 %collective-permute-done.4.refs_1_ = f32[4,128,128]{2,1,0:T(8,128)S(1)} collective-permute-done((f32[4,128,128]{2,1,0:T(8,128)S(1)}, f32[4,128,128]{2,1,0:T(8,128)S(1)}, u32[]{:S(2)}, u32[]{:S(2)}) %collective-permute-start.4) | collective-permute-done | bytes 262176 | tf_op jit(solution)/shard_map/ppermute | solution.py:302
  33.7 0.0 collective-permute-done.5.refs_2_
  33.7 0.2 combine.3
  33.9 0.1 collective-permute-start.9
  34.0 2.1 %finish.4 = (bf16[768,2048]{1,0:T(8,128)(2,1)}, bf16[768,2048]{1,0:T(8,128)(2,1)}, bf16[768,2048]{1,0:T(8,128)(2,1)}) custom-call(bf16[768,512]{1,0:T(8,128)(2,1)S(1)} %get-tuple-element.98.refs_1_.refs_0_, bf16[768,512]{1,0:T(8,128)(2,1)S(1)} %get-tuple-element.99.refs_2_.refs_1_, ...), custom_call_target="tpu_custom_call", output_to_operand_aliasing={{0}: (9, {}), {1}: (10, {}), {2}: (11, {})} | custom-call | flops 20000000000 | bytes 1000 | tf_op jit(solution)/shard_map/finish/pallas_call | solution.py:278
  36.1 0.0 collective-permute-done.9.refs_6_
  36.1 2.1 %finish.5 = (bf16[768,2048]{1,0:T(8,128)(2,1)}, bf16[768,2048]{1,0:T(8,128)(2,1)}, bf16[768,2048]{1,0:T(8,128)(2,1)}) custom-call(bf16[768,512]{1,0:T(8,128)(2,1)S(1)} %get-tuple-element.64.refs_1_.refs_0_, bf16[768,512]{1,0:T(8,128)(2,1)S(1)} %get-tuple-element.65.refs_2_.refs_1_, ...), custom_call_target="tpu_custom_call", output_to_operand_aliasing={{0}: (9, {}), {1}: (10, {}), {2}: (11, {})} | custom-call | flops 20000000000 | bytes 1000 | tf_op jit(solution)/shard_map/finish/pallas_call | solution.py:278
Async XLA Ops:
  3.0 2.8 %collective-permute-start = (f32[2,4,128,128]{3,2,1,0:T(8,128)S(1)}, f32[2,4,128,128]{3,2,1,0:T(8,128)S(1)}, u32[]{:S(2)}, u32[]{:S(2)}) collective-permute-start(f32[2,4,128,128]{3,2,1,0:T(8,128)S(1)} %get-tuple-element.59.refs_4_), channel_id=1, source_target_pairs={{0,1},{1,0},{2,3},{3,2},{4,5},{5,4},{6,7},{7,6},{8,9},{9,8},{10,11... | collective-permute-start | bytes 1572872 | tf_op jit(solution)/shard_map/ppermute | solution.py:302
  5.9 13.8 %collective-permute-start.1 = (f32[4,128,128]{2,1,0:T(8,128)S(1)}, f32[4,128,128]{2,1,0:T(8,128)S(1)}, u32[]{:S(2)}, u32[]{:S(2)}) collective-permute-start(f32[4,128,128]{2,1,0:T(8,128)S(1)} %get-tuple-element.61.refs_4_), channel_id=1, source_target_pairs={{0,2},{1,3},{2,0},{3,1},{4,6},{5,7},{6,4},{7,5},{8,10},{9,11},{10,... | collective-permute-start | bytes 786440 | tf_op jit(solution)/shard_map/ppermute | solution.py:302
  8.5 16.6 %collective-permute-start.6 = (f32[4,128,128]{2,1,0:T(8,128)S(1)}, f32[4,128,128]{2,1,0:T(8,128)S(1)}, u32[]{:S(2)}, u32[]{:S(2)}) collective-permute-start(f32[4,128,128]{2,1,0:T(8,128)S(1)} %get-tuple-element.62.refs_5_), channel_id=1, source_target_pairs={{0,4},{1,5},{2,6},{3,7},{4,0},{5,1},{6,2},{7,3},{8,12},{9,13},{10,... | collective-permute-start | bytes 786440 | tf_op jit(solution)/shard_map/ppermute | solution.py:302
  10.0 15.0 %collective-permute-start.7 = (f32[4,128,128]{2,1,0:T(8,128)S(1)}, f32[4,128,128]{2,1,0:T(8,128)S(1)}, u32[]{:S(2)}, u32[]{:S(2)}) collective-permute-start(f32[4,128,128]{2,1,0:T(8,128)S(1)} %get-tuple-element.63.refs_6_), channel_id=1, source_target_pairs={{0,6},{1,7},{2,4},{3,5},{4,2},{5,3},{6,0},{7,1},{8,14},{9,15},{10,... | collective-permute-start | bytes 786440 | tf_op jit(solution)/shard_map/ppermute | solution.py:302
  13.4 2.7 %collective-permute-start.2 = (f32[2,4,128,128]{3,2,1,0:T(8,128)S(1)}, f32[2,4,128,128]{3,2,1,0:T(8,128)S(1)}, u32[]{:S(2)}, u32[]{:S(2)}) collective-permute-start(f32[2,4,128,128]{3,2,1,0:T(8,128)S(1)} %get-tuple-element.73.refs_4_), channel_id=1, source_target_pairs={{0,1},{1,0},{2,3},{3,2},{4,5},{5,4},{6,7},{7,6},{8,9},{9,8},{10,11... | collective-permute-start | bytes 1572872 | tf_op jit(solution)/shard_map/ppermute | solution.py:302
  16.2 15.0 %collective-permute-start.3 = (f32[4,128,128]{2,1,0:T(8,128)S(1)}, f32[4,128,128]{2,1,0:T(8,128)S(1)}, u32[]{:S(2)}, u32[]{:S(2)}) collective-permute-start(f32[4,128,128]{2,1,0:T(8,128)S(1)} %get-tuple-element.79.refs_5_), channel_id=1, source_target_pairs={{0,2},{1,3},{2,0},{3,1},{4,6},{5,7},{6,4},{7,5},{8,10},{9,11},{10,... | collective-permute-start | bytes 786440 | tf_op jit(solution)/shard_map/ppermute | solution.py:302
  18.2 15.5 %collective-permute-start.4 = (f32[4,128,128]{2,1,0:T(8,128)S(1)}, f32[4,128,128]{2,1,0:T(8,128)S(1)}, u32[]{:S(2)}, u32[]{:S(2)}) collective-permute-start(f32[4,128,128]{2,1,0:T(8,128)S(1)} %get-tuple-element.80.refs_6_), channel_id=1, source_target_pairs={{0,4},{1,5},{2,6},{3,7},{4,0},{5,1},{6,2},{7,3},{8,12},{9,13},{10,... | collective-permute-start | bytes 786440 | tf_op jit(solution)/shard_map/ppermute | solution.py:302
  19.7 14.0 %collective-permute-start.5 = (f32[4,128,128]{2,1,0:T(8,128)S(1)}, f32[4,128,128]{2,1,0:T(8,128)S(1)}, u32[]{:S(2)}, u32[]{:S(2)}) collective-permute-start(f32[4,128,128]{2,1,0:T(8,128)S(1)} %get-tuple-element.81.refs_7_), channel_id=1, source_target_pairs={{0,6},{1,7},{2,4},{3,5},{4,2},{5,3},{6,0},{7,1},{8,14},{9,15},{10,... | collective-permute-start | bytes 786440 | tf_op jit(solution)/shard_map/ppermute | solution.py:302
  25.4 2.7 %collective-permute-start.8 = (f32[2,4,128,128]{3,2,1,0:T(8,128)S(1)}, f32[2,4,128,128]{3,2,1,0:T(8,128)S(1)}, u32[]{:S(2)}, u32[]{:S(2)}) collective-permute-start(f32[2,4,128,128]{3,2,1,0:T(8,128)S(1)} %get-tuple-element.93), channel_id=1, source_target_pairs={{0,1},{1,0},{2,3},{3,2},{4,5},{5,4},{6,7},{7,6},{8,9},{9,8},{10,11... | collective-permute-start | bytes 1572872 | tf_op jit(solution)/shard_map/ppermute | solution.py:302
  33.9 2.2 %collective-permute-start.9 = (f32[2,4,128,128]{3,2,1,0:T(8,128)S(1)}, f32[2,4,128,128]{3,2,1,0:T(8,128)S(1)}, u32[]{:S(2)}, u32[]{:S(2)}) collective-permute-start(f32[2,4,128,128]{3,2,1,0:T(8,128)S(1)} %get-tuple-element.102), channel_id=1, source_target_pairs={{0,1},{1,0},{2,3},{3,2},{4,5},{5,4},{6,7},{7,6},{8,9},{9,8},{10,11... | collective-permute-start | bytes 1572872 | tf_op jit(solution)/shard_map/ppermute | solution.py:302

commit v3 on v2

v3 whole, which is shorter than its diff:
```python
import functools

import jax
import jax.numpy as jnp
from jax import lax
from jax.experimental import pallas as pl
from jax.experimental.pallas import tpu as pltpu
from jax.sharding import PartitionSpec as P

HEADS = 16
HEAD_DIM = 128
HALF = HEADS // 2
COLUMNS = HALF * HEAD_DIM
GROUP = HALF // 2
SUB = 256
PARTIAL = jnp.float32

TN = (((0,), (0,)), ((), ()))
NT = (((1,), (1,)), ((), ()))
NN = (((1,), (0,)), ((), ()))

IN_VMEM = pl.BlockSpec(memory_space=pltpu.VMEM)
ANYWHERE = pl.BlockSpec(memory_space=pl.ANY)
SHORT = pl.CostEstimate(flops=1000, bytes_accessed=1000, transcendentals=0)
LONG = pl.CostEstimate(flops=2 * 10**10, bytes_accessed=1000, transcendentals=0)


def dot(left, right, dims):
    return lax.dot_general(left, right, dims, preferred_element_type=jnp.float32)


def state_of(heads):
    return pltpu.VMEM((2, heads, HEAD_DIM, HEAD_DIM), jnp.float32)


def head_columns(head):
    return pl.ds(head * HEAD_DIM, HEAD_DIM)


def my_core():
    return lax.rem(lax.axis_index("seq"), 2)


def my_pair():
    return lax.div(lax.axis_index("seq"), 2)


def first_column(square, mine, group):
    half = my_core() if mine else 1 - my_core()
    if square:
        pair = my_pair()
        group = jnp.where((pair == 1) | (pair == 2), 1 - group, group)
    return half * COLUMNS + group * (GROUP * HEAD_DIM)


def call(kernel, out, operands, after=(), scratch=(), cost=SHORT, limit=3, name=None):
    return pl.pallas_call(
        kernel,
        out_shape=out,
        in_specs=[IN_VMEM] * len(operands) + [ANYWHERE] * len(after),
        out_specs=[IN_VMEM] * len(out),
        scratch_shapes=list(scratch),
        compiler_params=pltpu.CompilerParams(vmem_limit_bytes=limit << 20),
        cost_estimate=cost,
        name=name,
    )(*operands, *after)


def read(square, mine, group, sources, local, sems):
    width = GROUP * HEAD_DIM
    at = pl.ds(pl.multiple_of(first_column(square, mine, group), width), width)
    copies = []
    for i in (1, 2, 0, 3):
        copy = pltpu.make_async_copy(sources[i].at[:, at], local[i], sems.at[i])
        copy.start()
        copies.append(copy)
    return copies


def sum_up(copies, local, sums, early, late):
    q, k, v, o = local
    subs = q.shape[0] // SUB
    for kind, (left, right) in enumerate(((k, v), (q, o))):
        copies[2 * kind].wait()
        copies[2 * kind + 1].wait()
        order = list(range(subs)) if kind == 0 else list(range(subs - 1, -1, -1))
        for head in range(sums.shape[1]):
            at = head_columns(head)
            total = None
            for sub in order:
                span = pl.ds(sub * SUB, SUB)
                part = dot(left[span, at], right[span, at], TN)
                total = part if total is None else total + part
                if sub != order[-1]:
                    if kind == 0:
                        early[head, sub] = total
                    else:
                        late[head, sub - 1] = total
            sums[kind, head] = total


def work_inside(scale, local, outs):
    (q, k, v, o), (dq, dk, dv) = local, outs
    rows, columns = q.shape
    part = SUB // 2
    at_row = lax.broadcasted_iota(jnp.int32, (SUB, SUB), 0)
    at_column = lax.broadcasted_iota(jnp.int32, (SUB, SUB), 1)
    lower = at_row >= at_column
    upper = at_row <= at_column
    nothing = jnp.zeros((part, HEAD_DIM), jnp.bfloat16)

    def weights_of(unit):
        pair, sub = unit
        span = pl.ds(sub * SUB, SUB)
        weights = []
        for head in (2 * pair, 2 * pair + 1):
            at = head_columns(head)
            grads = jnp.where(lower, scale * dot(o[span, at], v[span, at], NT), 0.0).astype(jnp.bfloat16)
            forward = jnp.where(upper, scale * dot(k[span, at], q[span, at], NT), 0.0).astype(jnp.bfloat16)
            weights.append((grads, grads.T, forward))
        return weights

    def side_by_side(weights, rows):
        left = jnp.concatenate([rows[0], nothing], axis=1)
        right = jnp.concatenate([nothing, rows[1]], axis=1)
        product = dot(jnp.concatenate(weights, axis=1), jnp.concatenate([left, right], axis=0), NN)
        return product[:, :HEAD_DIM], product[:, HEAD_DIM:]

    def lower_product(weights, rows):
        first = side_by_side([w[:part, :part] for w in weights], [r[:part] for r in rows])
        return [
            jnp.concatenate([top, dot(w[part:], r, NN)], axis=0) for top, w, r in zip(first, weights, rows, strict=True)
        ]

    def upper_product(weights, rows):
        last = side_by_side([w[part:, part:] for w in weights], [r[part:] for r in rows])
        return [
            jnp.concatenate([dot(w[:part], r, NN), below], axis=0) for below, w, r in zip(last, weights, rows, strict=True)
        ]

    units = [(pair, sub) for pair in range(columns // HEAD_DIM // 2) for sub in range(rows // SUB)]
    ahead = weights_of(units[0])
    for number, (pair, sub) in enumerate(units):
        grads, grads_t, forward = zip(*ahead, strict=True)
        if number + 1 < len(units):
            ahead = weights_of(units[number + 1])
        span = pl.ds(sub * SUB, SUB)
        places = [head_columns(2 * pair), head_columns(2 * pair + 1)]
        for product, weights, source, out in (
            (lower_product, grads, k, dq),
            (upper_product, grads_t, q, dk),
            (upper_product, forward, o, dv),
        ):
            for at, piece in zip(places, product(weights, [source[span, at] for at in places]), strict=True):
                out[span, at] = piece.astype(PARTIAL)


def shapes_of(rows):
    heads = GROUP
    local = [pltpu.VMEM((rows, heads * HEAD_DIM), jnp.bfloat16)] * 4
    inner = pltpu.VMEM((heads, rows // SUB - 1, HEAD_DIM, HEAD_DIM), jnp.float32)
    partials = [pltpu.VMEM((rows, heads * HEAD_DIM), PARTIAL)] * 3
    return local, [state_of(heads), inner, inner], partials


def states_kernel(square, mine, group, *refs):
    sources, local, sums, sems = refs[:4], refs[-8:-4], refs[-4:-1], refs[-1]
    sum_up(read(square, mine, group, sources, local, sems), local, *sums)


def states(square, mine, group, sources, after):
    local, sums, _ = shapes_of(sources[0].shape[0])
    result = pl.pallas_call(
        functools.partial(states_kernel, square, mine, group),
        out_shape=local + sums,
        in_specs=[ANYWHERE] * (4 + len(after)),
        out_specs=[IN_VMEM] * 7,
        scratch_shapes=[pltpu.SemaphoreType.DMA((4,))],
        compiler_params=pltpu.CompilerParams(vmem_limit_bytes=2 << 20),
        cost_estimate=LONG,
        name="states",
    )(*sources, *after)
    return result[:4], result[4], result[5:]


def states_both_kernel(square, group, *refs):
    sources, parts, sems = refs[:4], (refs[-15:-8], refs[-8:-1]), refs[-1]
    copies = [read(square, bool(mine), group, sources, parts[mine][:4], sems.at[mine]) for mine in range(2)]
    for mine in range(2):
        sum_up(copies[mine], parts[mine][:4], *parts[mine][4:])


def states_both(square, group, sources, after):
    local, sums, _ = shapes_of(sources[0].shape[0])
    result = pl.pallas_call(
        functools.partial(states_both_kernel, square, group),
        out_shape=(local + sums) * 2,
        in_specs=[ANYWHERE] * (4 + len(after)),
        out_specs=[IN_VMEM] * 14,
        scratch_shapes=[pltpu.SemaphoreType.DMA((2, 4))],
        compiler_params=pltpu.CompilerParams(vmem_limit_bytes=2 << 20),
        cost_estimate=LONG,
        name="states_both",
    )(*sources, *after)
    return [(part[:4], part[4], part[5:]) for part in (result[:7], result[7:])]


def within_kernel(scale, *refs):
    work_inside(scale, refs[:4], refs[-3:])


def within(scale, local, after):
    partials = shapes_of(local[0].shape[0])[2]
    return call(functools.partial(within_kernel, scale), partials, local, after, cost=LONG, name="within")


def settle(head, prefix, suffix, sums, sums_in, own, other):
    second = my_core() == 1
    own[0, head] = prefix + jnp.where(second, sums_in[0, head], 0.0)
    own[1, head] = suffix + jnp.where(second, 0.0, sums_in[1, head])
    other[0, head] = prefix + jnp.where(second, 0.0, sums[0, head])
    other[1, head] = suffix + jnp.where(second, sums[1, head], 0.0)


PIECE = pltpu.VMEM((GROUP, HEAD_DIM, HEAD_DIM), jnp.float32)
STATES = [state_of(GROUP)] * 2


def comes_earlier(turn):
    pair = my_pair()
    return jnp.bitwise_xor(pair, turn) < pair


def join_kernel(turns, sums, sums_in, *rest):
    sent = rest[-len(turns) :]
    for head in range(GROUP):
        forward = sums[0, head] + sums_in[0, head]
        backward = sums[1, head] + sums_in[1, head]
        for turn, out in zip(turns, sent, strict=True):
            out[head] = jnp.where(comes_earlier(turn), backward, forward)


def combine_kernel(turns, *refs):
    received, (sums, sums_in) = refs[: len(turns)], refs[len(turns) : len(turns) + 2]
    for head in range(GROUP):
        prefix = jnp.zeros((HEAD_DIM, HEAD_DIM), jnp.float32)
        suffix = jnp.zeros((HEAD_DIM, HEAD_DIM), jnp.float32)
        for turn, value in zip(turns, received, strict=True):
            earlier = comes_earlier(turn)
            prefix = prefix + jnp.where(earlier, value[head], 0.0)
            suffix = suffix + jnp.where(earlier, 0.0, value[head])
        settle(head, prefix, suffix, sums, sums_in, *refs[-2:])


def row_first_kernel(sums, sums_in, *rest):
    lower = lax.div(my_pair(), 2)
    for head in range(GROUP):
        rest[-1][head] = sums[lower, head] + sums_in[lower, head]


def row_second_kernel(sums, sums_in, *rest):
    right = lax.rem(my_pair(), 2)
    for head in range(GROUP):
        rest[-1][head] = sums[right, head] + sums_in[right, head]


def column_kernel(sums, sums_in, from_row, *rest):
    lower = lax.div(my_pair(), 2)
    for head in range(GROUP):
        rest[-1][head] = sums[lower, head] + sums_in[lower, head] + from_row[head]


def row_third_kernel(sums, sums_in, from_column, *rest):
    pair = my_pair()
    outer = (pair == 0) | (pair == 3)
    kind = jnp.where(pair == 1, 1, 0)
    for head in range(GROUP):
        rest[-1][head] = jnp.where(outer, from_column[head], sums[kind, head] + sums_in[kind, head])


def first_states_kernel(sums, sums_in, row_second, column_first, *rest):
    pair = my_pair()
    below, right = pair >= 2, lax.rem(pair, 2) == 1
    for head in range(GROUP):
        row, column = row_second[head], column_first[head]
        prefix = jnp.where(right, row, 0.0) + jnp.where(below, column, 0.0)
        suffix = jnp.where(right, 0.0, row) + jnp.where(below, 0.0, column)
        settle(head, prefix, suffix, sums, sums_in, *rest[-2:])


def second_states_kernel(sums, sums_in, row_first, row_third, column_second, *rest):
    pair = my_pair()
    below, outer = pair >= 2, (pair == 0) | (pair == 3)
    for head in range(GROUP):
        passed = row_third[head] + jnp.where(outer, column_second[head], 0.0)
        prefix = jnp.where(pair == 1, row_first[head], 0.0) + jnp.where(below, passed, 0.0)
        suffix = jnp.where(pair == 2, row_first[head], 0.0) + jnp.where(below, 0.0, passed)
        settle(head, prefix, suffix, sums, sums_in, *rest[-2:])


def finish_kernel(scale, square, group, halves, *refs):
    targets, staged, sems = refs[-7:-4], refs[-4:-1], refs[-1]
    heads = GROUP
    copies = []
    for number, mine in enumerate(halves):
        k, v, o, dq, dk, dv, state, early, late = refs[9 * number : 9 * number + 9]
        rows = k.shape[0]
        subs = rows // SUB
        base = first_column(square, mine, group)
        for head in range(heads):
            at = head_columns(head)
            to = head_columns(number * heads + head)
            for sub in range(subs):
                span = pl.ds(sub * SUB, SUB)
                before, later = state[0, head], state[1, head]
                if sub > 0:
                    before = before + early[head, sub - 1]
                if sub < subs - 1:
                    later = later + late[head, sub]
                before, later = before.astype(jnp.bfloat16), later.astype(jnp.bfloat16)
                pieces = (
                    dq[span, at] + scale * dot(o[span, at], before, NT),
                    dk[span, at] + scale * dot(v[span, at], later, NT),
                    dv[span, at] + scale * dot(k[span, at], later, NN),
                )
                for out, piece in zip(staged, pieces, strict=True):
                    out[span, to] = piece.astype(jnp.bfloat16)
            if head % 2 == 1 or head == heads - 1:
                first, width = (head - head % 2) * HEAD_DIM, (1 + head % 2) * HEAD_DIM
                for i in range(3):
                    copy = pltpu.make_async_copy(
                        staged[i].at[:, pl.ds(number * heads * HEAD_DIM + first, width)],
                        targets[i].at[:, pl.ds(pl.multiple_of(base + first, HEAD_DIM), width)],
                        sems.at[number, head // 2, i],
                    )
                    copy.start()
                    copies.append(copy)
    for copy in copies:
        copy.wait()


def finish(scale, square, group, parts, before):
    rows = parts[0][1][0].shape[0]
    out = [jax.ShapeDtypeStruct((rows, HEADS * HEAD_DIM), jnp.bfloat16)] * 3
    halves = tuple(part[0] for part in parts)
    operands = []
    for _, local, partials, state, inner in parts:
        operands += [*local[1:], *partials, state, *inner]
    width = len(parts) * GROUP * HEAD_DIM
    return pl.pallas_call(
        functools.partial(finish_kernel, scale, square, group, halves),
        out_shape=out,
        in_specs=[IN_VMEM] * len(operands) + [ANYWHERE] * len(before),
        out_specs=[ANYWHERE] * 3,
        scratch_shapes=[pltpu.VMEM((rows, width), jnp.bfloat16)] * 3
        + [pltpu.SemaphoreType.DMA((len(parts), (GROUP + 1) // 2, 3))],
        input_output_aliases={len(operands) + i: i for i in range(len(before))},
        compiler_params=pltpu.CompilerParams(vmem_limit_bytes=(2 + 3 * len(parts)) << 20),
        cost_estimate=LONG,
        name="finish",
    )(*operands, *before)


def on_device(queries, key_rows, value_rows, out_grad):
    count = lax.axis_size("seq")
    square = count == 8
    scale = (HEAD_DIM * queries.shape[0] * count) ** -0.5
    sources = [
        pltpu.with_memory_space_constraint(array, pltpu.HBM) for array in (queries, key_rows, value_rows, out_grad)
    ]

    def trade(value, distance):
        return lax.ppermute(value, "seq", [(i, i ^ distance) for i in range(count)])

    def run(kernel, out, operands, after):
        return call(kernel, out, operands, after, name=(kernel.func if hasattr(kernel, "func") else kernel).__name__)

    local_eo, sums_eo, inner_eo = states(square, False, 0, sources, ())
    sums_e_in = trade(sums_eo, 1)
    local_em, sums_em, inner_em = states(square, True, 0, sources, (sums_eo,))
    both_e = (sums_em, sums_e_in)
    if square:
        (sent,) = run(row_first_kernel, [PIECE], both_e, ())
        row_first = trade(sent, 2)
        after = (sent,)
    else:
        turns = range(1, count // 2)
        sent = run(functools.partial(join_kernel, turns), [PIECE] * len(turns), both_e, ())
        received = [trade(value, 2 * turn) for turn, value in zip(turns, sent, strict=True)]
        after = tuple(sent)

    (local_lo, sums_lo, inner_lo), (local_lm, sums_lm, inner_lm) = states_both(square, 1, sources, after)
    sums_l_in = trade(sums_lo, 1)
    both_l = (sums_lm, sums_l_in)
    partials_eo = within(scale, local_eo, (sums_lo,))
    if square:
        (sent,) = run(row_second_kernel, [PIECE], both_l, (partials_eo[0],))
        row_second = trade(sent, 2)
        (sent,) = run(column_kernel, [PIECE], (*both_l, row_first), (sent,))
        column_first = trade(sent, 4)
        partials_em = within(scale, local_em, (sent,))
        partials_lo = within(scale, local_lo, (partials_em[0],))
        (sent,) = run(column_kernel, [PIECE], (*both_e, row_second), (partials_lo[0],))
        column_second = trade(sent, 4)
        (sent,) = run(row_third_kernel, [PIECE], (*both_e, column_first), (sent,))
        row_third = trade(sent, 2)
        own_e, other_e = run(first_states_kernel, STATES, (*both_e, row_second, column_first), (sent,))
    else:
        sent = run(functools.partial(join_kernel, turns), [PIECE] * len(turns), both_l, (partials_eo[0],))
        received_l = [trade(value, 2 * turn) for turn, value in zip(turns, sent, strict=True)]
        partials_em = within(scale, local_em, tuple(sent))
        partials_lo = within(scale, local_lo, (partials_em[0],))
        kernel = functools.partial(combine_kernel, turns)
        own_e, other_e = run(kernel, STATES, (*received, *both_e), (partials_lo[0],))

    other_e = trade(other_e, 1)
    partials_lm = within(scale, local_lm, (own_e,))
    parts = [(True, local_em, partials_em, own_e, inner_em), (False, local_eo, partials_eo, other_e, inner_eo)]
    done = finish(scale, square, 0, parts, ())

    after = (pltpu.with_memory_space_constraint(done[0], pltpu.HBM), partials_lm[0])
    if square:
        arrived = (row_first, row_third, column_second)
        own_l, other_l = run(second_states_kernel, STATES, (*both_l, *arrived), after)
    else:
        own_l, other_l = run(kernel, STATES, (*received_l, *both_l), after)
    other_l = trade(other_l, 1)
    done = finish(scale, square, 1, [(True, local_lm, partials_lm, own_l, inner_lm)], done)
    return tuple(finish(scale, square, 1, [(False, local_lo, partials_lo, other_l, inner_lo)], done))


def solution(mesh):
    placed = P(("lists", "seq"), None)
    return jax.shard_map(
        on_device,
        mesh=mesh,
        in_specs=(placed,) * 4,
        out_specs=(placed,) * 3,
        check_vma=False,
    )
```

time: 38.5 us -> 36.6 us (0.951)
  Pallas kernels: 26.4 us -> 23.6 us
  waiting for transfers between devices: 2.58 us -> 3.71 us
    pallas_call x8 -> x11, Pallas kernels: 11.1 us -> 8.14 us  [call(): pl.pallas_call(kernel, out_shape=out, in_specs=[IN_VMEM] * len(operands)...]
    ppermute x10 -> x9, waiting for transfers between devices: 2.58 us -> 3.71 us  [trade(): return lax.ppermute(value, 'seq', [(i, i ^ distance) for i in range(count)])]
    ppermute x10 -> x9, starting transfers between devices: 8.42 us -> 8.17 us  [trade(): return lax.ppermute(value, 'seq', [(i, i ^ distance) for i in range(count)])]
  transfers between devices with their start and end apart: 10 -> 9, of which waited for: 1 -> 3; matrix products, arithmetic and copies ran while one was open for 0% -> 0% of each run, Pallas kernels for 57% -> 52%
where the time goes in v3:
time: 36.6 us; the launch traced here: 36.4 us
  Pallas kernels  23.6 us (64%)
  starting transfers between devices  8.17 us (22%)
  waiting for transfers between devices  3.71 us (10%)
  between operations  0.94 us (3%)
    ppermute x9, starting transfers between devices, trade(): return lax.ppermute(value, 'seq', [(i, i ^ distance) for i in range(count)])  8.17 us
    pallas_call x11, Pallas kernels, call(): pl.pallas_call(kernel, out_shape=out, in_specs=[IN_VMEM] * len(operands)...  8.14 us
    pallas_call x3, Pallas kernels, finish(): pl.pallas_call(functools.partial(finish_kernel, scale, square, group, hal...  7.42 us
    pallas_call x2, Pallas kernels, states(): pl.pallas_call(functools.partial(states_kernel, square, mine, group), out...  4.63 us
    ppermute x9, waiting for transfers between devices, trade(): return lax.ppermute(value, 'seq', [(i, i ^ distance) for i in range(count)])  3.71 us
    pallas_call x1, Pallas kernels, states_both(): pl.pallas_call(functools.partial(states_both_kernel, square, group), out_...  3.39 us
  transfers between devices with their start and end apart: 9, of which 3 were waited for; matrix products, arithmetic and copies ran while one was open for 0% of the time, Pallas kernels for 52%

profile of v3, /device:TPU:0, one launch (start us, length us, event | category | flops | bytes accessed | tf_op | source)
XLA Modules:
  0.0 36.4 jit_solution(3334466502733731012)
XLA Ops:
  0.6 2.3 %states.2 = (bf16[768,512]{1,0:T(8,128)(2,1)S(1)}, bf16[768,512]{1,0:T(8,128)(2,1)S(1)}, bf16[768,512]{1,0:T(8,128)(2,1)S(1)}, bf16[768,512]{1,0:T(8,128)(2,1)S(...) custom-call(bf16[768,2048]{1,0:T(8,128)(2,1)} %refs_0_.5, ...), custom_call_target="tpu_custom_call" | custom-call | flops 20000000000 | bytes 1000 | tf_op jit(solution)/shard_map/states/pallas_call | solution.py:173
  3.0 0.5 %collective-permute-start = (f32[2,4,128,128]{3,2,1,0:T(8,128)S(1)}, f32[2,4,128,128]{3,2,1,0:T(8,128)S(1)}, u32[]{:S(2)}, u32[]{:S(2)}) collective-permute-start(f32[2,4,128,128]{3,2,1,0:T(8,128)S(1)} %get-tuple-element.53.refs_4_), channel_id=1, source_target_pairs={{0,1},{1,0},{2,3},{3,2},{4,5},{5,4},{6,7},{7,6},{8,9},{9,8},{10,11... | collective-permute-start | bytes 1572872 | tf_op jit(solution)/shard_map/ppermute | solution.py:373
  3.5 2.3 %states.3 = (bf16[768,512]{1,0:T(8,128)(2,1)S(1)}, bf16[768,512]{1,0:T(8,128)(2,1)S(1)}, bf16[768,512]{1,0:T(8,128)(2,1)S(1)}, bf16[768,512]{1,0:T(8,128)(2,1)S(...) custom-call(bf16[768,2048]{1,0:T(8,128)(2,1)} %refs_0_.5, ...), custom_call_target="tpu_custom_call" | custom-call | flops 20000000000 | bytes 1000 | tf_op jit(solution)/shard_map/states/pallas_call | solution.py:173
  5.8 0.0 collective-permute-done.sums_in
  5.9 2.6 %collective-permute-start.2 = (f32[4,128,128]{2,1,0:T(8,128)S(1)}, f32[4,128,128]{2,1,0:T(8,128)S(1)}, u32[]{:S(2)}, u32[]{:S(2)}) collective-permute-start(f32[4,128,128]{2,1,0:T(8,128)S(1)} %row_first_kernel.1.refs_4_), channel_id=1, source_target_pairs={{0,2},{1,3},{2,0},{3,1},{4,6},{5,7},{6,4},{7,5},{8,10},{9,11},{10,... | collective-permute-start | bytes 786440 | tf_op jit(solution)/shard_map/ppermute | solution.py:373
  8.4 3.4 %states_both.1 = (bf16[768,512]{1,0:T(8,128)(2,1)S(1)}, bf16[768,512]{1,0:T(8,128)(2,1)S(1)}, bf16[768,512]{1,0:T(8,128)(2,1)S(1)}, bf16[768,512]{1,0:T(8,128)(2...) custom-call(bf16[768,2048]{1,0:T(8,128)(2,1)} %refs_0_.5, ...), custom_call_target="tpu_custom_call" | custom-call | flops 20000000000 | bytes 1000 | tf_op jit(solution)/shard_map/states_both/pallas_call | solution.py:195
  11.8 0.3 collective-permute-start.1
  12.1 1.9 %within.4 = (f32[768,512]{1,0:T(8,128)S(1)}, f32[768,512]{1,0:T(8,128)S(1)}, f32[768,512]{1,0:T(8,128)S(1)}) custom-call(bf16[768,512]{1,0:T(8,128)(2,1)S(1)} %get-tuple-element.65.refs_0_, bf16[768,512]{1,0:T(8,128)(2,1)S(1)} %get-tuple-element.66.refs_1_.refs_9_, bf16[768,512]{1,0:T(8,128)(2,1)S(1)} %get-tuple-element.67.refs_2_.refs_10_, ...), custom_call_target="tpu_custom_call" | custom-call | flops 20000000000 | bytes 1000 | tf_op jit(solution)/shard_map/within/pallas_call | solution.py:57
  14.0 0.0 collective-permute-done.1.sums_in
  14.1 0.3 collective-permute-start.4
  14.4 1.0 %collective-permute-done.2.from_row.row_first = f32[4,128,128]{2,1,0:T(8,128)S(1)} collective-permute-done((f32[4,128,128]{2,1,0:T(8,128)S(1)}, f32[4,128,128]{2,1,0:T(8,128)S(1)}, u32[]{:S(2)}, u32[]{:S(2)}) %collective-permute-start.2) | collective-permute-done | bytes 262176 | tf_op jit(solution)/shard_map/ppermute | solution.py:373
  15.4 1.8 %collective-permute-start.3 = (f32[4,128,128]{2,1,0:T(8,128)S(1)}, f32[4,128,128]{2,1,0:T(8,128)S(1)}, u32[]{:S(2)}, u32[]{:S(2)}) collective-permute-start(f32[4,128,128]{2,1,0:T(8,128)S(1)} %column_kernel.2.refs_4_), channel_id=1, source_target_pairs={{0,4},{1,5},{2,6},{3,7},{4,0},{5,1},{6,2},{7,3},{8,12},{9,13},{10,... | collective-permute-start | bytes 786440 | tf_op jit(solution)/shard_map/ppermute | solution.py:373
  17.3 1.9 %within.5 = (f32[768,512]{1,0:T(8,128)S(1)}, f32[768,512]{1,0:T(8,128)S(1)}, f32[768,512]{1,0:T(8,128)S(1)}) custom-call(bf16[768,512]{1,0:T(8,128)(2,1)S(1)} %get-tuple-element.59.refs_0_, bf16[768,512]{1,0:T(8,128)(2,1)S(1)} %get-tuple-element.60.refs_1_.refs_0_, bf16[768,512]{1,0:T(8,128)(2,1)S(1)} %get-tuple-element.61.refs_2_.refs_1_, ...), custom_call_target="tpu_custom_call" | custom-call | flops 20000000000 | bytes 1000 | tf_op jit(solution)/shard_map/within/pallas_call | solution.py:57
  19.2 1.9 %within.6 = (f32[768,512]{1,0:T(8,128)S(1)}, f32[768,512]{1,0:T(8,128)S(1)}, f32[768,512]{1,0:T(8,128)S(1)}) custom-call(bf16[768,512]{1,0:T(8,128)(2,1)S(1)} %get-tuple-element.58.refs_0_, bf16[768,512]{1,0:T(8,128)(2,1)S(1)} %get-tuple-element.55.refs_1_.refs_0_, bf16[768,512]{1,0:T(8,128)(2,1)S(1)} %get-tuple-element.56.refs_2_.refs_1_, ...), custom_call_target="tpu_custom_call" | custom-call | flops 20000000000 | bytes 1000 | tf_op jit(solution)/shard_map/within/pallas_call | solution.py:57
  21.1 1.6 %collective-permute-done.4.from_row.row_second = f32[4,128,128]{2,1,0:T(8,128)S(1)} collective-permute-done((f32[4,128,128]{2,1,0:T(8,128)S(1)}, f32[4,128,128]{2,1,0:T(8,128)S(1)}, u32[]{:S(2)}, u32[]{:S(2)}) %collective-permute-start.4) | collective-permute-done | bytes 262176 | tf_op jit(solution)/shard_map/ppermute | solution.py:373
  22.7 1.5 %collective-permute-start.6 = (f32[4,128,128]{2,1,0:T(8,128)S(1)}, f32[4,128,128]{2,1,0:T(8,128)S(1)}, u32[]{:S(2)}, u32[]{:S(2)}) collective-permute-start(f32[4,128,128]{2,1,0:T(8,128)S(1)} %column_kernel.3.rest_0_), channel_id=1, source_target_pairs={{0,4},{1,5},{2,6},{3,7},{4,0},{5,1},{6,2},{7,3},{8,12},{9,13},{10,... | collective-permute-start | bytes 786440 | tf_op jit(solution)/shard_map/ppermute | solution.py:373
  24.2 0.0 collective-permute-done.3.from_column.column_first
  24.3 1.0 %collective-permute-start.5 = (f32[4,128,128]{2,1,0:T(8,128)S(1)}, f32[4,128,128]{2,1,0:T(8,128)S(1)}, u32[]{:S(2)}, u32[]{:S(2)}) collective-permute-start(f32[4,128,128]{2,1,0:T(8,128)S(1)} %row_third_kernel.1.rest_0_), channel_id=1, source_target_pairs={{0,2},{1,3},{2,0},{3,1},{4,6},{5,7},{6,4},{7,5},{8,10},{9,11},{10,... | collective-permute-start | bytes 786440 | tf_op jit(solution)/shard_map/ppermute | solution.py:373
  25.2 0.1 first_states_kernel.1
  25.4 0.1 collective-permute-start.7
  25.5 1.9 %within.7 = (f32[768,512]{1,0:T(8,128)S(1)}, f32[768,512]{1,0:T(8,128)S(1)}, f32[768,512]{1,0:T(8,128)S(1)}) custom-call(bf16[768,512]{1,0:T(8,128)(2,1)S(1)} %get-tuple-element.85.refs_0_, bf16[768,512]{1,0:T(8,128)(2,1)S(1)} %get-tuple-element.86.refs_1_.refs_0_, bf16[768,512]{1,0:T(8,128)(2,1)S(1)} %get-tuple-element.87.refs_2_.refs_1_, ...), custom_call_target="tpu_custom_call" | custom-call | flops 20000000000 | bytes 1000 | tf_op jit(solution)/shard_map/within/pallas_call | solution.py:57
  27.4 0.0 collective-permute-done.7.refs_15_
  27.4 3.2 %finish.3 = (bf16[768,2048]{1,0:T(8,128)(2,1)}, bf16[768,2048]{1,0:T(8,128)(2,1)}, bf16[768,2048]{1,0:T(8,128)(2,1)}) custom-call(bf16[768,512]{1,0:T(8,128)(2,1)S(1)} %get-tuple-element.60.refs_1_.refs_0_, bf16[768,512]{1,0:T(8,128)(2,1)S(1)} %get-tuple-element.61.refs_2_.refs_1_, bf16[768,512]{1,0:T(8,128)(2,1)S(1)} %get-tuple-element.62.refs_3_.refs_2_, ...), custom_call_target="tpu_custom_call" | custom-call | flops 20000000000 | bytes 1000 | tf_op jit(solution)/shard_map/finish/pallas_call | solution.py:350
  30.6 1.2 %collective-permute-done.5.row_third = f32[4,128,128]{2,1,0:T(8,128)S(1)} collective-permute-done((f32[4,128,128]{2,1,0:T(8,128)S(1)}, f32[4,128,128]{2,1,0:T(8,128)S(1)}, u32[]{:S(2)}, u32[]{:S(2)}) %collective-permute-start.5) | collective-permute-done | bytes 262176 | tf_op jit(solution)/shard_map/ppermute | solution.py:373
  31.8 0.0 collective-permute-done.6.column_second
  31.8 0.2 second_states_kernel.1
  32.0 0.1 collective-permute-start.8
  32.0 2.1 %finish.4 = (bf16[768,2048]{1,0:T(8,128)(2,1)}, bf16[768,2048]{1,0:T(8,128)(2,1)}, bf16[768,2048]{1,0:T(8,128)(2,1)}) custom-call(bf16[768,512]{1,0:T(8,128)(2,1)S(1)} %get-tuple-element.86.refs_1_.refs_0_, bf16[768,512]{1,0:T(8,128)(2,1)S(1)} %get-tuple-element.87.refs_2_.refs_1_, ...), custom_call_target="tpu_custom_call", output_to_operand_aliasing={{0}: (9, {}), {1}: (10, {}), {2}: (11, {})} | custom-call | flops 20000000000 | bytes 1000 | tf_op jit(solution)/shard_map/finish/pallas_call | solution.py:350
  34.1 0.0 collective-permute-done.8.refs_6_
  34.1 2.1 %finish.5 = (bf16[768,2048]{1,0:T(8,128)(2,1)}, bf16[768,2048]{1,0:T(8,128)(2,1)}, bf16[768,2048]{1,0:T(8,128)(2,1)}) custom-call(bf16[768,512]{1,0:T(8,128)(2,1)S(1)} %get-tuple-element.55.refs_1_.refs_0_, bf16[768,512]{1,0:T(8,128)(2,1)S(1)} %get-tuple-element.56.refs_2_.refs_1_, ...), custom_call_target="tpu_custom_call", output_to_operand_aliasing={{0}: (9, {}), {1}: (10, {}), {2}: (11, {})} | custom-call | flops 20000000000 | bytes 1000 | tf_op jit(solution)/shard_map/finish/pallas_call | solution.py:350
  (5 shorter events, 0.2 us)
Async XLA Ops:
  3.0 2.8 %collective-permute-start = (f32[2,4,128,128]{3,2,1,0:T(8,128)S(1)}, f32[2,4,128,128]{3,2,1,0:T(8,128)S(1)}, u32[]{:S(2)}, u32[]{:S(2)}) collective-permute-start(f32[2,4,128,128]{3,2,1,0:T(8,128)S(1)} %get-tuple-element.53.refs_4_), channel_id=1, source_target_pairs={{0,1},{1,0},{2,3},{3,2},{4,5},{5,4},{6,7},{7,6},{8,9},{9,8},{10,11... | collective-permute-start | bytes 1572872 | tf_op jit(solution)/shard_map/ppermute | solution.py:373
  5.9 9.5 %collective-permute-start.2 = (f32[4,128,128]{2,1,0:T(8,128)S(1)}, f32[4,128,128]{2,1,0:T(8,128)S(1)}, u32[]{:S(2)}, u32[]{:S(2)}) collective-permute-start(f32[4,128,128]{2,1,0:T(8,128)S(1)} %row_first_kernel.1.refs_4_), channel_id=1, source_target_pairs={{0,2},{1,3},{2,0},{3,1},{4,6},{5,7},{6,4},{7,5},{8,10},{9,11},{10,... | collective-permute-start | bytes 786440 | tf_op jit(solution)/shard_map/ppermute | solution.py:373
  11.8 2.2 %collective-permute-start.1 = (f32[2,4,128,128]{3,2,1,0:T(8,128)S(1)}, f32[2,4,128,128]{3,2,1,0:T(8,128)S(1)}, u32[]{:S(2)}, u32[]{:S(2)}) collective-permute-start(f32[2,4,128,128]{3,2,1,0:T(8,128)S(1)} %get-tuple-element.64.refs_4_), channel_id=1, source_target_pairs={{0,1},{1,0},{2,3},{3,2},{4,5},{5,4},{6,7},{7,6},{8,9},{9,8},{10,11... | collective-permute-start | bytes 1572872 | tf_op jit(solution)/shard_map/ppermute | solution.py:373
  14.1 8.6 %collective-permute-start.4 = (f32[4,128,128]{2,1,0:T(8,128)S(1)}, f32[4,128,128]{2,1,0:T(8,128)S(1)}, u32[]{:S(2)}, u32[]{:S(2)}) collective-permute-start(f32[4,128,128]{2,1,0:T(8,128)S(1)} %row_second_kernel.1.rest_0_), channel_id=1, source_target_pairs={{0,2},{1,3},{2,0},{3,1},{4,6},{5,7},{6,4},{7,5},{8,10},{9,11},{10,... | collective-permute-start | bytes 786440 | tf_op jit(solution)/shard_map/ppermute | solution.py:373
  15.4 8.8 %collective-permute-start.3 = (f32[4,128,128]{2,1,0:T(8,128)S(1)}, f32[4,128,128]{2,1,0:T(8,128)S(1)}, u32[]{:S(2)}, u32[]{:S(2)}) collective-permute-start(f32[4,128,128]{2,1,0:T(8,128)S(1)} %column_kernel.2.refs_4_), channel_id=1, source_target_pairs={{0,4},{1,5},{2,6},{3,7},{4,0},{5,1},{6,2},{7,3},{8,12},{9,13},{10,... | collective-permute-start | bytes 786440 | tf_op jit(solution)/shard_map/ppermute | solution.py:373
  22.7 9.1 %collective-permute-start.6 = (f32[4,128,128]{2,1,0:T(8,128)S(1)}, f32[4,128,128]{2,1,0:T(8,128)S(1)}, u32[]{:S(2)}, u32[]{:S(2)}) collective-permute-start(f32[4,128,128]{2,1,0:T(8,128)S(1)} %column_kernel.3.rest_0_), channel_id=1, source_target_pairs={{0,4},{1,5},{2,6},{3,7},{4,0},{5,1},{6,2},{7,3},{8,12},{9,13},{10,... | collective-permute-start | bytes 786440 | tf_op jit(solution)/shard_map/ppermute | solution.py:373
  24.3 7.5 %collective-permute-start.5 = (f32[4,128,128]{2,1,0:T(8,128)S(1)}, f32[4,128,128]{2,1,0:T(8,128)S(1)}, u32[]{:S(2)}, u32[]{:S(2)}) collective-permute-start(f32[4,128,128]{2,1,0:T(8,128)S(1)} %row_third_kernel.1.rest_0_), channel_id=1, source_target_pairs={{0,2},{1,3},{2,0},{3,1},{4,6},{5,7},{6,4},{7,5},{8,10},{9,11},{10,... | collective-permute-start | bytes 786440 | tf_op jit(solution)/shard_map/ppermute | solution.py:373
  25.4 2.0 %collective-permute-start.7 = (f32[2,4,128,128]{3,2,1,0:T(8,128)S(1)}, f32[2,4,128,128]{3,2,1,0:T(8,128)S(1)}, u32[]{:S(2)}, u32[]{:S(2)}) collective-permute-start(f32[2,4,128,128]{3,2,1,0:T(8,128)S(1)} %get-tuple-element.81), channel_id=1, source_target_pairs={{0,1},{1,0},{2,3},{3,2},{4,5},{5,4},{6,7},{7,6},{8,9},{9,8},{10,11... | collective-permute-start | bytes 1572872 | tf_op jit(solution)/shard_map/ppermute | solution.py:373
  32.0 2.2 %collective-permute-start.8 = (f32[2,4,128,128]{3,2,1,0:T(8,128)S(1)}, f32[2,4,128,128]{3,2,1,0:T(8,128)S(1)}, u32[]{:S(2)}, u32[]{:S(2)}) collective-permute-start(f32[2,4,128,128]{3,2,1,0:T(8,128)S(1)} %get-tuple-element.90), channel_id=1, source_target_pairs={{0,1},{1,0},{2,3},{3,2},{4,5},{5,4},{6,7},{7,6},{8,9},{9,8},{10,11... | collective-permute-start | bytes 1572872 | tf_op jit(solution)/shard_map/ppermute | solution.py:373

commit v4 on v3

v4 whole, which is shorter than its diff:
```python
import functools

import jax
import jax.numpy as jnp
from jax import lax
from jax.experimental import pallas as pl
from jax.experimental.pallas import tpu as pltpu
from jax.sharding import PartitionSpec as P

HEADS = 16
HEAD_DIM = 128
HALF = HEADS // 2
COLUMNS = HALF * HEAD_DIM
GROUP = HALF // 2
SUB = 256
PARTIAL = jnp.float32

TN = (((0,), (0,)), ((), ()))
NT = (((1,), (1,)), ((), ()))
NN = (((1,), (0,)), ((), ()))

IN_VMEM = pl.BlockSpec(memory_space=pltpu.VMEM)
ANYWHERE = pl.BlockSpec(memory_space=pl.ANY)
SHORT = pl.CostEstimate(flops=1000, bytes_accessed=1000, transcendentals=0)
LONG = pl.CostEstimate(flops=2 * 10**10, bytes_accessed=1000, transcendentals=0)


def dot(left, right, dims):
    return lax.dot_general(left, right, dims, preferred_element_type=jnp.float32)


def state_of(heads):
    return pltpu.VMEM((2, heads, HEAD_DIM, HEAD_DIM), jnp.float32)


def head_columns(head):
    return pl.ds(head * HEAD_DIM, HEAD_DIM)


def my_core():
    return lax.rem(lax.axis_index("seq"), 2)


def my_pair():
    return lax.div(lax.axis_index("seq"), 2)


def first_column(square, mine, group):
    half = my_core() if mine else 1 - my_core()
    if square:
        pair = my_pair()
        group = jnp.where((pair == 1) | (pair == 2), 1 - group, group)
    return half * COLUMNS + group * (GROUP * HEAD_DIM)


def my_row(square):
    return lax.div(my_pair(), 2) if square else jnp.int32(0)


PIECE = pltpu.VMEM((GROUP, HEAD_DIM, HEAD_DIM), jnp.float32)
STATES = [state_of(GROUP)] * 2


def call(kernel, out, operands, after=(), scratch=(), cost=SHORT, limit=3, name=None):
    return pl.pallas_call(
        kernel,
        out_shape=out,
        in_specs=[IN_VMEM] * len(operands) + [ANYWHERE] * len(after),
        out_specs=[IN_VMEM] * len(out),
        scratch_shapes=list(scratch),
        compiler_params=pltpu.CompilerParams(vmem_limit_bytes=limit << 20),
        cost_estimate=cost,
        name=name,
    )(*operands, *after)


KINDS = ((1, 2), (0, 3))


def read(square, mine, group, kind, sources, local, sems):
    width = GROUP * HEAD_DIM
    at = pl.ds(pl.multiple_of(first_column(square, mine, group), width), width)
    return [pltpu.make_async_copy(sources[i].at[:, at], local[i], sems.at[i]) for i in KINDS[kind]]


def start_all(copies):
    for copy in copies:
        copy.start()


def sum_kind(kind, copies, local, sums, early, late):
    for copy in copies:
        copy.wait()
    q, k, v, o = local
    left, right = ((k, v), (q, o))[kind]
    subs = q.shape[0] // SUB
    order = list(range(subs)) if kind == 0 else list(range(subs - 1, -1, -1))
    for head in range(GROUP):
        at = head_columns(head)
        total = None
        for sub in order:
            span = pl.ds(sub * SUB, SUB)
            part = dot(left[span, at], right[span, at], TN)
            total = part if total is None else total + part
            if sub != order[-1]:
                if kind == 0:
                    early[head, sub] = total
                else:
                    late[head, sub - 1] = total
        sums[head] = total


def work_inside(scale, local, outs, pairs):
    (q, k, v, o), (dq, dk, dv) = local, outs
    rows = q.shape[0]
    part = SUB // 2
    at_row = lax.broadcasted_iota(jnp.int32, (SUB, SUB), 0)
    at_column = lax.broadcasted_iota(jnp.int32, (SUB, SUB), 1)
    lower = at_row >= at_column
    upper = at_row <= at_column
    nothing = jnp.zeros((part, HEAD_DIM), jnp.bfloat16)

    def weights_of(unit):
        pair, sub = unit
        span = pl.ds(sub * SUB, SUB)
        weights = []
        for head in (2 * pair, 2 * pair + 1):
            at = head_columns(head)
            grads = jnp.where(lower, scale * dot(o[span, at], v[span, at], NT), 0.0).astype(jnp.bfloat16)
            forward = jnp.where(upper, scale * dot(k[span, at], q[span, at], NT), 0.0).astype(jnp.bfloat16)
            weights.append((grads, grads.T, forward))
        return weights

    def side_by_side(weights, rows):
        left = jnp.concatenate([rows[0], nothing], axis=1)
        right = jnp.concatenate([nothing, rows[1]], axis=1)
        product = dot(jnp.concatenate(weights, axis=1), jnp.concatenate([left, right], axis=0), NN)
        return product[:, :HEAD_DIM], product[:, HEAD_DIM:]

    def lower_product(weights, rows):
        first = side_by_side([w[:part, :part] for w in weights], [r[:part] for r in rows])
        return [
            jnp.concatenate([top, dot(w[part:], r, NN)], axis=0) for top, w, r in zip(first, weights, rows, strict=True)
        ]

    def upper_product(weights, rows):
        last = side_by_side([w[part:, part:] for w in weights], [r[part:] for r in rows])
        return [
            jnp.concatenate([dot(w[:part], r, NN), below], axis=0) for below, w, r in zip(last, weights, rows, strict=True)
        ]

    units = [(pair, sub) for pair in pairs for sub in range(rows // SUB)]
    ahead = weights_of(units[0])
    for number, (pair, sub) in enumerate(units):
        grads, grads_t, forward = zip(*ahead, strict=True)
        if number + 1 < len(units):
            ahead = weights_of(units[number + 1])
        span = pl.ds(sub * SUB, SUB)
        places = [head_columns(2 * pair), head_columns(2 * pair + 1)]
        for product, weights, source, out in (
            (lower_product, grads, k, dq),
            (upper_product, grads_t, q, dk),
            (upper_product, forward, o, dv),
        ):
            for at, piece in zip(places, product(weights, [source[span, at] for at in places]), strict=True):
                out[span, at] = piece.astype(PARTIAL)


def part_shapes(rows):
    inner = pltpu.VMEM((GROUP, rows // SUB - 1, HEAD_DIM, HEAD_DIM), jnp.float32)
    return [pltpu.VMEM((rows, GROUP * HEAD_DIM), jnp.bfloat16)] * 4 + [inner] * 2


def states_first_kernel(square, mine, *refs):
    sources, part, sums, sems = refs[:4], refs[-8:-2], refs[-2], refs[-1]
    row = my_row(square)
    for kind in range(2):
        copies = read(square, mine, 0, kind, sources, part[:4], sems)

        @pl.when(row == kind)
        def _():
            start_all(copies)
            sum_kind(kind, copies, part[:4], sums, *part[4:])


def states_first(square, mine, sources, after):
    out = part_shapes(sources[0].shape[0]) + [PIECE]
    *part, sums = pl.pallas_call(
        functools.partial(states_first_kernel, square, mine),
        out_shape=out,
        in_specs=[ANYWHERE] * (4 + len(after)),
        out_specs=[IN_VMEM] * len(out),
        scratch_shapes=[pltpu.SemaphoreType.DMA((4,))],
        compiler_params=pltpu.CompilerParams(vmem_limit_bytes=2 << 20),
        cost_estimate=LONG,
        name="states_first",
    )(*sources, *after)
    return part, sums


def states_second_kernel(square, *refs):
    sources, parts, sums, sems = refs[:4], (refs[-15:-9], refs[-9:-3]), refs[-3:-1], refs[-1]
    copies = {}
    for mine in range(2):
        for kind in range(2):
            copies[mine, kind] = read(square, bool(mine), 1, kind, sources, parts[mine][:4], sems.at[mine])
            start_all(copies[mine, kind])
    for mine in range(2):
        for kind in range(2):
            sum_kind(kind, copies[mine, kind], parts[mine][:4], sums[mine].at[kind], *parts[mine][4:])


def states_second(square, sources, after):
    out = part_shapes(sources[0].shape[0]) * 2 + [state_of(GROUP)] * 2
    result = pl.pallas_call(
        functools.partial(states_second_kernel, square),
        out_shape=out,
        in_specs=[ANYWHERE] * (4 + len(after)),
        out_specs=[IN_VMEM] * len(out),
        scratch_shapes=[pltpu.SemaphoreType.DMA((2, 4))],
        compiler_params=pltpu.CompilerParams(vmem_limit_bytes=2 << 20),
        cost_estimate=LONG,
        name="states_second",
    )(*sources, *after)
    return result[:6], result[6:12], *result[12:]


def states_other_kernel(square, *refs):
    sources, parts, sums, sems = refs[:4], (refs[-15:-9], refs[-9:-3]), refs[-3:-1], refs[-1]
    row = my_row(square)
    copies = {}
    for mine in range(2):
        for kind in range(2):
            copies[mine, kind] = read(square, bool(mine), 0, kind, sources, parts[mine][:4], sems.at[mine])
    for kind in range(2):

        @pl.when(row != kind)
        def _():
            for mine in range(2):
                start_all(copies[mine, kind])
            for mine in range(2):
                sum_kind(kind, copies[mine, kind], parts[mine][:4], sums[mine], *parts[mine][4:])


def states_other(square, sources, other, mine, after):
    out = part_shapes(sources[0].shape[0]) * 2 + [PIECE] * 2
    result = pl.pallas_call(
        functools.partial(states_other_kernel, square),
        out_shape=out,
        in_specs=[ANYWHERE] * 4 + [IN_VMEM] * 12 + [ANYWHERE] * len(after),
        out_specs=[IN_VMEM] * len(out),
        scratch_shapes=[pltpu.SemaphoreType.DMA((2, 4))],
        input_output_aliases={4 + i: i for i in range(12)},
        compiler_params=pltpu.CompilerParams(vmem_limit_bytes=2 << 20),
        cost_estimate=LONG,
        name="states_other",
    )(*sources, *other, *mine, *after)
    return result[:6], result[6:12], *result[12:]


def within_kernel(scale, pairs, *refs):
    work_inside(scale, refs[:4], refs[-3:], pairs)


def within(scale, local, after, pairs=range(GROUP // 2), into=()):
    out = [pltpu.VMEM(local[0].shape, PARTIAL)] * 3
    return pl.pallas_call(
        functools.partial(within_kernel, scale, tuple(pairs)),
        out_shape=out,
        in_specs=[IN_VMEM] * (4 + len(into)) + [ANYWHERE] * len(after),
        out_specs=[IN_VMEM] * 3,
        input_output_aliases={4 + i: i for i in range(len(into))},
        compiler_params=pltpu.CompilerParams(vmem_limit_bytes=3 << 20),
        cost_estimate=LONG,
        name="within",
    )(*local, *into, *after)


def first_group(square, head, start, later):
    upper = my_row(square) == 0
    one, other = start[head], later[head]
    return jnp.where(upper, one, other), jnp.where(upper, other, one)


def second_group(head, rest):
    return rest[0, head], rest[1, head]


def settle(head, prefix, suffix, sums, sums_in, own, other):
    second = my_core() == 1
    own[0, head] = prefix + jnp.where(second, sums_in[0], 0.0)
    own[1, head] = suffix + jnp.where(second, 0.0, sums_in[1])
    other[0, head] = prefix + jnp.where(second, 0.0, sums[0])
    other[1, head] = suffix + jnp.where(second, sums[1], 0.0)


def comes_earlier(turn):
    pair = my_pair()
    return jnp.bitwise_xor(pair, turn) < pair


def sums_of_group(group, head, start, start_in, later, later_in, rest, rest_in):
    if group == 0:
        return first_group(False, head, start, later), first_group(False, head, start_in, later_in)
    return second_group(head, rest), second_group(head, rest_in)


def join_kernel(turns, group, *refs):
    for head in range(GROUP):
        sums, sums_in = sums_of_group(group, head, *refs[:6])
        for turn, out in zip(turns, refs[-len(turns) :], strict=True):
            out[head] = jnp.where(comes_earlier(turn), sums[1] + sums_in[1], sums[0] + sums_in[0])


def combine_kernel(turns, group, *refs):
    received = refs[6 : 6 + len(turns)]
    for head in range(GROUP):
        sums, sums_in = sums_of_group(group, head, *refs[:6])
        prefix = jnp.zeros((HEAD_DIM, HEAD_DIM), jnp.float32)
        suffix = jnp.zeros((HEAD_DIM, HEAD_DIM), jnp.float32)
        for turn, value in zip(turns, received, strict=True):
            earlier = comes_earlier(turn)
            prefix = prefix + jnp.where(earlier, value[head], 0.0)
            suffix = suffix + jnp.where(earlier, 0.0, value[head])
        settle(head, prefix, suffix, sums, sums_in, *refs[-2:])


def row_first_kernel(start, start_in, *refs):
    for head in range(GROUP):
        refs[-1][head] = start[head] + start_in[head]


def row_second_kernel(rest, rest_in, *refs):
    kind = lax.rem(my_pair(), 2)
    for head in range(GROUP):
        refs[-1][head] = rest[kind, head] + rest_in[kind, head]


def column_first_kernel(rest, rest_in, from_row, *refs):
    kind = my_row(True)
    for head in range(GROUP):
        refs[-1][head] = rest[kind, head] + rest_in[kind, head] + from_row[head]


def column_second_kernel(start, start_in, from_row, *refs):
    for head in range(GROUP):
        refs[-1][head] = start[head] + start_in[head] + from_row[head]


def row_third_kernel(later, later_in, from_column, *refs):
    pair = my_pair()
    outer = (pair == 0) | (pair == 3)
    for head in range(GROUP):
        refs[-1][head] = jnp.where(outer, from_column[head], later[head] + later_in[head])


def first_states_kernel(start, start_in, later, later_in, row_second, column_first, *refs):
    pair = my_pair()
    below, right = pair >= 2, lax.rem(pair, 2) == 1
    for head in range(GROUP):
        row, column = row_second[head], column_first[head]
        prefix = jnp.where(right, row, 0.0) + jnp.where(below, column, 0.0)
        suffix = jnp.where(right, 0.0, row) + jnp.where(below, 0.0, column)
        sums, sums_in = first_group(True, head, start, later), first_group(True, head, start_in, later_in)
        settle(head, prefix, suffix, sums, sums_in, *refs[-2:])


def second_states_kernel(rest, rest_in, row_first, row_third, column_second, *refs):
    pair = my_pair()
    below, outer = pair >= 2, (pair == 0) | (pair == 3)
    for head in range(GROUP):
        passed = row_third[head] + jnp.where(outer, column_second[head], 0.0)
        prefix = jnp.where(pair == 1, row_first[head], 0.0) + jnp.where(below, passed, 0.0)
        suffix = jnp.where(pair == 2, row_first[head], 0.0) + jnp.where(below, 0.0, passed)
        settle(head, prefix, suffix, second_group(head, rest), second_group(head, rest_in), *refs[-2:])


def finish_kernel(scale, square, group, halves, *refs):
    targets, staged, sems = refs[-7:-4], refs[-4:-1], refs[-1]
    heads = GROUP
    copies = []
    for number, mine in enumerate(halves):
        k, v, o, dq, dk, dv, state, early, late = refs[9 * number : 9 * number + 9]
        rows = k.shape[0]
        subs = rows // SUB
        base = first_column(square, mine, group)
        for head in range(heads):
            at = head_columns(head)
            to = head_columns(number * heads + head)
            for sub in range(subs):
                span = pl.ds(sub * SUB, SUB)
                before, later = state[0, head], state[1, head]
                if sub > 0:
                    before = before + early[head, sub - 1]
                if sub < subs - 1:
                    later = later + late[head, sub]
                before, later = before.astype(jnp.bfloat16), later.astype(jnp.bfloat16)
                pieces = (
                    dq[span, at] + scale * dot(o[span, at], before, NT),
                    dk[span, at] + scale * dot(v[span, at], later, NT),
                    dv[span, at] + scale * dot(k[span, at], later, NN),
                )
                for out, piece in zip(staged, pieces, strict=True):
                    out[span, to] = piece.astype(jnp.bfloat16)
            if head % 2 == 1 or head == heads - 1:
                first, width = (head - head % 2) * HEAD_DIM, (1 + head % 2) * HEAD_DIM
                for i in range(3):
                    copy = pltpu.make_async_copy(
                        staged[i].at[:, pl.ds(number * heads * HEAD_DIM + first, width)],
                        targets[i].at[:, pl.ds(pl.multiple_of(base + first, HEAD_DIM), width)],
                        sems.at[number, head // 2, i],
                    )
                    copy.start()
                    copies.append(copy)
    for copy in copies:
        copy.wait()


def finish(scale, square, group, parts, before):
    rows = parts[0][1][0].shape[0]
    out = [jax.ShapeDtypeStruct((rows, HEADS * HEAD_DIM), jnp.bfloat16)] * 3
    halves = tuple(part[0] for part in parts)
    operands = []
    for _, local, partials, state, inner in parts:
        operands += [*local[1:], *partials, state, *inner]
    width = len(parts) * GROUP * HEAD_DIM
    return pl.pallas_call(
        functools.partial(finish_kernel, scale, square, group, halves),
        out_shape=out,
        in_specs=[IN_VMEM] * len(operands) + [ANYWHERE] * len(before),
        out_specs=[ANYWHERE] * 3,
        scratch_shapes=[pltpu.VMEM((rows, width), jnp.bfloat16)] * 3
        + [pltpu.SemaphoreType.DMA((len(parts), (GROUP + 1) // 2, 3))],
        input_output_aliases={len(operands) + i: i for i in range(len(before))},
        compiler_params=pltpu.CompilerParams(vmem_limit_bytes=(2 + 3 * len(parts)) << 20),
        cost_estimate=LONG,
        name="finish",
    )(*operands, *before)


def on_device(queries, key_rows, value_rows, out_grad):
    count = lax.axis_size("seq")
    square = count == 8
    scale = (HEAD_DIM * queries.shape[0] * count) ** -0.5
    sources = [
        pltpu.with_memory_space_constraint(array, pltpu.HBM) for array in (queries, key_rows, value_rows, out_grad)
    ]

    def trade(value, distance):
        return lax.ppermute(value, "seq", [(i, i ^ distance) for i in range(count)])

    def run(kernel, out, operands, after):
        return call(kernel, out, operands, after, name=(kernel.func if hasattr(kernel, "func") else kernel).__name__)

    part_eo, start_o = states_first(square, False, sources, ())
    start_in = trade(start_o, 1)
    part_em, start = states_first(square, True, sources, (start_o,))
    after = (start,)
    if square:
        (sent,) = run(row_first_kernel, [PIECE], (start, start_in), ())
        row_first = trade(sent, 2)
        after = (sent,)

    part_lo, part_lm, rest_o, rest = states_second(square, sources, after)
    rest_in = trade(rest_o, 1)
    sums_e, sums_l = (start, start_in), (rest, rest_in)
    partials_lo = within(scale, part_lo[:4], (rest_o,))
    after = (partials_lo[0],)
    if square:
        (sent,) = run(row_second_kernel, [PIECE], sums_l, after)
        row_second = trade(sent, 2)
        partials_lm = within(scale, part_lm[:4], (sent,), range(GROUP // 4))
        (sent,) = run(column_first_kernel, [PIECE], (*sums_l, row_first), (partials_lm[0],))
        column_first = trade(sent, 4)
        after = (sent,)
    else:
        partials_lm = within(scale, part_lm[:4], after, range(GROUP // 4))

    part_eo, part_em, later_o, later = states_other(square, sources, part_eo, part_em, after)
    later_in = trade(later_o, 1)
    sums_b = (later, later_in)
    partials_lm = within(scale, part_lm[:4], (later_o,), range(GROUP // 4, GROUP // 2), partials_lm)
    partials_eo = within(scale, part_eo[:4], (partials_lm[0],))
    if square:
        (sent,) = run(column_second_kernel, [PIECE], (*sums_e, row_second), (partials_eo[0],))
        column_second = trade(sent, 4)
        (sent,) = run(row_third_kernel, [PIECE], (*sums_b, column_first), (sent,))
        row_third = trade(sent, 2)
        arrived = (row_second, column_first)
        own_e, other_e = run(first_states_kernel, STATES, (*sums_e, *sums_b, *arrived), (sent,))
    else:
        turns = range(1, count // 2)
        arrived = []
        sums = (*sums_e, *sums_b, *sums_l)
        for group in range(2):
            kernel = functools.partial(join_kernel, turns, group)
            sent = run(kernel, [PIECE] * len(turns), sums, (partials_eo[0],))
            arrived.append([trade(value, 2 * turn) for turn, value in zip(turns, sent, strict=True)])
        kernel = functools.partial(combine_kernel, turns, 0)
        own_e, other_e = run(kernel, STATES, (*sums, *arrived[0]), ())

    other_e = trade(other_e, 1)
    partials_em = within(scale, part_em[:4], (own_e,))
    parts = [(True, part_em[:4], partials_em, own_e, part_em[4:]), (False, part_eo[:4], partials_eo, other_e, part_eo[4:])]
    done = finish(scale, square, 0, parts, ())

    after = (pltpu.with_memory_space_constraint(done[0], pltpu.HBM),)
    if square:
        arrived = (row_first, row_third, column_second)
        own_l, other_l = run(second_states_kernel, STATES, (*sums_l, *arrived), after)
    else:
        kernel = functools.partial(combine_kernel, turns, 1)
        own_l, other_l = run(kernel, STATES, (*sums, *arrived[1]), after)
    other_l = trade(other_l, 1)
    done = finish(scale, square, 1, [(True, part_lm[:4], partials_lm, own_l, part_lm[4:])], done)
    return tuple(finish(scale, square, 1, [(False, part_lo[:4], partials_lo, other_l, part_lo[4:])], done))


def solution(mesh):
    placed = P(("lists", "seq"), None)
    return jax.shard_map(
        on_device,
        mesh=mesh,
        in_specs=(placed,) * 4,
        out_specs=(placed,) * 3,
        check_vma=False,
    )
```

time: 36.6 us -> 35.8 us (0.978)
  waiting for transfers between devices: 3.71 us -> 1.08 us
  Pallas kernels: 23.6 us -> 25.1 us
    pallas_call x3 -> x9, Pallas kernels: 8.02 us -> 17.4 us  [the longest x5 7.8 us: within(): pl.pallas_call(functools.partial(within_kernel, scale, tuple(pairs)), out...]
    pallas_call x11 -> x7, Pallas kernels: 8.14 us -> 0.53 us  [call(): pl.pallas_call(kernel, out_shape=out, in_specs=[IN_VMEM] * len(operands)...]
    ppermute x9 -> x10, waiting for transfers between devices: 3.71 us -> 1.08 us  [trade(): return lax.ppermute(value, 'seq', [(i, i ^ distance) for i in range(count)])]
    ppermute x9 -> x10, starting transfers between devices: 8.17 us -> 8.42 us  [trade(): return lax.ppermute(value, 'seq', [(i, i ^ distance) for i in range(count)])]
  transfers between devices with their start and end apart: 9 -> 10, of which waited for: 3 -> 1; matrix products, arithmetic and copies ran while one was open for 0% -> 0% of each run, Pallas kernels for 52% -> 59%
where the time goes in v4:
time: 35.8 us; the launch traced here: 35.6 us
  Pallas kernels  25.1 us (70%)
  starting transfers between devices  8.42 us (24%)
  waiting for transfers between devices  1.08 us (3%)
  between operations  0.99 us (3%)
    ppermute x10, starting transfers between devices, trade(): return lax.ppermute(value, 'seq', [(i, i ^ distance) for i in range(count)])  8.42 us
    pallas_call x5, Pallas kernels, within(): pl.pallas_call(functools.partial(within_kernel, scale, tuple(pairs)), out...  7.8 us
    pallas_call x3, Pallas kernels, finish(): pl.pallas_call(functools.partial(finish_kernel, scale, square, group, hal...  7.23 us
    pallas_call x2, Pallas kernels, states_first(): pl.pallas_call(functools.partial(states_first_kernel, square, mine), out_...  3.66 us
    pallas_call x1, Pallas kernels, states_second(): pl.pallas_call(functools.partial(states_second_kernel, square), out_shape...  3.39 us
    pallas_call x1, Pallas kernels, states_other(): pl.pallas_call(functools.partial(states_other_kernel, square), out_shape=...  2.52 us
    ppermute x10, waiting for transfers between devices, trade(): return lax.ppermute(value, 'seq', [(i, i ^ distance) for i in range(count)])  1.08 us
  transfers between devices with their start and end apart: 10, of which 1 were waited for; matrix products, arithmetic and copies ran while one was open for 0% of the time, Pallas kernels for 59%

profile of v4, /device:TPU:0, one launch (start us, length us, event | category | flops | bytes accessed | tf_op | source)
XLA Modules:
  0.0 35.6 jit_solution(15073617105901413521)
XLA Ops:
  0.6 1.8 %states_first.2 = (bf16[768,512]{1,0:T(8,128)(2,1)S(1)}, bf16[768,512]{1,0:T(8,128)(2,1)S(1)}, bf16[768,512]{1,0:T(8,128)(2,1)S(1)}, bf16[768,512]{1,0:T(8,128)(...) custom-call(bf16[768,2048]{1,0:T(8,128)(2,1)} %refs_0_.7, ...), custom_call_target="tpu_custom_call" | custom-call | flops 20000000000 | bytes 1000 | tf_op jit(solution)/shard_map/states_first/pallas_call | solution.py:188
  2.5 0.5 %collective-permute-start = (f32[4,128,128]{2,1,0:T(8,128)S(1)}, f32[4,128,128]{2,1,0:T(8,128)S(1)}, u32[]{:S(2)}, u32[]{:S(2)}) collective-permute-start(f32[4,128,128]{2,1,0:T(8,128)S(1)} %get-tuple-element.70.refs_4_), channel_id=1, source_target_pairs={{0,1},{1,0},{2,3},{3,2},{4,5},{5,4},{6,7},{7,6},{8,9},{9,8},{10,11... | collective-permute-start | bytes 786440 | tf_op jit(solution)/shard_map/ppermute | solution.py:450
  3.0 1.8 %states_first.3 = (bf16[768,512]{1,0:T(8,128)(2,1)S(1)}, bf16[768,512]{1,0:T(8,128)(2,1)S(1)}, bf16[768,512]{1,0:T(8,128)(2,1)S(1)}, bf16[768,512]{1,0:T(8,128)(...) custom-call(bf16[768,2048]{1,0:T(8,128)(2,1)} %refs_0_.7, ...), custom_call_target="tpu_custom_call" | custom-call | flops 20000000000 | bytes 1000 | tf_op jit(solution)/shard_map/states_first/pallas_call | solution.py:188
  4.8 0.0 collective-permute-done.start_in
  4.9 2.6 %collective-permute-start.2 = (f32[4,128,128]{2,1,0:T(8,128)S(1)}, f32[4,128,128]{2,1,0:T(8,128)S(1)}, u32[]{:S(2)}, u32[]{:S(2)}) collective-permute-start(f32[4,128,128]{2,1,0:T(8,128)S(1)} %row_first_kernel.1.refs_4_), channel_id=1, source_target_pairs={{0,2},{1,3},{2,0},{3,1},{4,6},{5,7},{6,4},{7,5},{8,10},{9,11},{10,... | collective-permute-start | bytes 786440 | tf_op jit(solution)/shard_map/ppermute | solution.py:450
  7.5 3.4 %states_second.1 = (bf16[768,512]{1,0:T(8,128)(2,1)S(1)}, bf16[768,512]{1,0:T(8,128)(2,1)S(1)}, bf16[768,512]{1,0:T(8,128)(2,1)S(1)}, bf16[768,512]{1,0:T(8,128)...) custom-call(bf16[768,2048]{1,0:T(8,128)(2,1)} %refs_0_.7, ...), custom_call_target="tpu_custom_call" | custom-call | flops 20000000000 | bytes 1000 | tf_op jit(solution)/shard_map/states_second/pallas_call | solution.py:215
  10.9 0.3 collective-permute-start.1
  11.1 1.9 %within.5 = (f32[768,512]{1,0:T(8,128)S(1)}, f32[768,512]{1,0:T(8,128)S(1)}, f32[768,512]{1,0:T(8,128)S(1)}) custom-call(bf16[768,512]{1,0:T(8,128)(2,1)S(1)} %get-tuple-element.75.refs_0_, bf16[768,512]{1,0:T(8,128)(2,1)S(1)} %get-tuple-element.72.refs_1_.refs_0_, bf16[768,512]{1,0:T(8,128)(2,1)S(1)} %get-tuple-element.73.refs_2_.refs_1_, ...), custom_call_target="tpu_custom_call" | custom-call | flops 20000000000 | bytes 1000 | tf_op jit(solution)/shard_map/within/pallas_call | solution.py:267
  13.0 0.0 collective-permute-done.1.rest_in
  13.1 0.3 collective-permute-start.5
  13.4 1.0 %within.6 = (f32[768,512]{1,0:T(8,128)S(1)}, f32[768,512]{1,0:T(8,128)S(1)}, f32[768,512]{1,0:T(8,128)S(1)}) custom-call(bf16[768,512]{1,0:T(8,128)(2,1)S(1)} %get-tuple-element.93.refs_0_, bf16[768,512]{1,0:T(8,128)(2,1)S(1)} %get-tuple-element.94.refs_1_.refs_0_, bf16[768,512]{1,0:T(8,128)(2,1)S(1)} %get-tuple-element.95.refs_2_.refs_1_, ...), custom_call_target="tpu_custom_call" | custom-call | flops 20000000000 | bytes 1000 | tf_op jit(solution)/shard_map/within/pallas_call | solution.py:267
  14.5 0.0 collective-permute-done.2.from_row.row_first
  14.5 0.1 column_first_kernel.1.refs_16_
  14.5 1.8 %collective-permute-start.4 = (f32[4,128,128]{2,1,0:T(8,128)S(1)}, f32[4,128,128]{2,1,0:T(8,128)S(1)}, u32[]{:S(2)}, u32[]{:S(2)}) collective-permute-start(f32[4,128,128]{2,1,0:T(8,128)S(1)} %column_first_kernel.1.refs_16_), channel_id=1, source_target_pairs={{0,4},{1,5},{2,6},{3,7},{4,0},{5,1},{6,2},{7,3},{8,12},{9,13},{10,... | collective-permute-start | bytes 786440 | tf_op jit(solution)/shard_map/ppermute | solution.py:450
  16.4 2.5 %states_other.1 = (bf16[768,512]{1,0:T(8,128)(2,1)S(1)}, bf16[768,512]{1,0:T(8,128)(2,1)S(1)}, bf16[768,512]{1,0:T(8,128)(2,1)S(1)}, bf16[768,512]{1,0:T(8,128)(...) custom-call(bf16[768,2048]{1,0:T(8,128)(2,1)} %refs_0_.7, ...), custom_call_target="tpu_custom_call", output_to_operand_aliasing={{0}: (4, {}), {1}: (5, {}), {2}: (6, {}), {3}: (7, {}), {4}... | custom-call | flops 20000000000 | bytes 1000 | tf_op jit(solution)/shard_map/states_other/pallas_call | solution.py:247
  18.9 0.1 collective-permute-start.3
  19.0 1.0 %within.7 = (f32[768,512]{1,0:T(8,128)S(1)}, f32[768,512]{1,0:T(8,128)S(1)}, f32[768,512]{1,0:T(8,128)S(1)}) custom-call(bf16[768,512]{1,0:T(8,128)(2,1)S(1)} %get-tuple-element.93.refs_0_, bf16[768,512]{1,0:T(8,128)(2,1)S(1)} %get-tuple-element.94.refs_1_.refs_0_, ...), custom_call_target="tpu_custom_call", output_to_operand_aliasing={{0}: (4, {}), {1}: (5, {}), {2}: (6, {})} | custom-call | flops 20000000000 | bytes 1000 | tf_op jit(solution)/shard_map/within/pallas_call | solution.py:267
  20.0 1.9 %within.8 = (f32[768,512]{1,0:T(8,128)S(1)}, f32[768,512]{1,0:T(8,128)S(1)}, f32[768,512]{1,0:T(8,128)S(1)}) custom-call(bf16[768,512]{1,0:T(8,128)(2,1)S(1)} %get-tuple-element.100.refs_0_, bf16[768,512]{1,0:T(8,128)(2,1)S(1)} %get-tuple-element.101.refs_1_.refs_9_, bf16[768,512]{1,0:T(8,128)(2,1)S(1)} %get-tuple-element.102.refs_2_.refs_10_, ...), custom_call_target="tpu_custom_call" | custom-call | flops 20000000000 | bytes 1000 | tf_op jit(solution)/shard_map/within/pallas_call | solution.py:267
  21.9 0.0 collective-permute-done.5.from_row.row_second
  22.0 1.3 %collective-permute-start.7 = (f32[4,128,128]{2,1,0:T(8,128)S(1)}, f32[4,128,128]{2,1,0:T(8,128)S(1)}, u32[]{:S(2)}, u32[]{:S(2)}) collective-permute-start(f32[4,128,128]{2,1,0:T(8,128)S(1)} %column_second_kernel.1.refs_0_), channel_id=1, source_target_pairs={{0,4},{1,5},{2,6},{3,7},{4,0},{5,1},{6,2},{7,3},{8,12},{9,13},{10,... | collective-permute-start | bytes 786440 | tf_op jit(solution)/shard_map/ppermute | solution.py:450
  23.3 0.0 collective-permute-done.4.from_column.column_first
  23.3 0.0 collective-permute-done.3.later_in
  23.3 1.4 %collective-permute-start.6 = (f32[4,128,128]{2,1,0:T(8,128)S(1)}, f32[4,128,128]{2,1,0:T(8,128)S(1)}, u32[]{:S(2)}, u32[]{:S(2)}) collective-permute-start(f32[4,128,128]{2,1,0:T(8,128)S(1)} %row_third_kernel.1.refs_0_), channel_id=1, source_target_pairs={{0,2},{1,3},{2,0},{3,1},{4,6},{5,7},{6,4},{7,5},{8,10},{9,11},{10,... | collective-permute-start | bytes 786440 | tf_op jit(solution)/shard_map/ppermute | solution.py:450
  24.7 0.2 first_states_kernel.1
  24.9 0.1 collective-permute-start.8
  25.0 1.9 %within.9 = (f32[768,512]{1,0:T(8,128)S(1)}, f32[768,512]{1,0:T(8,128)S(1)}, f32[768,512]{1,0:T(8,128)S(1)}) custom-call(bf16[768,512]{1,0:T(8,128)(2,1)S(1)} %get-tuple-element.111.refs_0_, bf16[768,512]{1,0:T(8,128)(2,1)S(1)} %get-tuple-element.108.refs_1_.refs_0_, bf16[768,512]{1,0:T(8,128)(2,1)S(1)} %get-tuple-element.109.refs_2_.refs_1_, ...), custom_call_target="tpu_custom_call" | custom-call | flops 20000000000 | bytes 1000 | tf_op jit(solution)/shard_map/within/pallas_call | solution.py:267
  26.9 0.0 collective-permute-done.8.refs_15_
  26.9 3.0 %finish.3 = (bf16[768,2048]{1,0:T(8,128)(2,1)}, bf16[768,2048]{1,0:T(8,128)(2,1)}, bf16[768,2048]{1,0:T(8,128)(2,1)}) custom-call(bf16[768,512]{1,0:T(8,128)(2,1)S(1)} %get-tuple-element.108.refs_1_.refs_0_, bf16[768,512]{1,0:T(8,128)(2,1)S(1)} %get-tuple-element.109.refs_2_.refs_1_, bf16[768,512]{1,0:T(8,128)(2,1)S(1)} %get-tuple-element.110.refs_3_.refs_2_, ...), custom_call_target="tpu_custom_call" | custom-call | flops 20000000000 | bytes 1000 | tf_op jit(solution)/shard_map/finish/pallas_call | solution.py:427
  29.9 1.1 %collective-permute-done.6.row_third = f32[4,128,128]{2,1,0:T(8,128)S(1)} collective-permute-done((f32[4,128,128]{2,1,0:T(8,128)S(1)}, f32[4,128,128]{2,1,0:T(8,128)S(1)}, u32[]{:S(2)}, u32[]{:S(2)}) %collective-permute-start.6) | collective-permute-done | bytes 262176 | tf_op jit(solution)/shard_map/ppermute | solution.py:450
  31.0 0.0 collective-permute-done.7.column_second
  31.0 0.2 second_states_kernel.1
  31.2 0.1 collective-permute-start.9
  31.2 2.1 %finish.4 = (bf16[768,2048]{1,0:T(8,128)(2,1)}, bf16[768,2048]{1,0:T(8,128)(2,1)}, bf16[768,2048]{1,0:T(8,128)(2,1)}) custom-call(bf16[768,512]{1,0:T(8,128)(2,1)S(1)} %get-tuple-element.94.refs_1_.refs_0_, bf16[768,512]{1,0:T(8,128)(2,1)S(1)} %get-tuple-element.95.refs_2_.refs_1_, ...), custom_call_target="tpu_custom_call", output_to_operand_aliasing={{0}: (9, {}), {1}: (10, {}), {2}: (11, {})} | custom-call | flops 20000000000 | bytes 1000 | tf_op jit(solution)/shard_map/finish/pallas_call | solution.py:427
  33.4 0.0 collective-permute-done.9.refs_6_
  33.4 2.1 %finish.5 = (bf16[768,2048]{1,0:T(8,128)(2,1)}, bf16[768,2048]{1,0:T(8,128)(2,1)}, bf16[768,2048]{1,0:T(8,128)(2,1)}) custom-call(bf16[768,512]{1,0:T(8,128)(2,1)S(1)} %get-tuple-element.72.refs_1_.refs_0_, bf16[768,512]{1,0:T(8,128)(2,1)S(1)} %get-tuple-element.73.refs_2_.refs_1_, ...), custom_call_target="tpu_custom_call", output_to_operand_aliasing={{0}: (9, {}), {1}: (10, {}), {2}: (11, {})} | custom-call | flops 20000000000 | bytes 1000 | tf_op jit(solution)/shard_map/finish/pallas_call | solution.py:427
  (4 shorter events, 0.2 us)
Async XLA Ops:
  2.5 2.4 %collective-permute-start = (f32[4,128,128]{2,1,0:T(8,128)S(1)}, f32[4,128,128]{2,1,0:T(8,128)S(1)}, u32[]{:S(2)}, u32[]{:S(2)}) collective-permute-start(f32[4,128,128]{2,1,0:T(8,128)S(1)} %get-tuple-element.70.refs_4_), channel_id=1, source_target_pairs={{0,1},{1,0},{2,3},{3,2},{4,5},{5,4},{6,7},{7,6},{8,9},{9,8},{10,11... | collective-permute-start | bytes 786440 | tf_op jit(solution)/shard_map/ppermute | solution.py:450
  4.9 9.6 %collective-permute-start.2 = (f32[4,128,128]{2,1,0:T(8,128)S(1)}, f32[4,128,128]{2,1,0:T(8,128)S(1)}, u32[]{:S(2)}, u32[]{:S(2)}) collective-permute-start(f32[4,128,128]{2,1,0:T(8,128)S(1)} %row_first_kernel.1.refs_4_), channel_id=1, source_target_pairs={{0,2},{1,3},{2,0},{3,1},{4,6},{5,7},{6,4},{7,5},{8,10},{9,11},{10,... | collective-permute-start | bytes 786440 | tf_op jit(solution)/shard_map/ppermute | solution.py:450
  10.9 2.2 %collective-permute-start.1 = (f32[2,4,128,128]{3,2,1,0:T(8,128)S(1)}, f32[2,4,128,128]{3,2,1,0:T(8,128)S(1)}, u32[]{:S(2)}, u32[]{:S(2)}) collective-permute-start(f32[2,4,128,128]{3,2,1,0:T(8,128)S(1)} %get-tuple-element.76.refs_4_), channel_id=1, source_target_pairs={{0,1},{1,0},{2,3},{3,2},{4,5},{5,4},{6,7},{7,6},{8,9},{9,8},{10,11... | collective-permute-start | bytes 1572872 | tf_op jit(solution)/shard_map/ppermute | solution.py:450
  13.1 8.9 %collective-permute-start.5 = (f32[4,128,128]{2,1,0:T(8,128)S(1)}, f32[4,128,128]{2,1,0:T(8,128)S(1)}, u32[]{:S(2)}, u32[]{:S(2)}) collective-permute-start(f32[4,128,128]{2,1,0:T(8,128)S(1)} %row_second_kernel.1.refs_4_), channel_id=1, source_target_pairs={{0,2},{1,3},{2,0},{3,1},{4,6},{5,7},{6,4},{7,5},{8,10},{9,11},{10,... | collective-permute-start | bytes 786440 | tf_op jit(solution)/shard_map/ppermute | solution.py:450
  14.5 8.7 %collective-permute-start.4 = (f32[4,128,128]{2,1,0:T(8,128)S(1)}, f32[4,128,128]{2,1,0:T(8,128)S(1)}, u32[]{:S(2)}, u32[]{:S(2)}) collective-permute-start(f32[4,128,128]{2,1,0:T(8,128)S(1)} %column_first_kernel.1.refs_16_), channel_id=1, source_target_pairs={{0,4},{1,5},{2,6},{3,7},{4,0},{5,1},{6,2},{7,3},{8,12},{9,13},{10,... | collective-permute-start | bytes 786440 | tf_op jit(solution)/shard_map/ppermute | solution.py:450
  18.9 4.4 %collective-permute-start.3 = (f32[4,128,128]{2,1,0:T(8,128)S(1)}, f32[4,128,128]{2,1,0:T(8,128)S(1)}, u32[]{:S(2)}, u32[]{:S(2)}) collective-permute-start(f32[4,128,128]{2,1,0:T(8,128)S(1)} %get-tuple-element.99.refs_7_), channel_id=1, source_target_pairs={{0,1},{1,0},{2,3},{3,2},{4,5},{5,4},{6,7},{7,6},{8,9},{9,8},{10,11... | collective-permute-start | bytes 786440 | tf_op jit(solution)/shard_map/ppermute | solution.py:450
  22.0 9.0 %collective-permute-start.7 = (f32[4,128,128]{2,1,0:T(8,128)S(1)}, f32[4,128,128]{2,1,0:T(8,128)S(1)}, u32[]{:S(2)}, u32[]{:S(2)}) collective-permute-start(f32[4,128,128]{2,1,0:T(8,128)S(1)} %column_second_kernel.1.refs_0_), channel_id=1, source_target_pairs={{0,4},{1,5},{2,6},{3,7},{4,0},{5,1},{6,2},{7,3},{8,12},{9,13},{10,... | collective-permute-start | bytes 786440 | tf_op jit(solution)/shard_map/ppermute | solution.py:450
  23.3 7.7 %collective-permute-start.6 = (f32[4,128,128]{2,1,0:T(8,128)S(1)}, f32[4,128,128]{2,1,0:T(8,128)S(1)}, u32[]{:S(2)}, u32[]{:S(2)}) collective-permute-start(f32[4,128,128]{2,1,0:T(8,128)S(1)} %row_third_kernel.1.refs_0_), channel_id=1, source_target_pairs={{0,2},{1,3},{2,0},{3,1},{4,6},{5,7},{6,4},{7,5},{8,10},{9,11},{10,... | collective-permute-start | bytes 786440 | tf_op jit(solution)/shard_map/ppermute | solution.py:450
  24.9 2.0 %collective-permute-start.8 = (f32[2,4,128,128]{3,2,1,0:T(8,128)S(1)}, f32[2,4,128,128]{3,2,1,0:T(8,128)S(1)}, u32[]{:S(2)}, u32[]{:S(2)}) collective-permute-start(f32[2,4,128,128]{3,2,1,0:T(8,128)S(1)} %get-tuple-element.120), channel_id=1, source_target_pairs={{0,1},{1,0},{2,3},{3,2},{4,5},{5,4},{6,7},{7,6},{8,9},{9,8},{10,11... | collective-permute-start | bytes 1572872 | tf_op jit(solution)/shard_map/ppermute | solution.py:450
  31.2 2.2 %collective-permute-start.9 = (f32[2,4,128,128]{3,2,1,0:T(8,128)S(1)}, f32[2,4,128,128]{3,2,1,0:T(8,128)S(1)}, u32[]{:S(2)}, u32[]{:S(2)}) collective-permute-start(f32[2,4,128,128]{3,2,1,0:T(8,128)S(1)} %get-tuple-element.124), channel_id=1, source_target_pairs={{0,1},{1,0},{2,3},{3,2},{4,5},{5,4},{6,7},{7,6},{8,9},{9,8},{10,11... | collective-permute-start | bytes 1572872 | tf_op jit(solution)/shard_map/ppermute | solution.py:450

commit v5 on v4

--- a/solution.py
+++ b/solution.py
@@ -354,7 +354,9 @@
         refs[-1][head] = jnp.where(outer, from_column[head], later[head] + later_in[head])
 
 
-def first_states_kernel(start, start_in, later, later_in, row_second, column_first, *refs):
+def first_states_kernel(start, start_in, later, later_in, rest, rest_in, row_first, row_second, column_first, *refs):
+    own, other, own_prefix = refs[-3:]
+    second = my_core() == 1
     pair = my_pair()
     below, right = pair >= 2, lax.rem(pair, 2) == 1
     for head in range(GROUP):
@@ -362,7 +364,10 @@
         prefix = jnp.where(right, row, 0.0) + jnp.where(below, column, 0.0)
         suffix = jnp.where(right, 0.0, row) + jnp.where(below, 0.0, column)
         sums, sums_in = first_group(True, head, start, later), first_group(True, head, start_in, later_in)
-        settle(head, prefix, suffix, sums, sums_in, *refs[-2:])
+        settle(head, prefix, suffix, sums, sums_in, own, other.at[pl.ds(0, 2)])
+        prefix = jnp.where(pair == 1, row_first[head], 0.0)
+        own_prefix[head] = prefix + jnp.where(second, rest_in[0, head], 0.0)
+        other[2, head] = prefix + jnp.where(second, 0.0, rest[0, head])
 
 
 def second_states_kernel(rest, rest_in, row_first, row_third, column_second, *refs):
@@ -375,64 +380,105 @@
         settle(head, prefix, suffix, second_group(head, rest), second_group(head, rest_in), *refs[-2:])
 
 
-def finish_kernel(scale, square, group, halves, *refs):
+def add_state(scale, head, partial, rows, states, inner, dims, out, to):
+    at = head_columns(head)
+    subs = rows.shape[0] // SUB
+    for sub in range(subs):
+        span = pl.ds(sub * SUB, SUB)
+        state = states[head]
+        if dims[1] == 0:
+            state = state + inner[head, sub - 1] if sub > 0 else state
+        else:
+            state = state + inner[head, sub] if sub < subs - 1 else state
+        piece = partial[span, at] + scale * dot(rows[span, at], state.astype(jnp.bfloat16), dims[0])
+        out[span, to] = piece.astype(jnp.bfloat16)
+
+
+QUERY, KEY, VALUE = (NT, 0), (NT, 1), (NN, 1)
+
+
+def finish_kernel(scale, square, group, halves, ahead, *refs):
     targets, staged, sems = refs[-7:-4], refs[-4:-1], refs[-1]
-    heads = GROUP
-    copies = []
-    for number, mine in enumerate(halves):
+    row = my_row(square)
+
+    def copies_of(i, number, which, first, heads):
+        mine, at_group = halves[number % len(halves)], 1 if number >= len(halves) else group
+        width = heads * HEAD_DIM
+        column = first_column(square, mine, at_group) + first * HEAD_DIM
+        return pltpu.make_async_copy(
+            staged[i].at[:, pl.ds((number * GROUP + first) * HEAD_DIM, width)],
+            targets[i].at[:, pl.ds(pl.multiple_of(column, HEAD_DIM), width)],
+            sems.at[number, which, i],
+        )
+
+    def run(i, number, copies, partial, rows, states, inner, dims):
+        for head in range(GROUP):
+            to = head_columns(number * GROUP + head)
+            add_state(scale, head, partial, rows, states, inner, dims, staged[i], to)
+            if head % 2 == 1:
+                copies[head // 2].start()
+
+    def pieces(i, number):
+        return [copies_of(i, number, which, 2 * which, 2) for which in range(GROUP // 2)]
+
+    sometimes, always = [], []
+    for number in range(len(halves)):
         k, v, o, dq, dk, dv, state, early, late = refs[9 * number : 9 * number + 9]
-        rows = k.shape[0]
-        subs = rows // SUB
-        base = first_column(square, mine, group)
-        for head in range(heads):
-            at = head_columns(head)
-            to = head_columns(number * heads + head)
-            for sub in range(subs):
-                span = pl.ds(sub * SUB, SUB)
-                before, later = state[0, head], state[1, head]
-                if sub > 0:
-                    before = before + early[head, sub - 1]
-                if sub < subs - 1:
-                    later = later + late[head, sub]
-                before, later = before.astype(jnp.bfloat16), later.astype(jnp.bfloat16)
-                pieces = (
-                    dq[span, at] + scale * dot(o[span, at], before, NT),
-                    dk[span, at] + scale * dot(v[span, at], later, NT),
-                    dv[span, at] + scale * dot(k[span, at], later, NN),
-                )
-                for out, piece in zip(staged, pieces, strict=True):
-                    out[span, to] = piece.astype(jnp.bfloat16)
-            if head % 2 == 1 or head == heads - 1:
-                first, width = (head - head % 2) * HEAD_DIM, (1 + head % 2) * HEAD_DIM
-                for i in range(3):
-                    copy = pltpu.make_async_copy(
-                        staged[i].at[:, pl.ds(number * heads * HEAD_DIM + first, width)],
-                        targets[i].at[:, pl.ds(pl.multiple_of(base + first, HEAD_DIM), width)],
-                        sems.at[number, head // 2, i],
-                    )
-                    copy.start()
-                    copies.append(copy)
-    for copy in copies:
+        query = pieces(0, number)
+        if square and group == 1:
+            sometimes += query
+
+            @pl.when(row == 1)
+            def _():
+                run(0, number, query, dq, o, state.at[0], early, QUERY)
+        else:
+            always += query
+            run(0, number, query, dq, o, state.at[0], early, QUERY)
+        for i, arguments in ((1, (dk, v, state.at[1], late, KEY)), (2, (dv, k, state.at[1], late, VALUE))):
+            copies = pieces(i, number)
+            always += copies
+            run(i, number, copies, *arguments)
+    rest = refs[9 * len(halves) :]
+    for n in range(ahead):
+        number = len(halves) + n
+        o, dq, prefix, early = rest[4 * n : 4 * n + 4]
+        prefix = prefix if n == 0 else prefix.at[2]
+        query = pieces(0, number)
+        sometimes += query
+
+        @pl.when(row == 0)
+        def _():
+            run(0, number, query, dq, o, prefix, early, QUERY)
+
+    for copy in always:
         copy.wait()
-
-
-def finish(scale, square, group, parts, before):
+    if sometimes:
+
+        @pl.when(row == (0 if ahead else 1))
+        def _():
+            for copy in sometimes:
+                copy.wait()
+
+
+def finish(scale, square, group, parts, before, ahead=()):
     rows = parts[0][1][0].shape[0]
     out = [jax.ShapeDtypeStruct((rows, HEADS * HEAD_DIM), jnp.bfloat16)] * 3
     halves = tuple(part[0] for part in parts)
     operands = []
     for _, local, partials, state, inner in parts:
         operands += [*local[1:], *partials, state, *inner]
-    width = len(parts) * GROUP * HEAD_DIM
+    for arrays in ahead:
+        operands += arrays
+    widths = [(len(parts) + extra) * GROUP * HEAD_DIM for extra in (len(ahead), 0, 0)]
     return pl.pallas_call(
-        functools.partial(finish_kernel, scale, square, group, halves),
+        functools.partial(finish_kernel, scale, square, group, halves, len(ahead)),
         out_shape=out,
         in_specs=[IN_VMEM] * len(operands) + [ANYWHERE] * len(before),
         out_specs=[ANYWHERE] * 3,
-        scratch_shapes=[pltpu.VMEM((rows, width), jnp.bfloat16)] * 3
-        + [pltpu.SemaphoreType.DMA((len(parts), (GROUP + 1) // 2, 3))],
+        scratch_shapes=[pltpu.VMEM((rows, width), jnp.bfloat16) for width in widths]
+        + [pltpu.SemaphoreType.DMA((len(parts) + len(ahead), GROUP // 2, 3))],
         input_output_aliases={len(operands) + i: i for i in range(len(before))},
-        compiler_params=pltpu.CompilerParams(vmem_limit_bytes=(2 + 3 * len(parts)) << 20),
+        compiler_params=pltpu.CompilerParams(vmem_limit_bytes=(2 + 3 * len(parts) + len(ahead)) << 20),
         cost_estimate=LONG,
         name="finish",
     )(*operands, *before)
@@ -486,8 +532,9 @@
         column_second = trade(sent, 4)
         (sent,) = run(row_third_kernel, [PIECE], (*sums_b, column_first), (sent,))
         row_third = trade(sent, 2)
-        arrived = (row_second, column_first)
-        own_e, other_e = run(first_states_kernel, STATES, (*sums_e, *sums_b, *arrived), (sent,))
+        arrived = (row_first, row_second, column_first)
+        out = [state_of(GROUP), pltpu.VMEM((3, GROUP, HEAD_DIM, HEAD_DIM), jnp.float32), PIECE]
+        own_e, other_e, own_prefix = run(first_states_kernel, out, (*sums_e, *sums_b, *sums_l, *arrived), (sent,))
     else:
         turns = range(1, count // 2)
         arrived = []
@@ -502,7 +549,13 @@
     other_e = trade(other_e, 1)
     partials_em = within(scale, part_em[:4], (own_e,))
     parts = [(True, part_em[:4], partials_em, own_e, part_em[4:]), (False, part_eo[:4], partials_eo, other_e, part_eo[4:])]
-    done = finish(scale, square, 0, parts, ())
+    ahead = ()
+    if square:
+        ahead = (
+            (part_lm[3], partials_lm[0], own_prefix, part_lm[4]),
+            (part_lo[3], partials_lo[0], other_e, part_lo[4]),
+        )
+    done = finish(scale, square, 0, parts, (), ahead)
 
     after = (pltpu.with_memory_space_constraint(done[0], pltpu.HBM),)
     if square:

time: 35.8 us -> 35.1 us (0.980)
  waiting for transfers between devices: 1.08 us -> 0.54 us
    ppermute x10, waiting for transfers between devices: 1.08 us -> 0.54 us  [trade(): return lax.ppermute(value, 'seq', [(i, i ^ distance) for i in range(count)])]
  transfers between devices with their start and end apart: 10 -> 10, of which waited for: 1 -> 2; matrix products, arithmetic and copies ran while one was open for 0% -> 0% of each run, Pallas kernels for 59% -> 61%
where the time goes in v5:
time: 35.1 us; the launch traced here: 34.9 us
  Pallas kernels  24.9 us (71%)
  starting transfers between devices  8.56 us (24%)
  between operations  0.97 us (3%)
  waiting for transfers between devices  0.54 us (2%)
    ppermute x10, starting transfers between devices, trade(): return lax.ppermute(value, 'seq', [(i, i ^ distance) for i in range(count)])  8.56 us
    pallas_call x5, Pallas kernels, within(): pl.pallas_call(functools.partial(within_kernel, scale, tuple(pairs)), out...  7.8 us
    pallas_call x3, Pallas kernels, finish(): pl.pallas_call(functools.partial(finish_kernel, scale, square, group, hal...  6.9 us
    pallas_call x2, Pallas kernels, states_first(): pl.pallas_call(functools.partial(states_first_kernel, square, mine), out_...  3.66 us
    pallas_call x1, Pallas kernels, states_second(): pl.pallas_call(functools.partial(states_second_kernel, square), out_shape...  3.39 us
    pallas_call x1, Pallas kernels, states_other(): pl.pallas_call(functools.partial(states_other_kernel, square), out_shape=...  2.52 us
  transfers between devices with their start and end apart: 10, of which 2 were waited for; matrix products, arithmetic and copies ran while one was open for 0% of the time, Pallas kernels for 61%

profile of v5, /device:TPU:0, one launch (start us, length us, event | category | flops | bytes accessed | tf_op | source)
XLA Modules:
  0.0 34.9 jit_solution(7939396969794997697)
XLA Ops:
  0.6 1.8 %states_first.2 = (bf16[768,512]{1,0:T(8,128)(2,1)S(1)}, bf16[768,512]{1,0:T(8,128)(2,1)S(1)}, bf16[768,512]{1,0:T(8,128)(2,1)S(1)}, bf16[768,512]{1,0:T(8,128)(...) custom-call(bf16[768,2048]{1,0:T(8,128)(2,1)} %refs_0_.7, ...), custom_call_target="tpu_custom_call" | custom-call | flops 20000000000 | bytes 1000 | tf_op jit(solution)/shard_map/states_first/pallas_call | solution.py:188
  2.5 0.5 %collective-permute-start = (f32[4,128,128]{2,1,0:T(8,128)S(1)}, f32[4,128,128]{2,1,0:T(8,128)S(1)}, u32[]{:S(2)}, u32[]{:S(2)}) collective-permute-start(f32[4,128,128]{2,1,0:T(8,128)S(1)} %get-tuple-element.71.refs_4_), channel_id=1, source_target_pairs={{0,1},{1,0},{2,3},{3,2},{4,5},{5,4},{6,7},{7,6},{8,9},{9,8},{10,11... | collective-permute-start | bytes 786440 | tf_op jit(solution)/shard_map/ppermute | solution.py:496
  3.0 1.8 %states_first.3 = (bf16[768,512]{1,0:T(8,128)(2,1)S(1)}, bf16[768,512]{1,0:T(8,128)(2,1)S(1)}, bf16[768,512]{1,0:T(8,128)(2,1)S(1)}, bf16[768,512]{1,0:T(8,128)(...) custom-call(bf16[768,2048]{1,0:T(8,128)(2,1)} %refs_0_.7, ...), custom_call_target="tpu_custom_call" | custom-call | flops 20000000000 | bytes 1000 | tf_op jit(solution)/shard_map/states_first/pallas_call | solution.py:188
  4.8 0.0 collective-permute-done.start_in
  4.9 2.6 %collective-permute-start.2 = (f32[4,128,128]{2,1,0:T(8,128)S(1)}, f32[4,128,128]{2,1,0:T(8,128)S(1)}, u32[]{:S(2)}, u32[]{:S(2)}) collective-permute-start(f32[4,128,128]{2,1,0:T(8,128)S(1)} %row_first_kernel.1.refs_4_), channel_id=1, source_target_pairs={{0,2},{1,3},{2,0},{3,1},{4,6},{5,7},{6,4},{7,5},{8,10},{9,11},{10,... | collective-permute-start | bytes 786440 | tf_op jit(solution)/shard_map/ppermute | solution.py:496
  7.5 3.4 %states_second.1 = (bf16[768,512]{1,0:T(8,128)(2,1)S(1)}, bf16[768,512]{1,0:T(8,128)(2,1)S(1)}, bf16[768,512]{1,0:T(8,128)(2,1)S(1)}, bf16[768,512]{1,0:T(8,128)...) custom-call(bf16[768,2048]{1,0:T(8,128)(2,1)} %refs_0_.7, ...), custom_call_target="tpu_custom_call" | custom-call | flops 20000000000 | bytes 1000 | tf_op jit(solution)/shard_map/states_second/pallas_call | solution.py:215
  10.9 0.3 collective-permute-start.1
  11.1 1.9 %within.5 = (f32[768,512]{1,0:T(8,128)S(1)}, f32[768,512]{1,0:T(8,128)S(1)}, f32[768,512]{1,0:T(8,128)S(1)}) custom-call(bf16[768,512]{1,0:T(8,128)(2,1)S(1)} %get-tuple-element.76.refs_0_, bf16[768,512]{1,0:T(8,128)(2,1)S(1)} %get-tuple-element.73.refs_1_.refs_0_, bf16[768,512]{1,0:T(8,128)(2,1)S(1)} %get-tuple-element.74.refs_2_.refs_1_, ...), custom_call_target="tpu_custom_call" | custom-call | flops 20000000000 | bytes 1000 | tf_op jit(solution)/shard_map/within/pallas_call | solution.py:267
  13.0 0.0 collective-permute-done.1.rest_in
  13.1 0.3 collective-permute-start.5
  13.4 1.0 %within.6 = (f32[768,512]{1,0:T(8,128)S(1)}, f32[768,512]{1,0:T(8,128)S(1)}, f32[768,512]{1,0:T(8,128)S(1)}) custom-call(bf16[768,512]{1,0:T(8,128)(2,1)S(1)} %get-tuple-element.94.refs_0_, bf16[768,512]{1,0:T(8,128)(2,1)S(1)} %get-tuple-element.95.refs_1_.refs_0_, bf16[768,512]{1,0:T(8,128)(2,1)S(1)} %get-tuple-element.96.refs_2_.refs_1_, ...), custom_call_target="tpu_custom_call" | custom-call | flops 20000000000 | bytes 1000 | tf_op jit(solution)/shard_map/within/pallas_call | solution.py:267
  14.5 0.0 collective-permute-done.2.from_row.row_first
  14.5 0.1 column_first_kernel.1.refs_16_
  14.5 1.8 %collective-permute-start.4 = (f32[4,128,128]{2,1,0:T(8,128)S(1)}, f32[4,128,128]{2,1,0:T(8,128)S(1)}, u32[]{:S(2)}, u32[]{:S(2)}) collective-permute-start(f32[4,128,128]{2,1,0:T(8,128)S(1)} %column_first_kernel.1.refs_16_), channel_id=1, source_target_pairs={{0,4},{1,5},{2,6},{3,7},{4,0},{5,1},{6,2},{7,3},{8,12},{9,13},{10,... | collective-permute-start | bytes 786440 | tf_op jit(solution)/shard_map/ppermute | solution.py:496
  16.4 2.5 %states_other.1 = (bf16[768,512]{1,0:T(8,128)(2,1)S(1)}, bf16[768,512]{1,0:T(8,128)(2,1)S(1)}, bf16[768,512]{1,0:T(8,128)(2,1)S(1)}, bf16[768,512]{1,0:T(8,128)(...) custom-call(bf16[768,2048]{1,0:T(8,128)(2,1)} %refs_0_.7, ...), custom_call_target="tpu_custom_call", output_to_operand_aliasing={{0}: (4, {}), {1}: (5, {}), {2}: (6, {}), {3}: (7, {}), {4}... | custom-call | flops 20000000000 | bytes 1000 | tf_op jit(solution)/shard_map/states_other/pallas_call | solution.py:247
  18.9 0.1 collective-permute-start.3
  19.0 1.0 %within.7 = (f32[768,512]{1,0:T(8,128)S(1)}, f32[768,512]{1,0:T(8,128)S(1)}, f32[768,512]{1,0:T(8,128)S(1)}) custom-call(bf16[768,512]{1,0:T(8,128)(2,1)S(1)} %get-tuple-element.94.refs_0_, bf16[768,512]{1,0:T(8,128)(2,1)S(1)} %get-tuple-element.95.refs_1_.refs_0_, ...), custom_call_target="tpu_custom_call", output_to_operand_aliasing={{0}: (4, {}), {1}: (5, {}), {2}: (6, {})} | custom-call | flops 20000000000 | bytes 1000 | tf_op jit(solution)/shard_map/within/pallas_call | solution.py:267
  20.0 1.9 %within.8 = (f32[768,512]{1,0:T(8,128)S(1)}, f32[768,512]{1,0:T(8,128)S(1)}, f32[768,512]{1,0:T(8,128)S(1)}) custom-call(bf16[768,512]{1,0:T(8,128)(2,1)S(1)} %get-tuple-element.101.refs_0_, bf16[768,512]{1,0:T(8,128)(2,1)S(1)} %get-tuple-element.102.refs_1_.refs_9_, bf16[768,512]{1,0:T(8,128)(2,1)S(1)} %get-tuple-element.103.refs_2_.refs_10_, ...), custom_call_target="tpu_custom_call" | custom-call | flops 20000000000 | bytes 1000 | tf_op jit(solution)/shard_map/within/pallas_call | solution.py:267
  21.9 0.0 collective-permute-done.5.from_row.row_second
  22.0 1.3 %collective-permute-start.7 = (f32[4,128,128]{2,1,0:T(8,128)S(1)}, f32[4,128,128]{2,1,0:T(8,128)S(1)}, u32[]{:S(2)}, u32[]{:S(2)}) collective-permute-start(f32[4,128,128]{2,1,0:T(8,128)S(1)} %column_second_kernel.1.refs_0_), channel_id=1, source_target_pairs={{0,4},{1,5},{2,6},{3,7},{4,0},{5,1},{6,2},{7,3},{8,12},{9,13},{10,... | collective-permute-start | bytes 786440 | tf_op jit(solution)/shard_map/ppermute | solution.py:496
  23.3 0.0 collective-permute-done.4.from_column.column_first
  23.3 0.0 collective-permute-done.3.later_in
  23.3 1.4 %collective-permute-start.6 = (f32[4,128,128]{2,1,0:T(8,128)S(1)}, f32[4,128,128]{2,1,0:T(8,128)S(1)}, u32[]{:S(2)}, u32[]{:S(2)}) collective-permute-start(f32[4,128,128]{2,1,0:T(8,128)S(1)} %row_third_kernel.1.refs_0_), channel_id=1, source_target_pairs={{0,2},{1,3},{2,0},{3,1},{4,6},{5,7},{6,4},{7,5},{8,10},{9,11},{10,... | collective-permute-start | bytes 786440 | tf_op jit(solution)/shard_map/ppermute | solution.py:496
  24.7 0.2 first_states_kernel.1
  25.0 0.1 collective-permute-start.8
  25.0 1.9 %within.9 = (f32[768,512]{1,0:T(8,128)S(1)}, f32[768,512]{1,0:T(8,128)S(1)}, f32[768,512]{1,0:T(8,128)S(1)}) custom-call(bf16[768,512]{1,0:T(8,128)(2,1)S(1)} %get-tuple-element.112.refs_0_, bf16[768,512]{1,0:T(8,128)(2,1)S(1)} %get-tuple-element.109.refs_1_.refs_0_, bf16[768,512]{1,0:T(8,128)(2,1)S(1)} %get-tuple-element.110.refs_2_.refs_1_, ...), custom_call_target="tpu_custom_call" | custom-call | flops 20000000000 | bytes 1000 | tf_op jit(solution)/shard_map/within/pallas_call | solution.py:267
  26.9 0.4 %collective-permute-done.8.refs_15_.refs_24_ = f32[3,4,128,128]{3,2,1,0:T(8,128)S(1)} collective-permute-done((f32[3,4,128,128]{3,2,1,0:T(8,128)S(1)}, f32[3,4,128,128]{3,2,1,0:T(8,128)S(1)}, u32[]{:S(2)}, u32[]{:S(2)}) %collective-permute-start.8) | collective-permute-done | bytes 786464 | tf_op jit(solution)/shard_map/ppermute | solution.py:496
  27.3 3.6 %finish.3 = (bf16[768,2048]{1,0:T(8,128)(2,1)}, bf16[768,2048]{1,0:T(8,128)(2,1)}, bf16[768,2048]{1,0:T(8,128)(2,1)}) custom-call(bf16[768,512]{1,0:T(8,128)(2,1)S(1)} %get-tuple-element.109.refs_1_.refs_0_, bf16[768,512]{1,0:T(8,128)(2,1)S(1)} %get-tuple-element.110.refs_2_.refs_1_, bf16[768,512]{1,0:T(8,128)(2,1)S(1)} %get-tuple-element.111.refs_3_.refs_2_, ...), custom_call_target="tpu_custom_call" | custom-call | flops 20000000000 | bytes 1000 | tf_op jit(solution)/shard_map/finish/pallas_call | solution.py:473
  31.0 0.0 collective-permute-done.6.row_third
  31.0 0.0 collective-permute-done.7.column_second
  31.0 0.2 second_states_kernel.1
  31.2 0.2 collective-permute-start.9
  31.4 1.6 %finish.4 = (bf16[768,2048]{1,0:T(8,128)(2,1)}, bf16[768,2048]{1,0:T(8,128)(2,1)}, bf16[768,2048]{1,0:T(8,128)(2,1)}) custom-call(bf16[768,512]{1,0:T(8,128)(2,1)S(1)} %get-tuple-element.95.refs_1_.refs_0_, bf16[768,512]{1,0:T(8,128)(2,1)S(1)} %get-tuple-element.96.refs_2_.refs_1_, ...), custom_call_target="tpu_custom_call", output_to_operand_aliasing={{0}: (9, {}), {1}: (10, {}), {2}: (11, {})} | custom-call | flops 20000000000 | bytes 1000 | tf_op jit(solution)/shard_map/finish/pallas_call | solution.py:473
  33.0 0.1 collective-permute-done.9.refs_6_
  33.1 1.6 %finish.5 = (bf16[768,2048]{1,0:T(8,128)(2,1)}, bf16[768,2048]{1,0:T(8,128)(2,1)}, bf16[768,2048]{1,0:T(8,128)(2,1)}) custom-call(bf16[768,512]{1,0:T(8,128)(2,1)S(1)} %get-tuple-element.73.refs_1_.refs_0_, bf16[768,512]{1,0:T(8,128)(2,1)S(1)} %get-tuple-element.74.refs_2_.refs_1_, ...), custom_call_target="tpu_custom_call", output_to_operand_aliasing={{0}: (9, {}), {1}: (10, {}), {2}: (11, {})} | custom-call | flops 20000000000 | bytes 1000 | tf_op jit(solution)/shard_map/finish/pallas_call | solution.py:473
  (4 shorter events, 0.2 us)
Async XLA Ops:
  2.5 2.4 %collective-permute-start = (f32[4,128,128]{2,1,0:T(8,128)S(1)}, f32[4,128,128]{2,1,0:T(8,128)S(1)}, u32[]{:S(2)}, u32[]{:S(2)}) collective-permute-start(f32[4,128,128]{2,1,0:T(8,128)S(1)} %get-tuple-element.71.refs_4_), channel_id=1, source_target_pairs={{0,1},{1,0},{2,3},{3,2},{4,5},{5,4},{6,7},{7,6},{8,9},{9,8},{10,11... | collective-permute-start | bytes 786440 | tf_op jit(solution)/shard_map/ppermute | solution.py:496
  4.9 9.6 %collective-permute-start.2 = (f32[4,128,128]{2,1,0:T(8,128)S(1)}, f32[4,128,128]{2,1,0:T(8,128)S(1)}, u32[]{:S(2)}, u32[]{:S(2)}) collective-permute-start(f32[4,128,128]{2,1,0:T(8,128)S(1)} %row_first_kernel.1.refs_4_), channel_id=1, source_target_pairs={{0,2},{1,3},{2,0},{3,1},{4,6},{5,7},{6,4},{7,5},{8,10},{9,11},{10,... | collective-permute-start | bytes 786440 | tf_op jit(solution)/shard_map/ppermute | solution.py:496
  10.9 2.2 %collective-permute-start.1 = (f32[2,4,128,128]{3,2,1,0:T(8,128)S(1)}, f32[2,4,128,128]{3,2,1,0:T(8,128)S(1)}, u32[]{:S(2)}, u32[]{:S(2)}) collective-permute-start(f32[2,4,128,128]{3,2,1,0:T(8,128)S(1)} %get-tuple-element.77.refs_4_), channel_id=1, source_target_pairs={{0,1},{1,0},{2,3},{3,2},{4,5},{5,4},{6,7},{7,6},{8,9},{9,8},{10,11... | collective-permute-start | bytes 1572872 | tf_op jit(solution)/shard_map/ppermute | solution.py:496
  13.1 8.9 %collective-permute-start.5 = (f32[4,128,128]{2,1,0:T(8,128)S(1)}, f32[4,128,128]{2,1,0:T(8,128)S(1)}, u32[]{:S(2)}, u32[]{:S(2)}) collective-permute-start(f32[4,128,128]{2,1,0:T(8,128)S(1)} %row_second_kernel.1.refs_4_), channel_id=1, source_target_pairs={{0,2},{1,3},{2,0},{3,1},{4,6},{5,7},{6,4},{7,5},{8,10},{9,11},{10,... | collective-permute-start | bytes 786440 | tf_op jit(solution)/shard_map/ppermute | solution.py:496
  14.5 8.7 %collective-permute-start.4 = (f32[4,128,128]{2,1,0:T(8,128)S(1)}, f32[4,128,128]{2,1,0:T(8,128)S(1)}, u32[]{:S(2)}, u32[]{:S(2)}) collective-permute-start(f32[4,128,128]{2,1,0:T(8,128)S(1)} %column_first_kernel.1.refs_16_), channel_id=1, source_target_pairs={{0,4},{1,5},{2,6},{3,7},{4,0},{5,1},{6,2},{7,3},{8,12},{9,13},{10,... | collective-permute-start | bytes 786440 | tf_op jit(solution)/shard_map/ppermute | solution.py:496
  18.9 4.4 %collective-permute-start.3 = (f32[4,128,128]{2,1,0:T(8,128)S(1)}, f32[4,128,128]{2,1,0:T(8,128)S(1)}, u32[]{:S(2)}, u32[]{:S(2)}) collective-permute-start(f32[4,128,128]{2,1,0:T(8,128)S(1)} %get-tuple-element.100.refs_7_), channel_id=1, source_target_pairs={{0,1},{1,0},{2,3},{3,2},{4,5},{5,4},{6,7},{7,6},{8,9},{9,8},{10,11... | collective-permute-start | bytes 786440 | tf_op jit(solution)/shard_map/ppermute | solution.py:496
  22.0 9.0 %collective-permute-start.7 = (f32[4,128,128]{2,1,0:T(8,128)S(1)}, f32[4,128,128]{2,1,0:T(8,128)S(1)}, u32[]{:S(2)}, u32[]{:S(2)}) collective-permute-start(f32[4,128,128]{2,1,0:T(8,128)S(1)} %column_second_kernel.1.refs_0_), channel_id=1, source_target_pairs={{0,4},{1,5},{2,6},{3,7},{4,0},{5,1},{6,2},{7,3},{8,12},{9,13},{10,... | collective-permute-start | bytes 786440 | tf_op jit(solution)/shard_map/ppermute | solution.py:496
  23.3 7.7 %collective-permute-start.6 = (f32[4,128,128]{2,1,0:T(8,128)S(1)}, f32[4,128,128]{2,1,0:T(8,128)S(1)}, u32[]{:S(2)}, u32[]{:S(2)}) collective-permute-start(f32[4,128,128]{2,1,0:T(8,128)S(1)} %row_third_kernel.1.refs_0_), channel_id=1, source_target_pairs={{0,2},{1,3},{2,0},{3,1},{4,6},{5,7},{6,4},{7,5},{8,10},{9,11},{10,... | collective-permute-start | bytes 786440 | tf_op jit(solution)/shard_map/ppermute | solution.py:496
  25.0 2.4 %collective-permute-start.8 = (f32[3,4,128,128]{3,2,1,0:T(8,128)S(1)}, f32[3,4,128,128]{3,2,1,0:T(8,128)S(1)}, u32[]{:S(2)}, u32[]{:S(2)}) collective-permute-start(f32[3,4,128,128]{3,2,1,0:T(8,128)S(1)} %get-tuple-element.121), channel_id=1, source_target_pairs={{0,1},{1,0},{2,3},{3,2},{4,5},{5,4},{6,7},{7,6},{8,9},{9,8},{10,11... | collective-permute-start | bytes 2359304 | tf_op jit(solution)/shard_map/ppermute | solution.py:496
  31.2 2.0 %collective-permute-start.9 = (f32[2,4,128,128]{3,2,1,0:T(8,128)S(1)}, f32[2,4,128,128]{3,2,1,0:T(8,128)S(1)}, u32[]{:S(2)}, u32[]{:S(2)}) collective-permute-start(f32[2,4,128,128]{3,2,1,0:T(8,128)S(1)} %get-tuple-element.128), channel_id=1, source_target_pairs={{0,1},{1,0},{2,3},{3,2},{4,5},{5,4},{6,7},{7,6},{8,9},{9,8},{10,11... | collective-permute-start | bytes 1572872 | tf_op jit(solution)/shard_map/ppermute | solution.py:496

commit v6 on v5

--- a/solution.py
+++ b/solution.py
@@ -171,31 +171,54 @@
     return [pltpu.VMEM((rows, GROUP * HEAD_DIM), jnp.bfloat16)] * 4 + [inner] * 2
 
 
-def states_first_kernel(square, mine, *refs):
-    sources, part, sums, sems = refs[:4], refs[-8:-2], refs[-2], refs[-1]
+def states_first_kernel(square, *refs):
+    sources, part, local, sums, sems = refs[:4], refs[4:10], refs[10:14], refs[14], refs[15]
     row = my_row(square)
     for kind in range(2):
-        copies = read(square, mine, 0, kind, sources, part[:4], sems)
+        copies = read(square, False, 0, kind, sources, part[:4], sems.at[0])
+        behind = read(square, True, 0, kind, sources, local, sems.at[1])
 
         @pl.when(row == kind)
         def _():
             start_all(copies)
+            start_all(behind)
             sum_kind(kind, copies, part[:4], sums, *part[4:])
-
-
-def states_first(square, mine, sources, after):
-    out = part_shapes(sources[0].shape[0]) + [PIECE]
-    *part, sums = pl.pallas_call(
-        functools.partial(states_first_kernel, square, mine),
+            for copy in behind:
+                copy.wait()
+
+
+def states_first(square, sources):
+    part = part_shapes(sources[0].shape[0])
+    out = part + part[:4] + [PIECE]
+    result = pl.pallas_call(
+        functools.partial(states_first_kernel, square),
         out_shape=out,
-        in_specs=[ANYWHERE] * (4 + len(after)),
+        in_specs=[ANYWHERE] * 4,
         out_specs=[IN_VMEM] * len(out),
-        scratch_shapes=[pltpu.SemaphoreType.DMA((4,))],
+        scratch_shapes=[pltpu.SemaphoreType.DMA((2, 4))],
         compiler_params=pltpu.CompilerParams(vmem_limit_bytes=2 << 20),
         cost_estimate=LONG,
         name="states_first",
-    )(*sources, *after)
-    return part, sums
+    )(*sources)
+    return result[:6], result[6:10], result[10]
+
+
+def states_mine_kernel(square, *refs):
+    local, inner, sums = refs[:4], refs[-3:-1], refs[-1]
+    row = my_row(square)
+    for kind in range(2):
+
+        @pl.when(row == kind)
+        def _():
+            sum_kind(kind, (), local, sums, *inner)
+
+
+def states_mine(square, local, after):
+    inner = part_shapes(local[0].shape[0])[4:]
+    out = [*inner, PIECE]
+    kernel = functools.partial(states_mine_kernel, square)
+    *inner, sums = call(kernel, out, local, after, cost=LONG, limit=2, name="states_mine")
+    return [*local, *inner], sums
 
 
 def states_second_kernel(square, *refs):
@@ -498,9 +521,9 @@
     def run(kernel, out, operands, after):
         return call(kernel, out, operands, after, name=(kernel.func if hasattr(kernel, "func") else kernel).__name__)
 
-    part_eo, start_o = states_first(square, False, sources, ())
+    part_eo, local_em, start_o = states_first(square, sources)
     start_in = trade(start_o, 1)
-    part_em, start = states_first(square, True, sources, (start_o,))
+    part_em, start = states_mine(square, local_em, (start_o,))
     after = (start,)
     if square:
         (sent,) = run(row_first_kernel, [PIECE], (start, start_in), ())

time: 35.1 us -> 35 us (level)
  Pallas kernels: 24.9 us -> 23.7 us
  waiting for transfers between devices: 0.54 us -> 1.27 us
    pallas_call x2 -> x1, Pallas kernels: 3.66 us -> 2.06 us  [states_first(): pl.pallas_call(functools.partial(states_first_kernel, square), out_shape=...]
    ppermute x10, waiting for transfers between devices: 0.54 us -> 1.27 us  [trade(): return lax.ppermute(value, 'seq', [(i, i ^ distance) for i in range(count)])]
    pallas_call x7 -> x8, Pallas kernels: 0.59 us -> 1.01 us  [call(): pl.pallas_call(kernel, out_shape=out, in_specs=[IN_VMEM] * len(operands)...]
    ppermute x10, starting transfers between devices: 8.56 us -> 8.91 us  [trade(): return lax.ppermute(value, 'seq', [(i, i ^ distance) for i in range(count)])]
  transfers between devices with their start and end apart: 10 -> 10, of which waited for: 2 -> 3; matrix products, arithmetic and copies ran while one was open for 0% -> 0% of each run, Pallas kernels for 61% -> 57%
where the time goes in v6:
time: 35 us; the launch traced here: 34.8 us
  Pallas kernels  23.7 us (68%)
  starting transfers between devices  8.91 us (25%)
  waiting for transfers between devices  1.27 us (4%)
  between operations  0.97 us (3%)
    ppermute x10, starting transfers between devices, trade(): return lax.ppermute(value, 'seq', [(i, i ^ distance) for i in range(count)])  8.91 us
    pallas_call x5, Pallas kernels, within(): pl.pallas_call(functools.partial(within_kernel, scale, tuple(pairs)), out...  7.8 us
    pallas_call x3, Pallas kernels, finish(): pl.pallas_call(functools.partial(finish_kernel, scale, square, group, hal...  6.9 us
    pallas_call x1, Pallas kernels, states_second(): pl.pallas_call(functools.partial(states_second_kernel, square), out_shape...  3.39 us
    pallas_call x1, Pallas kernels, states_other(): pl.pallas_call(functools.partial(states_other_kernel, square), out_shape=...  2.52 us
    pallas_call x1, Pallas kernels, states_first(): pl.pallas_call(functools.partial(states_first_kernel, square), out_shape=...  2.06 us
    ppermute x10, waiting for transfers between devices, trade(): return lax.ppermute(value, 'seq', [(i, i ^ distance) for i in range(count)])  1.27 us
    pallas_call x8, Pallas kernels, call(): pl.pallas_call(kernel, out_shape=out, in_specs=[IN_VMEM] * len(operands)...  1.01 us
  transfers between devices with their start and end apart: 10, of which 3 were waited for; matrix products, arithmetic and copies ran while one was open for 0% of the time, Pallas kernels for 57%

profile of v6, /device:TPU:0, one launch (start us, length us, event | category | flops | bytes accessed | tf_op | source)
XLA Modules:
  0.0 34.8 jit_solution(16552349533876482590)
XLA Ops:
  0.6 2.1 %states_first.1 = (bf16[768,512]{1,0:T(8,128)(2,1)S(1)}, bf16[768,512]{1,0:T(8,128)(2,1)S(1)}, bf16[768,512]{1,0:T(8,128)(2,1)S(1)}, bf16[768,512]{1,0:T(8,128)(...) custom-call(bf16[768,2048]{1,0:T(8,128)(2,1)} %refs_0_.5, ...), custom_call_target="tpu_custom_call" | custom-call | flops 20000000000 | bytes 1000 | tf_op jit(solution)/shard_map/states_first/pallas_call | solution.py:193
  2.7 0.5 %collective-permute-start = (f32[4,128,128]{2,1,0:T(8,128)S(1)}, f32[4,128,128]{2,1,0:T(8,128)S(1)}, u32[]{:S(2)}, u32[]{:S(2)}) collective-permute-start(f32[4,128,128]{2,1,0:T(8,128)S(1)} %get-tuple-element.75.refs_4_), channel_id=1, source_target_pairs={{0,1},{1,0},{2,3},{3,2},{4,5},{5,4},{6,7},{7,6},{8,9},{9,8},{10,11... | collective-permute-start | bytes 786440 | tf_op jit(solution)/shard_map/ppermute | solution.py:519
  3.2 0.4 %states_mine.1 = (f32[4,2,128,128]{3,2,1,0:T(8,128)S(1)}, f32[4,2,128,128]{3,2,1,0:T(8,128)S(1)}, f32[4,128,128]{2,1,0:T(8,128)S(1)}) custom-call(bf16[768,512]{1,0:T(8,128)(2,1)S(1)} %get-tuple-element.71.refs_0_.refs_10_, bf16[768,512]{1,0:T(8,128)(2,1)S(1)} %get-tuple-element.72.refs_1_.refs_11_, bf16[768,512]{1,0:T(8,128)(2,1)S(1)} %get-tuple-element.73.refs_2_.refs_12_, ...), custom_call_target="tpu_custom_call" | custom-call | flops 20000000000 | bytes 1000 | tf_op jit(solution)/shard_map/states_mine/pallas_call | solution.py:65
  3.6 0.7 %collective-permute-done.start_in = f32[4,128,128]{2,1,0:T(8,128)S(1)} collective-permute-done((f32[4,128,128]{2,1,0:T(8,128)S(1)}, f32[4,128,128]{2,1,0:T(8,128)S(1)}, u32[]{:S(2)}, u32[]{:S(2)}) %collective-permute-start) | collective-permute-done | bytes 262176 | tf_op jit(solution)/shard_map/ppermute | solution.py:519
  4.4 3.0 %collective-permute-start.2 = (f32[4,128,128]{2,1,0:T(8,128)S(1)}, f32[4,128,128]{2,1,0:T(8,128)S(1)}, u32[]{:S(2)}, u32[]{:S(2)}) collective-permute-start(f32[4,128,128]{2,1,0:T(8,128)S(1)} %row_first_kernel.1.refs_4_), channel_id=1, source_target_pairs={{0,2},{1,3},{2,0},{3,1},{4,6},{5,7},{6,4},{7,5},{8,10},{9,11},{10,... | collective-permute-start | bytes 786440 | tf_op jit(solution)/shard_map/ppermute | solution.py:519
  7.4 3.4 %states_second.1 = (bf16[768,512]{1,0:T(8,128)(2,1)S(1)}, bf16[768,512]{1,0:T(8,128)(2,1)S(1)}, bf16[768,512]{1,0:T(8,128)(2,1)S(1)}, bf16[768,512]{1,0:T(8,128)...) custom-call(bf16[768,2048]{1,0:T(8,128)(2,1)} %refs_0_.5, ...), custom_call_target="tpu_custom_call" | custom-call | flops 20000000000 | bytes 1000 | tf_op jit(solution)/shard_map/states_second/pallas_call | solution.py:238
  10.8 0.1 collective-permute-start.1
  10.8 1.9 %within.5 = (f32[768,512]{1,0:T(8,128)S(1)}, f32[768,512]{1,0:T(8,128)S(1)}, f32[768,512]{1,0:T(8,128)S(1)}) custom-call(bf16[768,512]{1,0:T(8,128)(2,1)S(1)} %get-tuple-element.80.refs_0_, bf16[768,512]{1,0:T(8,128)(2,1)S(1)} %get-tuple-element.77.refs_1_.refs_0_, bf16[768,512]{1,0:T(8,128)(2,1)S(1)} %get-tuple-element.78.refs_2_.refs_1_, ...), custom_call_target="tpu_custom_call" | custom-call | flops 20000000000 | bytes 1000 | tf_op jit(solution)/shard_map/within/pallas_call | solution.py:290
  12.8 0.0 collective-permute-done.1.rest_in
  12.8 0.2 collective-permute-start.5
  13.0 1.0 %within.6 = (f32[768,512]{1,0:T(8,128)S(1)}, f32[768,512]{1,0:T(8,128)S(1)}, f32[768,512]{1,0:T(8,128)S(1)}) custom-call(bf16[768,512]{1,0:T(8,128)(2,1)S(1)} %get-tuple-element.94.refs_0_, bf16[768,512]{1,0:T(8,128)(2,1)S(1)} %get-tuple-element.95.refs_1_.refs_0_, bf16[768,512]{1,0:T(8,128)(2,1)S(1)} %get-tuple-element.96.refs_2_.refs_1_, ...), custom_call_target="tpu_custom_call" | custom-call | flops 20000000000 | bytes 1000 | tf_op jit(solution)/shard_map/within/pallas_call | solution.py:290
  14.1 0.0 collective-permute-done.2.from_row.row_first
  14.1 0.1 column_first_kernel.1.refs_16_
  14.1 1.9 %collective-permute-start.4 = (f32[4,128,128]{2,1,0:T(8,128)S(1)}, f32[4,128,128]{2,1,0:T(8,128)S(1)}, u32[]{:S(2)}, u32[]{:S(2)}) collective-permute-start(f32[4,128,128]{2,1,0:T(8,128)S(1)} %column_first_kernel.1.refs_16_), channel_id=1, source_target_pairs={{0,4},{1,5},{2,6},{3,7},{4,0},{5,1},{6,2},{7,3},{8,12},{9,13},{10,... | collective-permute-start | bytes 786440 | tf_op jit(solution)/shard_map/ppermute | solution.py:519
  16.0 2.5 %states_other.1 = (bf16[768,512]{1,0:T(8,128)(2,1)S(1)}, bf16[768,512]{1,0:T(8,128)(2,1)S(1)}, bf16[768,512]{1,0:T(8,128)(2,1)S(1)}, bf16[768,512]{1,0:T(8,128)(...) custom-call(bf16[768,2048]{1,0:T(8,128)(2,1)} %refs_0_.5, ...), custom_call_target="tpu_custom_call", output_to_operand_aliasing={{0}: (4, {}), {1}: (5, {}), {2}: (6, {}), {3}: (7, {}), {4}... | custom-call | flops 20000000000 | bytes 1000 | tf_op jit(solution)/shard_map/states_other/pallas_call | solution.py:270
  18.5 0.1 collective-permute-start.3
  18.6 1.0 %within.7 = (f32[768,512]{1,0:T(8,128)S(1)}, f32[768,512]{1,0:T(8,128)S(1)}, f32[768,512]{1,0:T(8,128)S(1)}) custom-call(bf16[768,512]{1,0:T(8,128)(2,1)S(1)} %get-tuple-element.94.refs_0_, bf16[768,512]{1,0:T(8,128)(2,1)S(1)} %get-tuple-element.95.refs_1_.refs_0_, ...), custom_call_target="tpu_custom_call", output_to_operand_aliasing={{0}: (4, {}), {1}: (5, {}), {2}: (6, {})} | custom-call | flops 20000000000 | bytes 1000 | tf_op jit(solution)/shard_map/within/pallas_call | solution.py:290
  19.6 1.9 %within.8 = (f32[768,512]{1,0:T(8,128)S(1)}, f32[768,512]{1,0:T(8,128)S(1)}, f32[768,512]{1,0:T(8,128)S(1)}) custom-call(bf16[768,512]{1,0:T(8,128)(2,1)S(1)} %get-tuple-element.101.refs_0_, bf16[768,512]{1,0:T(8,128)(2,1)S(1)} %get-tuple-element.102.refs_1_.refs_9_, bf16[768,512]{1,0:T(8,128)(2,1)S(1)} %get-tuple-element.103.refs_2_.refs_10_, ...), custom_call_target="tpu_custom_call" | custom-call | flops 20000000000 | bytes 1000 | tf_op jit(solution)/shard_map/within/pallas_call | solution.py:290
  21.5 0.0 collective-permute-done.5.from_row.row_second
  21.6 1.4 %collective-permute-start.7 = (f32[4,128,128]{2,1,0:T(8,128)S(1)}, f32[4,128,128]{2,1,0:T(8,128)S(1)}, u32[]{:S(2)}, u32[]{:S(2)}) collective-permute-start(f32[4,128,128]{2,1,0:T(8,128)S(1)} %column_second_kernel.1.refs_0_), channel_id=1, source_target_pairs={{0,4},{1,5},{2,6},{3,7},{4,0},{5,1},{6,2},{7,3},{8,12},{9,13},{10,... | collective-permute-start | bytes 786440 | tf_op jit(solution)/shard_map/ppermute | solution.py:519
  23.0 0.0 collective-permute-done.4.from_column.column_first
  23.0 0.0 collective-permute-done.3.later_in
  23.1 1.5 %collective-permute-start.6 = (f32[4,128,128]{2,1,0:T(8,128)S(1)}, f32[4,128,128]{2,1,0:T(8,128)S(1)}, u32[]{:S(2)}, u32[]{:S(2)}) collective-permute-start(f32[4,128,128]{2,1,0:T(8,128)S(1)} %row_third_kernel.1.refs_0_), channel_id=1, source_target_pairs={{0,2},{1,3},{2,0},{3,1},{4,6},{5,7},{6,4},{7,5},{8,10},{9,11},{10,... | collective-permute-start | bytes 786440 | tf_op jit(solution)/shard_map/ppermute | solution.py:519
  24.6 0.2 first_states_kernel.1
  24.9 0.1 collective-permute-start.8
  24.9 1.9 %within.9 = (f32[768,512]{1,0:T(8,128)S(1)}, f32[768,512]{1,0:T(8,128)S(1)}, f32[768,512]{1,0:T(8,128)S(1)}) custom-call(bf16[768,512]{1,0:T(8,128)(2,1)S(1)} %get-tuple-element.112.refs_0_, bf16[768,512]{1,0:T(8,128)(2,1)S(1)} %get-tuple-element.109.refs_1_.refs_0_, bf16[768,512]{1,0:T(8,128)(2,1)S(1)} %get-tuple-element.110.refs_2_.refs_1_, ...), custom_call_target="tpu_custom_call" | custom-call | flops 20000000000 | bytes 1000 | tf_op jit(solution)/shard_map/within/pallas_call | solution.py:290
  26.9 0.4 %collective-permute-done.8.refs_15_.refs_24_ = f32[3,4,128,128]{3,2,1,0:T(8,128)S(1)} collective-permute-done((f32[3,4,128,128]{3,2,1,0:T(8,128)S(1)}, f32[3,4,128,128]{3,2,1,0:T(8,128)S(1)}, u32[]{:S(2)}, u32[]{:S(2)}) %collective-permute-start.8) | collective-permute-done | bytes 786464 | tf_op jit(solution)/shard_map/ppermute | solution.py:519
  27.2 3.6 %finish.3 = (bf16[768,2048]{1,0:T(8,128)(2,1)}, bf16[768,2048]{1,0:T(8,128)(2,1)}, bf16[768,2048]{1,0:T(8,128)(2,1)}) custom-call(bf16[768,512]{1,0:T(8,128)(2,1)S(1)} %get-tuple-element.109.refs_1_.refs_0_, bf16[768,512]{1,0:T(8,128)(2,1)S(1)} %get-tuple-element.110.refs_2_.refs_1_, bf16[768,512]{1,0:T(8,128)(2,1)S(1)} %get-tuple-element.111.refs_3_.refs_2_, ...), custom_call_target="tpu_custom_call" | custom-call | flops 20000000000 | bytes 1000 | tf_op jit(solution)/shard_map/finish/pallas_call | solution.py:496
  30.9 0.0 collective-permute-done.6.row_third
  30.9 0.0 collective-permute-done.7.column_second
  30.9 0.2 second_states_kernel.1
  31.1 0.2 collective-permute-start.9
  31.3 1.6 %finish.4 = (bf16[768,2048]{1,0:T(8,128)(2,1)}, bf16[768,2048]{1,0:T(8,128)(2,1)}, bf16[768,2048]{1,0:T(8,128)(2,1)}) custom-call(bf16[768,512]{1,0:T(8,128)(2,1)S(1)} %get-tuple-element.95.refs_1_.refs_0_, bf16[768,512]{1,0:T(8,128)(2,1)S(1)} %get-tuple-element.96.refs_2_.refs_1_, ...), custom_call_target="tpu_custom_call", output_to_operand_aliasing={{0}: (9, {}), {1}: (10, {}), {2}: (11, {})} | custom-call | flops 20000000000 | bytes 1000 | tf_op jit(solution)/shard_map/finish/pallas_call | solution.py:496
  32.9 0.1 collective-permute-done.9.refs_6_
  33.0 1.6 %finish.5 = (bf16[768,2048]{1,0:T(8,128)(2,1)}, bf16[768,2048]{1,0:T(8,128)(2,1)}, bf16[768,2048]{1,0:T(8,128)(2,1)}) custom-call(bf16[768,512]{1,0:T(8,128)(2,1)S(1)} %get-tuple-element.77.refs_1_.refs_0_, bf16[768,512]{1,0:T(8,128)(2,1)S(1)} %get-tuple-element.78.refs_2_.refs_1_, ...), custom_call_target="tpu_custom_call", output_to_operand_aliasing={{0}: (9, {}), {1}: (10, {}), {2}: (11, {})} | custom-call | flops 20000000000 | bytes 1000 | tf_op jit(solution)/shard_map/finish/pallas_call | solution.py:496
  (4 shorter events, 0.2 us)
Async XLA Ops:
  2.7 1.7 %collective-permute-start = (f32[4,128,128]{2,1,0:T(8,128)S(1)}, f32[4,128,128]{2,1,0:T(8,128)S(1)}, u32[]{:S(2)}, u32[]{:S(2)}) collective-permute-start(f32[4,128,128]{2,1,0:T(8,128)S(1)} %get-tuple-element.75.refs_4_), channel_id=1, source_target_pairs={{0,1},{1,0},{2,3},{3,2},{4,5},{5,4},{6,7},{7,6},{8,9},{9,8},{10,11... | collective-permute-start | bytes 786440 | tf_op jit(solution)/shard_map/ppermute | solution.py:519
  4.4 9.6 %collective-permute-start.2 = (f32[4,128,128]{2,1,0:T(8,128)S(1)}, f32[4,128,128]{2,1,0:T(8,128)S(1)}, u32[]{:S(2)}, u32[]{:S(2)}) collective-permute-start(f32[4,128,128]{2,1,0:T(8,128)S(1)} %row_first_kernel.1.refs_4_), channel_id=1, source_target_pairs={{0,2},{1,3},{2,0},{3,1},{4,6},{5,7},{6,4},{7,5},{8,10},{9,11},{10,... | collective-permute-start | bytes 786440 | tf_op jit(solution)/shard_map/ppermute | solution.py:519
  10.8 2.0 %collective-permute-start.1 = (f32[2,4,128,128]{3,2,1,0:T(8,128)S(1)}, f32[2,4,128,128]{3,2,1,0:T(8,128)S(1)}, u32[]{:S(2)}, u32[]{:S(2)}) collective-permute-start(f32[2,4,128,128]{3,2,1,0:T(8,128)S(1)} %get-tuple-element.81.refs_4_), channel_id=1, source_target_pairs={{0,1},{1,0},{2,3},{3,2},{4,5},{5,4},{6,7},{7,6},{8,9},{9,8},{10,11... | collective-permute-start | bytes 1572872 | tf_op jit(solution)/shard_map/ppermute | solution.py:519
  12.8 8.8 %collective-permute-start.5 = (f32[4,128,128]{2,1,0:T(8,128)S(1)}, f32[4,128,128]{2,1,0:T(8,128)S(1)}, u32[]{:S(2)}, u32[]{:S(2)}) collective-permute-start(f32[4,128,128]{2,1,0:T(8,128)S(1)} %row_second_kernel.1.refs_4_), channel_id=1, source_target_pairs={{0,2},{1,3},{2,0},{3,1},{4,6},{5,7},{6,4},{7,5},{8,10},{9,11},{10,... | collective-permute-start | bytes 786440 | tf_op jit(solution)/shard_map/ppermute | solution.py:519
  14.1 8.9 %collective-permute-start.4 = (f32[4,128,128]{2,1,0:T(8,128)S(1)}, f32[4,128,128]{2,1,0:T(8,128)S(1)}, u32[]{:S(2)}, u32[]{:S(2)}) collective-permute-start(f32[4,128,128]{2,1,0:T(8,128)S(1)} %column_first_kernel.1.refs_16_), channel_id=1, source_target_pairs={{0,4},{1,5},{2,6},{3,7},{4,0},{5,1},{6,2},{7,3},{8,12},{9,13},{10,... | collective-permute-start | bytes 786440 | tf_op jit(solution)/shard_map/ppermute | solution.py:519
  18.5 4.5 %collective-permute-start.3 = (f32[4,128,128]{2,1,0:T(8,128)S(1)}, f32[4,128,128]{2,1,0:T(8,128)S(1)}, u32[]{:S(2)}, u32[]{:S(2)}) collective-permute-start(f32[4,128,128]{2,1,0:T(8,128)S(1)} %get-tuple-element.100.refs_7_), channel_id=1, source_target_pairs={{0,1},{1,0},{2,3},{3,2},{4,5},{5,4},{6,7},{7,6},{8,9},{9,8},{10,11... | collective-permute-start | bytes 786440 | tf_op jit(solution)/shard_map/ppermute | solution.py:519
  21.6 9.2 %collective-permute-start.7 = (f32[4,128,128]{2,1,0:T(8,128)S(1)}, f32[4,128,128]{2,1,0:T(8,128)S(1)}, u32[]{:S(2)}, u32[]{:S(2)}) collective-permute-start(f32[4,128,128]{2,1,0:T(8,128)S(1)} %column_second_kernel.1.refs_0_), channel_id=1, source_target_pairs={{0,4},{1,5},{2,6},{3,7},{4,0},{5,1},{6,2},{7,3},{8,12},{9,13},{10,... | collective-permute-start | bytes 786440 | tf_op jit(solution)/shard_map/ppermute | solution.py:519
  23.1 7.8 %collective-permute-start.6 = (f32[4,128,128]{2,1,0:T(8,128)S(1)}, f32[4,128,128]{2,1,0:T(8,128)S(1)}, u32[]{:S(2)}, u32[]{:S(2)}) collective-permute-start(f32[4,128,128]{2,1,0:T(8,128)S(1)} %row_third_kernel.1.refs_0_), channel_id=1, source_target_pairs={{0,2},{1,3},{2,0},{3,1},{4,6},{5,7},{6,4},{7,5},{8,10},{9,11},{10,... | collective-permute-start | bytes 786440 | tf_op jit(solution)/shard_map/ppermute | solution.py:519
  24.9 2.4 %collective-permute-start.8 = (f32[3,4,128,128]{3,2,1,0:T(8,128)S(1)}, f32[3,4,128,128]{3,2,1,0:T(8,128)S(1)}, u32[]{:S(2)}, u32[]{:S(2)}) collective-permute-start(f32[3,4,128,128]{3,2,1,0:T(8,128)S(1)} %get-tuple-element.121), channel_id=1, source_target_pairs={{0,1},{1,0},{2,3},{3,2},{4,5},{5,4},{6,7},{7,6},{8,9},{9,8},{10,11... | collective-permute-start | bytes 2359304 | tf_op jit(solution)/shard_map/ppermute | solution.py:519
  31.1 2.0 %collective-permute-start.9 = (f32[2,4,128,128]{3,2,1,0:T(8,128)S(1)}, f32[2,4,128,128]{3,2,1,0:T(8,128)S(1)}, u32[]{:S(2)}, u32[]{:S(2)}) collective-permute-start(f32[2,4,128,128]{3,2,1,0:T(8,128)S(1)} %get-tuple-element.128), channel_id=1, source_target_pairs={{0,1},{1,0},{2,3},{3,2},{4,5},{5,4},{6,7},{7,6},{8,9},{9,8},{10,11... | collective-permute-start | bytes 1572872 | tf_op jit(solution)/shard_map/ppermute | solution.py:519

commit v7 on v6

--- a/solution.py
+++ b/solution.py
@@ -249,7 +249,9 @@
 
 
 def states_other_kernel(square, *refs):
-    sources, parts, sums, sems = refs[:4], (refs[-15:-9], refs[-9:-3]), refs[-3:-1], refs[-1]
+    sources, along, parts, sems = refs[:4], refs[16], (refs[-15:-9], refs[-9:-3]), refs[-1]
+    sums = refs[-3].at[0], refs[-2]
+    refs[-3][1] = along[...]
     row = my_row(square)
     copies = {}
     for mine in range(2):
@@ -265,19 +267,19 @@
                 sum_kind(kind, copies[mine, kind], parts[mine][:4], sums[mine], *parts[mine][4:])
 
 
-def states_other(square, sources, other, mine, after):
-    out = part_shapes(sources[0].shape[0]) * 2 + [PIECE] * 2
+def states_other(square, sources, other, mine, along, after):
+    out = part_shapes(sources[0].shape[0]) * 2 + [state_of(GROUP), PIECE]
     result = pl.pallas_call(
         functools.partial(states_other_kernel, square),
         out_shape=out,
-        in_specs=[ANYWHERE] * 4 + [IN_VMEM] * 12 + [ANYWHERE] * len(after),
+        in_specs=[ANYWHERE] * 4 + [IN_VMEM] * 13 + [ANYWHERE] * len(after),
         out_specs=[IN_VMEM] * len(out),
         scratch_shapes=[pltpu.SemaphoreType.DMA((2, 4))],
         input_output_aliases={4 + i: i for i in range(12)},
         compiler_params=pltpu.CompilerParams(vmem_limit_bytes=2 << 20),
         cost_estimate=LONG,
         name="states_other",
-    )(*sources, *other, *mine, *after)
+    )(*sources, *other, *mine, along, *after)
     return result[:6], result[6:12], *result[12:]
 
 
@@ -324,7 +326,7 @@
 
 def sums_of_group(group, head, start, start_in, later, later_in, rest, rest_in):
     if group == 0:
-        return first_group(False, head, start, later), first_group(False, head, start_in, later_in)
+        return first_group(False, head, start, later), first_group(False, head, start_in, later_in.at[0])
     return second_group(head, rest), second_group(head, rest_in)
 
 
@@ -360,9 +362,14 @@
 
 
 def column_first_kernel(rest, rest_in, from_row, *refs):
+    sent, own_prefix, other_prefix = refs[-3:]
     kind = my_row(True)
-    for head in range(GROUP):
-        refs[-1][head] = rest[kind, head] + rest_in[kind, head] + from_row[head]
+    second = my_core() == 1
+    for head in range(GROUP):
+        sent[head] = rest[kind, head] + rest_in[kind, head] + from_row[head]
+        prefix = jnp.where(my_pair() == 1, from_row[head], 0.0)
+        own_prefix[head] = prefix + jnp.where(second, rest_in[0, head], 0.0)
+        other_prefix[head] = prefix + jnp.where(second, 0.0, rest[0, head])
 
 
 def column_second_kernel(start, start_in, from_row, *refs):
@@ -374,23 +381,18 @@
     pair = my_pair()
     outer = (pair == 0) | (pair == 3)
     for head in range(GROUP):
-        refs[-1][head] = jnp.where(outer, from_column[head], later[head] + later_in[head])
-
-
-def first_states_kernel(start, start_in, later, later_in, rest, rest_in, row_first, row_second, column_first, *refs):
-    own, other, own_prefix = refs[-3:]
-    second = my_core() == 1
+        refs[-1][head] = jnp.where(outer, from_column[head], later[head] + later_in[0, head])
+
+
+def first_states_kernel(start, start_in, later, later_in, row_second, column_first, *refs):
     pair = my_pair()
     below, right = pair >= 2, lax.rem(pair, 2) == 1
     for head in range(GROUP):
         row, column = row_second[head], column_first[head]
         prefix = jnp.where(right, row, 0.0) + jnp.where(below, column, 0.0)
         suffix = jnp.where(right, 0.0, row) + jnp.where(below, 0.0, column)
-        sums, sums_in = first_group(True, head, start, later), first_group(True, head, start_in, later_in)
-        settle(head, prefix, suffix, sums, sums_in, own, other.at[pl.ds(0, 2)])
-        prefix = jnp.where(pair == 1, row_first[head], 0.0)
-        own_prefix[head] = prefix + jnp.where(second, rest_in[0, head], 0.0)
-        other[2, head] = prefix + jnp.where(second, 0.0, rest[0, head])
+        sums, sums_in = first_group(True, head, start, later), first_group(True, head, start_in, later_in.at[0])
+        settle(head, prefix, suffix, sums, sums_in, *refs[-2:])
 
 
 def second_states_kernel(rest, rest_in, row_first, row_third, column_second, *refs):
@@ -465,7 +467,7 @@
     for n in range(ahead):
         number = len(halves) + n
         o, dq, prefix, early = rest[4 * n : 4 * n + 4]
-        prefix = prefix if n == 0 else prefix.at[2]
+        prefix = prefix if n == 0 else prefix.at[1]
         query = pieces(0, number)
         sometimes += query
 
@@ -539,13 +541,14 @@
         (sent,) = run(row_second_kernel, [PIECE], sums_l, after)
         row_second = trade(sent, 2)
         partials_lm = within(scale, part_lm[:4], (sent,), range(GROUP // 4))
-        (sent,) = run(column_first_kernel, [PIECE], (*sums_l, row_first), (partials_lm[0],))
+        sent, own_prefix, along = run(column_first_kernel, [PIECE] * 3, (*sums_l, row_first), (partials_lm[0],))
         column_first = trade(sent, 4)
         after = (sent,)
     else:
         partials_lm = within(scale, part_lm[:4], after, range(GROUP // 4))
-
-    part_eo, part_em, later_o, later = states_other(square, sources, part_eo, part_em, after)
+        along = start
+
+    part_eo, part_em, later_o, later = states_other(square, sources, part_eo, part_em, along, after)
     later_in = trade(later_o, 1)
     sums_b = (later, later_in)
     partials_lm = within(scale, part_lm[:4], (later_o,), range(GROUP // 4, GROUP // 2), partials_lm)
@@ -555,9 +558,8 @@
         column_second = trade(sent, 4)
         (sent,) = run(row_third_kernel, [PIECE], (*sums_b, column_first), (sent,))
         row_third = trade(sent, 2)
-        arrived = (row_first, row_second, column_first)
-        out = [state_of(GROUP), pltpu.VMEM((3, GROUP, HEAD_DIM, HEAD_DIM), jnp.float32), PIECE]
-        own_e, other_e, own_prefix = run(first_states_kernel, out, (*sums_e, *sums_b, *sums_l, *arrived), (sent,))
+        arrived = (row_second, column_first)
+        own_e, other_e = run(first_states_kernel, STATES, (*sums_e, *sums_b, *arrived), (sent,))
     else:
         turns = range(1, count // 2)
         arrived = []
@@ -576,7 +578,7 @@
     if square:
         ahead = (
             (part_lm[3], partials_lm[0], own_prefix, part_lm[4]),
-            (part_lo[3], partials_lo[0], other_e, part_lo[4]),
+            (part_lo[3], partials_lo[0], later_in, part_lo[4]),
         )
     done = finish(scale, square, 0, parts, (), ahead)
 

time: 35 us -> 34.9 us (level)
  transfers between devices with their start and end apart: 10 -> 10, of which waited for: 3 -> 2; matrix products, arithmetic and copies ran while one was open for 0% -> 0% of each run, Pallas kernels for 57% -> 57%
where the time goes in v7:
time: 34.9 us; the launch traced here: 34.7 us
  Pallas kernels  23.7 us (68%)
  starting transfers between devices  9 us (26%)
  waiting for transfers between devices  1.05 us (3%)
  between operations  0.98 us (3%)
    ppermute x10, starting transfers between devices, trade(): return lax.ppermute(value, 'seq', [(i, i ^ distance) for i in range(count)])  9 us
    pallas_call x5, Pallas kernels, within(): pl.pallas_call(functools.partial(within_kernel, scale, tuple(pairs)), out...  7.8 us
    pallas_call x3, Pallas kernels, finish(): pl.pallas_call(functools.partial(finish_kernel, scale, square, group, hal...  6.93 us
    pallas_call x1, Pallas kernels, states_second(): pl.pallas_call(functools.partial(states_second_kernel, square), out_shape...  3.39 us
    pallas_call x1, Pallas kernels, states_other(): pl.pallas_call(functools.partial(states_other_kernel, square), out_shape=...  2.54 us
    pallas_call x1, Pallas kernels, states_first(): pl.pallas_call(functools.partial(states_first_kernel, square), out_shape=...  2.06 us
    ppermute x10, waiting for transfers between devices, trade(): return lax.ppermute(value, 'seq', [(i, i ^ distance) for i in range(count)])  1.05 us
    pallas_call x8, Pallas kernels, call(): pl.pallas_call(kernel, out_shape=out, in_specs=[IN_VMEM] * len(operands)...  1 us
  transfers between devices with their start and end apart: 10, of which 2 were waited for; matrix products, arithmetic and copies ran while one was open for 0% of the time, Pallas kernels for 57%

profile of v7, /device:TPU:0, one launch (start us, length us, event | category | flops | bytes accessed | tf_op | source)
XLA Modules:
  0.0 34.7 jit_solution(8141320080002841706)
XLA Ops:
  0.6 2.1 %states_first.1 = (bf16[768,512]{1,0:T(8,128)(2,1)S(1)}, bf16[768,512]{1,0:T(8,128)(2,1)S(1)}, bf16[768,512]{1,0:T(8,128)(2,1)S(1)}, bf16[768,512]{1,0:T(8,128)(...) custom-call(bf16[768,2048]{1,0:T(8,128)(2,1)} %refs_0_.5, ...), custom_call_target="tpu_custom_call" | custom-call | flops 20000000000 | bytes 1000 | tf_op jit(solution)/shard_map/states_first/pallas_call | solution.py:193
  2.7 0.5 %collective-permute-start = (f32[4,128,128]{2,1,0:T(8,128)S(1)}, f32[4,128,128]{2,1,0:T(8,128)S(1)}, u32[]{:S(2)}, u32[]{:S(2)}) collective-permute-start(f32[4,128,128]{2,1,0:T(8,128)S(1)} %get-tuple-element.77.refs_4_), channel_id=1, source_target_pairs={{0,1},{1,0},{2,3},{3,2},{4,5},{5,4},{6,7},{7,6},{8,9},{9,8},{10,11... | collective-permute-start | bytes 786440 | tf_op jit(solution)/shard_map/ppermute | solution.py:521
  3.2 0.4 %states_mine.1 = (f32[4,2,128,128]{3,2,1,0:T(8,128)S(1)}, f32[4,2,128,128]{3,2,1,0:T(8,128)S(1)}, f32[4,128,128]{2,1,0:T(8,128)S(1)}) custom-call(bf16[768,512]{1,0:T(8,128)(2,1)S(1)} %get-tuple-element.73.refs_0_.refs_10_, bf16[768,512]{1,0:T(8,128)(2,1)S(1)} %get-tuple-element.74.refs_1_.refs_11_, bf16[768,512]{1,0:T(8,128)(2,1)S(1)} %get-tuple-element.75.refs_2_.refs_12_, ...), custom_call_target="tpu_custom_call" | custom-call | flops 20000000000 | bytes 1000 | tf_op jit(solution)/shard_map/states_mine/pallas_call | solution.py:65
  3.6 0.7 %collective-permute-done.start_in = f32[4,128,128]{2,1,0:T(8,128)S(1)} collective-permute-done((f32[4,128,128]{2,1,0:T(8,128)S(1)}, f32[4,128,128]{2,1,0:T(8,128)S(1)}, u32[]{:S(2)}, u32[]{:S(2)}) %collective-permute-start) | collective-permute-done | bytes 262176 | tf_op jit(solution)/shard_map/ppermute | solution.py:521
  4.4 3.0 %collective-permute-start.2 = (f32[4,128,128]{2,1,0:T(8,128)S(1)}, f32[4,128,128]{2,1,0:T(8,128)S(1)}, u32[]{:S(2)}, u32[]{:S(2)}) collective-permute-start(f32[4,128,128]{2,1,0:T(8,128)S(1)} %row_first_kernel.1.refs_4_), channel_id=1, source_target_pairs={{0,2},{1,3},{2,0},{3,1},{4,6},{5,7},{6,4},{7,5},{8,10},{9,11},{10,... | collective-permute-start | bytes 786440 | tf_op jit(solution)/shard_map/ppermute | solution.py:521
  7.4 3.4 %states_second.1 = (bf16[768,512]{1,0:T(8,128)(2,1)S(1)}, bf16[768,512]{1,0:T(8,128)(2,1)S(1)}, bf16[768,512]{1,0:T(8,128)(2,1)S(1)}, bf16[768,512]{1,0:T(8,128)...) custom-call(bf16[768,2048]{1,0:T(8,128)(2,1)} %refs_0_.5, ...), custom_call_target="tpu_custom_call" | custom-call | flops 20000000000 | bytes 1000 | tf_op jit(solution)/shard_map/states_second/pallas_call | solution.py:238
  10.8 0.1 collective-permute-start.1
  10.8 1.9 %within.5 = (f32[768,512]{1,0:T(8,128)S(1)}, f32[768,512]{1,0:T(8,128)S(1)}, f32[768,512]{1,0:T(8,128)S(1)}) custom-call(bf16[768,512]{1,0:T(8,128)(2,1)S(1)} %get-tuple-element.82.refs_0_, bf16[768,512]{1,0:T(8,128)(2,1)S(1)} %get-tuple-element.79.refs_1_.refs_0_, bf16[768,512]{1,0:T(8,128)(2,1)S(1)} %get-tuple-element.80.refs_2_.refs_1_, ...), custom_call_target="tpu_custom_call" | custom-call | flops 20000000000 | bytes 1000 | tf_op jit(solution)/shard_map/within/pallas_call | solution.py:292
  12.8 0.0 collective-permute-done.1.rest_in
  12.8 0.2 collective-permute-start.5
  13.0 1.0 %within.6 = (f32[768,512]{1,0:T(8,128)S(1)}, f32[768,512]{1,0:T(8,128)S(1)}, f32[768,512]{1,0:T(8,128)S(1)}) custom-call(bf16[768,512]{1,0:T(8,128)(2,1)S(1)} %get-tuple-element.96.refs_0_, bf16[768,512]{1,0:T(8,128)(2,1)S(1)} %get-tuple-element.97.refs_1_.refs_0_, bf16[768,512]{1,0:T(8,128)(2,1)S(1)} %get-tuple-element.98.refs_2_.refs_1_, ...), custom_call_target="tpu_custom_call" | custom-call | flops 20000000000 | bytes 1000 | tf_op jit(solution)/shard_map/within/pallas_call | solution.py:292
  14.1 0.0 collective-permute-done.2.from_row.row_first
  14.1 0.1 column_first_kernel.1
  14.2 1.9 %collective-permute-start.4 = (f32[4,128,128]{2,1,0:T(8,128)S(1)}, f32[4,128,128]{2,1,0:T(8,128)S(1)}, u32[]{:S(2)}, u32[]{:S(2)}) collective-permute-start(f32[4,128,128]{2,1,0:T(8,128)S(1)} %get-tuple-element.102.refs_17_), channel_id=1, source_target_pairs={{0,4},{1,5},{2,6},{3,7},{4,0},{5,1},{6,2},{7,3},{8,12},{9,13},{10,... | collective-permute-start | bytes 786440 | tf_op jit(solution)/shard_map/ppermute | solution.py:521
  16.0 2.5 %states_other.1 = (bf16[768,512]{1,0:T(8,128)(2,1)S(1)}, bf16[768,512]{1,0:T(8,128)(2,1)S(1)}, bf16[768,512]{1,0:T(8,128)(2,1)S(1)}, bf16[768,512]{1,0:T(8,128)(...) custom-call(bf16[768,2048]{1,0:T(8,128)(2,1)} %refs_0_.5, ...), custom_call_target="tpu_custom_call", output_to_operand_aliasing={{0}: (4, {}), {1}: (5, {}), {2}: (6, {}), {3}: (7, {}), {4}... | custom-call | flops 20000000000 | bytes 1000 | tf_op jit(solution)/shard_map/states_other/pallas_call | solution.py:272
  18.6 0.1 collective-permute-start.3
  18.7 1.0 %within.7 = (f32[768,512]{1,0:T(8,128)S(1)}, f32[768,512]{1,0:T(8,128)S(1)}, f32[768,512]{1,0:T(8,128)S(1)}) custom-call(bf16[768,512]{1,0:T(8,128)(2,1)S(1)} %get-tuple-element.96.refs_0_, bf16[768,512]{1,0:T(8,128)(2,1)S(1)} %get-tuple-element.97.refs_1_.refs_0_, ...), custom_call_target="tpu_custom_call", output_to_operand_aliasing={{0}: (4, {}), {1}: (5, {}), {2}: (6, {})} | custom-call | flops 20000000000 | bytes 1000 | tf_op jit(solution)/shard_map/within/pallas_call | solution.py:292
  19.7 1.9 %within.8 = (f32[768,512]{1,0:T(8,128)S(1)}, f32[768,512]{1,0:T(8,128)S(1)}, f32[768,512]{1,0:T(8,128)S(1)}) custom-call(bf16[768,512]{1,0:T(8,128)(2,1)S(1)} %get-tuple-element.105.refs_0_, bf16[768,512]{1,0:T(8,128)(2,1)S(1)} %get-tuple-element.106.refs_1_.refs_9_, bf16[768,512]{1,0:T(8,128)(2,1)S(1)} %get-tuple-element.107.refs_2_.refs_10_, ...), custom_call_target="tpu_custom_call" | custom-call | flops 20000000000 | bytes 1000 | tf_op jit(solution)/shard_map/within/pallas_call | solution.py:292
  21.6 0.0 collective-permute-done.5.from_row.row_second
  21.7 1.4 %collective-permute-start.7 = (f32[4,128,128]{2,1,0:T(8,128)S(1)}, f32[4,128,128]{2,1,0:T(8,128)S(1)}, u32[]{:S(2)}, u32[]{:S(2)}) collective-permute-start(f32[4,128,128]{2,1,0:T(8,128)S(1)} %column_second_kernel.1.refs_0_), channel_id=1, source_target_pairs={{0,4},{1,5},{2,6},{3,7},{4,0},{5,1},{6,2},{7,3},{8,12},{9,13},{10,... | collective-permute-start | bytes 786440 | tf_op jit(solution)/shard_map/ppermute | solution.py:521
  23.0 0.0 collective-permute-done.4.from_column.column_first
  23.0 0.0 collective-permute-done.3.later_in.refs_24_
  23.1 1.6 %collective-permute-start.6 = (f32[4,128,128]{2,1,0:T(8,128)S(1)}, f32[4,128,128]{2,1,0:T(8,128)S(1)}, u32[]{:S(2)}, u32[]{:S(2)}) collective-permute-start(f32[4,128,128]{2,1,0:T(8,128)S(1)} %row_third_kernel.1.refs_0_), channel_id=1, source_target_pairs={{0,2},{1,3},{2,0},{3,1},{4,6},{5,7},{6,4},{7,5},{8,10},{9,11},{10,... | collective-permute-start | bytes 786440 | tf_op jit(solution)/shard_map/ppermute | solution.py:521
  24.7 0.2 first_states_kernel.1
  24.9 0.1 collective-permute-start.8
  24.9 1.9 %within.9 = (f32[768,512]{1,0:T(8,128)S(1)}, f32[768,512]{1,0:T(8,128)S(1)}, f32[768,512]{1,0:T(8,128)S(1)}) custom-call(bf16[768,512]{1,0:T(8,128)(2,1)S(1)} %get-tuple-element.116.refs_0_, bf16[768,512]{1,0:T(8,128)(2,1)S(1)} %get-tuple-element.113.refs_1_.refs_0_, bf16[768,512]{1,0:T(8,128)(2,1)S(1)} %get-tuple-element.114.refs_2_.refs_1_, ...), custom_call_target="tpu_custom_call" | custom-call | flops 20000000000 | bytes 1000 | tf_op jit(solution)/shard_map/within/pallas_call | solution.py:292
  26.9 0.0 collective-permute-done.8.refs_15_
  26.9 3.7 %finish.3 = (bf16[768,2048]{1,0:T(8,128)(2,1)}, bf16[768,2048]{1,0:T(8,128)(2,1)}, bf16[768,2048]{1,0:T(8,128)(2,1)}) custom-call(bf16[768,512]{1,0:T(8,128)(2,1)S(1)} %get-tuple-element.113.refs_1_.refs_0_, bf16[768,512]{1,0:T(8,128)(2,1)S(1)} %get-tuple-element.114.refs_2_.refs_1_, bf16[768,512]{1,0:T(8,128)(2,1)S(1)} %get-tuple-element.115.refs_3_.refs_2_, ...), custom_call_target="tpu_custom_call" | custom-call | flops 20000000000 | bytes 1000 | tf_op jit(solution)/shard_map/finish/pallas_call | solution.py:498
  30.5 0.0 collective-permute-done.7.column_second
  30.5 0.3 collective-permute-done.6.row_third
  30.8 0.2 second_states_kernel.1
  31.0 0.3 collective-permute-start.9
  31.3 1.6 %finish.4 = (bf16[768,2048]{1,0:T(8,128)(2,1)}, bf16[768,2048]{1,0:T(8,128)(2,1)}, bf16[768,2048]{1,0:T(8,128)(2,1)}) custom-call(bf16[768,512]{1,0:T(8,128)(2,1)S(1)} %get-tuple-element.97.refs_1_.refs_0_, bf16[768,512]{1,0:T(8,128)(2,1)S(1)} %get-tuple-element.98.refs_2_.refs_1_, ...), custom_call_target="tpu_custom_call", output_to_operand_aliasing={{0}: (9, {}), {1}: (10, {}), {2}: (11, {})} | custom-call | flops 20000000000 | bytes 1000 | tf_op jit(solution)/shard_map/finish/pallas_call | solution.py:498
  32.9 0.0 collective-permute-done.9.refs_6_
  32.9 1.6 %finish.5 = (bf16[768,2048]{1,0:T(8,128)(2,1)}, bf16[768,2048]{1,0:T(8,128)(2,1)}, bf16[768,2048]{1,0:T(8,128)(2,1)}) custom-call(bf16[768,512]{1,0:T(8,128)(2,1)S(1)} %get-tuple-element.79.refs_1_.refs_0_, bf16[768,512]{1,0:T(8,128)(2,1)S(1)} %get-tuple-element.80.refs_2_.refs_1_, ...), custom_call_target="tpu_custom_call", output_to_operand_aliasing={{0}: (9, {}), {1}: (10, {}), {2}: (11, {})} | custom-call | flops 20000000000 | bytes 1000 | tf_op jit(solution)/shard_map/finish/pallas_call | solution.py:498
  (4 shorter events, 0.2 us)
Async XLA Ops:
  2.7 1.7 %collective-permute-start = (f32[4,128,128]{2,1,0:T(8,128)S(1)}, f32[4,128,128]{2,1,0:T(8,128)S(1)}, u32[]{:S(2)}, u32[]{:S(2)}) collective-permute-start(f32[4,128,128]{2,1,0:T(8,128)S(1)} %get-tuple-element.77.refs_4_), channel_id=1, source_target_pairs={{0,1},{1,0},{2,3},{3,2},{4,5},{5,4},{6,7},{7,6},{8,9},{9,8},{10,11... | collective-permute-start | bytes 786440 | tf_op jit(solution)/shard_map/ppermute | solution.py:521
  4.4 9.6 %collective-permute-start.2 = (f32[4,128,128]{2,1,0:T(8,128)S(1)}, f32[4,128,128]{2,1,0:T(8,128)S(1)}, u32[]{:S(2)}, u32[]{:S(2)}) collective-permute-start(f32[4,128,128]{2,1,0:T(8,128)S(1)} %row_first_kernel.1.refs_4_), channel_id=1, source_target_pairs={{0,2},{1,3},{2,0},{3,1},{4,6},{5,7},{6,4},{7,5},{8,10},{9,11},{10,... | collective-permute-start | bytes 786440 | tf_op jit(solution)/shard_map/ppermute | solution.py:521
  10.8 2.0 %collective-permute-start.1 = (f32[2,4,128,128]{3,2,1,0:T(8,128)S(1)}, f32[2,4,128,128]{3,2,1,0:T(8,128)S(1)}, u32[]{:S(2)}, u32[]{:S(2)}) collective-permute-start(f32[2,4,128,128]{3,2,1,0:T(8,128)S(1)} %get-tuple-element.83.refs_4_), channel_id=1, source_target_pairs={{0,1},{1,0},{2,3},{3,2},{4,5},{5,4},{6,7},{7,6},{8,9},{9,8},{10,11... | collective-permute-start | bytes 1572872 | tf_op jit(solution)/shard_map/ppermute | solution.py:521
  12.8 8.8 %collective-permute-start.5 = (f32[4,128,128]{2,1,0:T(8,128)S(1)}, f32[4,128,128]{2,1,0:T(8,128)S(1)}, u32[]{:S(2)}, u32[]{:S(2)}) collective-permute-start(f32[4,128,128]{2,1,0:T(8,128)S(1)} %row_second_kernel.1.refs_4_), channel_id=1, source_target_pairs={{0,2},{1,3},{2,0},{3,1},{4,6},{5,7},{6,4},{7,5},{8,10},{9,11},{10,... | collective-permute-start | bytes 786440 | tf_op jit(solution)/shard_map/ppermute | solution.py:521
  14.2 8.9 %collective-permute-start.4 = (f32[4,128,128]{2,1,0:T(8,128)S(1)}, f32[4,128,128]{2,1,0:T(8,128)S(1)}, u32[]{:S(2)}, u32[]{:S(2)}) collective-permute-start(f32[4,128,128]{2,1,0:T(8,128)S(1)} %get-tuple-element.102.refs_17_), channel_id=1, source_target_pairs={{0,4},{1,5},{2,6},{3,7},{4,0},{5,1},{6,2},{7,3},{8,12},{9,13},{10,... | collective-permute-start | bytes 786440 | tf_op jit(solution)/shard_map/ppermute | solution.py:521
  18.6 4.5 %collective-permute-start.3 = (f32[2,4,128,128]{3,2,1,0:T(8,128)S(1)}, f32[2,4,128,128]{3,2,1,0:T(8,128)S(1)}, u32[]{:S(2)}, u32[]{:S(2)}) collective-permute-start(f32[2,4,128,128]{3,2,1,0:T(8,128)S(1)} %get-tuple-element.104.refs_7_), channel_id=1, source_target_pairs={{0,1},{1,0},{2,3},{3,2},{4,5},{5,4},{6,7},{7,6},{8,9},{9,8},{10,11... | collective-permute-start | bytes 1572872 | tf_op jit(solution)/shard_map/ppermute | solution.py:521
  21.7 8.9 %collective-permute-start.7 = (f32[4,128,128]{2,1,0:T(8,128)S(1)}, f32[4,128,128]{2,1,0:T(8,128)S(1)}, u32[]{:S(2)}, u32[]{:S(2)}) collective-permute-start(f32[4,128,128]{2,1,0:T(8,128)S(1)} %column_second_kernel.1.refs_0_), channel_id=1, source_target_pairs={{0,4},{1,5},{2,6},{3,7},{4,0},{5,1},{6,2},{7,3},{8,12},{9,13},{10,... | collective-permute-start | bytes 786440 | tf_op jit(solution)/shard_map/ppermute | solution.py:521
  23.1 7.7 %collective-permute-start.6 = (f32[4,128,128]{2,1,0:T(8,128)S(1)}, f32[4,128,128]{2,1,0:T(8,128)S(1)}, u32[]{:S(2)}, u32[]{:S(2)}) collective-permute-start(f32[4,128,128]{2,1,0:T(8,128)S(1)} %row_third_kernel.1.refs_0_), channel_id=1, source_target_pairs={{0,2},{1,3},{2,0},{3,1},{4,6},{5,7},{6,4},{7,5},{8,10},{9,11},{10,... | collective-permute-start | bytes 786440 | tf_op jit(solution)/shard_map/ppermute | solution.py:521
  24.9 2.0 %collective-permute-start.8 = (f32[2,4,128,128]{3,2,1,0:T(8,128)S(1)}, f32[2,4,128,128]{3,2,1,0:T(8,128)S(1)}, u32[]{:S(2)}, u32[]{:S(2)}) collective-permute-start(f32[2,4,128,128]{3,2,1,0:T(8,128)S(1)} %get-tuple-element.125), channel_id=1, source_target_pairs={{0,1},{1,0},{2,3},{3,2},{4,5},{5,4},{6,7},{7,6},{8,9},{9,8},{10,11... | collective-permute-start | bytes 1572872 | tf_op jit(solution)/shard_map/ppermute | solution.py:521
  31.0 2.0 %collective-permute-start.9 = (f32[2,4,128,128]{3,2,1,0:T(8,128)S(1)}, f32[2,4,128,128]{3,2,1,0:T(8,128)S(1)}, u32[]{:S(2)}, u32[]{:S(2)}) collective-permute-start(f32[2,4,128,128]{3,2,1,0:T(8,128)S(1)} %get-tuple-element.132), channel_id=1, source_target_pairs={{0,1},{1,0},{2,3},{3,2},{4,5},{5,4},{6,7},{7,6},{8,9},{9,8},{10,11... | collective-permute-start | bytes 1572872 | tf_op jit(solution)/shard_map/ppermute | solution.py:521

commit v8 on v7

--- a/solution.py
+++ b/solution.py
@@ -13,7 +13,7 @@
 COLUMNS = HALF * HEAD_DIM
 GROUP = HALF // 2
 SUB = 256
-PARTIAL = jnp.float32
+PARTIAL = jnp.bfloat16
 
 TN = (((0,), (0,)), ((), ()))
 NT = (((1,), (1,)), ((), ()))

time: 34.9 us -> 34.8 us (level)
  transfers between devices with their start and end apart: 10 -> 10, of which waited for: 2 -> 3; matrix products, arithmetic and copies ran while one was open for 0% -> 0% of each run, Pallas kernels for 57% -> 57%
where the time goes in v8:
time: 34.8 us; the launch traced here: 34.7 us
  Pallas kernels  23.5 us (68%)
  starting transfers between devices  8.88 us (26%)
  waiting for transfers between devices  1.33 us (4%)
  between operations  0.97 us (3%)
    ppermute x10, starting transfers between devices, trade(): return lax.ppermute(value, 'seq', [(i, i ^ distance) for i in range(count)])  8.88 us
    pallas_call x5, Pallas kernels, within(): pl.pallas_call(functools.partial(within_kernel, scale, tuple(pairs)), out...  7.81 us
    pallas_call x3, Pallas kernels, finish(): pl.pallas_call(functools.partial(finish_kernel, scale, square, group, hal...  6.73 us
    pallas_call x1, Pallas kernels, states_second(): pl.pallas_call(functools.partial(states_second_kernel, square), out_shape...  3.39 us
    pallas_call x1, Pallas kernels, states_other(): pl.pallas_call(functools.partial(states_other_kernel, square), out_shape=...  2.54 us
    pallas_call x1, Pallas kernels, states_first(): pl.pallas_call(functools.partial(states_first_kernel, square), out_shape=...  2.06 us
    ppermute x10, waiting for transfers between devices, trade(): return lax.ppermute(value, 'seq', [(i, i ^ distance) for i in range(count)])  1.33 us
    pallas_call x8, Pallas kernels, call(): pl.pallas_call(kernel, out_shape=out, in_specs=[IN_VMEM] * len(operands)...  1 us
  transfers between devices with their start and end apart: 10, of which 3 were waited for; matrix products, arithmetic and copies ran while one was open for 0% of the time, Pallas kernels for 57%

profile of v8, /device:TPU:0, one launch (start us, length us, event | category | flops | bytes accessed | tf_op | source)
XLA Modules:
  0.0 34.7 jit_solution(17377005728234178978)
XLA Ops:
  0.6 2.1 %states_first.1 = (bf16[768,512]{1,0:T(8,128)(2,1)S(1)}, bf16[768,512]{1,0:T(8,128)(2,1)S(1)}, bf16[768,512]{1,0:T(8,128)(2,1)S(1)}, bf16[768,512]{1,0:T(8,128)(...) custom-call(bf16[768,2048]{1,0:T(8,128)(2,1)} %refs_0_.5, ...), custom_call_target="tpu_custom_call" | custom-call | flops 20000000000 | bytes 1000 | tf_op jit(solution)/shard_map/states_first/pallas_call | solution.py:193
  2.7 0.5 %collective-permute-start = (f32[4,128,128]{2,1,0:T(8,128)S(1)}, f32[4,128,128]{2,1,0:T(8,128)S(1)}, u32[]{:S(2)}, u32[]{:S(2)}) collective-permute-start(f32[4,128,128]{2,1,0:T(8,128)S(1)} %get-tuple-element.77.refs_4_), channel_id=1, source_target_pairs={{0,1},{1,0},{2,3},{3,2},{4,5},{5,4},{6,7},{7,6},{8,9},{9,8},{10,11... | collective-permute-start | bytes 786440 | tf_op jit(solution)/shard_map/ppermute | solution.py:521
  3.2 0.4 %states_mine.1 = (f32[4,2,128,128]{3,2,1,0:T(8,128)S(1)}, f32[4,2,128,128]{3,2,1,0:T(8,128)S(1)}, f32[4,128,128]{2,1,0:T(8,128)S(1)}) custom-call(bf16[768,512]{1,0:T(8,128)(2,1)S(1)} %get-tuple-element.73.refs_0_.refs_10_, bf16[768,512]{1,0:T(8,128)(2,1)S(1)} %get-tuple-element.74.refs_1_.refs_11_, bf16[768,512]{1,0:T(8,128)(2,1)S(1)} %get-tuple-element.75.refs_2_.refs_12_, ...), custom_call_target="tpu_custom_call" | custom-call | flops 20000000000 | bytes 1000 | tf_op jit(solution)/shard_map/states_mine/pallas_call | solution.py:65
  3.6 0.7 %collective-permute-done.start_in = f32[4,128,128]{2,1,0:T(8,128)S(1)} collective-permute-done((f32[4,128,128]{2,1,0:T(8,128)S(1)}, f32[4,128,128]{2,1,0:T(8,128)S(1)}, u32[]{:S(2)}, u32[]{:S(2)}) %collective-permute-start) | collective-permute-done | bytes 262176 | tf_op jit(solution)/shard_map/ppermute | solution.py:521
  4.4 3.0 %collective-permute-start.2 = (f32[4,128,128]{2,1,0:T(8,128)S(1)}, f32[4,128,128]{2,1,0:T(8,128)S(1)}, u32[]{:S(2)}, u32[]{:S(2)}) collective-permute-start(f32[4,128,128]{2,1,0:T(8,128)S(1)} %row_first_kernel.1.refs_4_), channel_id=1, source_target_pairs={{0,2},{1,3},{2,0},{3,1},{4,6},{5,7},{6,4},{7,5},{8,10},{9,11},{10,... | collective-permute-start | bytes 786440 | tf_op jit(solution)/shard_map/ppermute | solution.py:521
  7.4 3.4 %states_second.1 = (bf16[768,512]{1,0:T(8,128)(2,1)S(1)}, bf16[768,512]{1,0:T(8,128)(2,1)S(1)}, bf16[768,512]{1,0:T(8,128)(2,1)S(1)}, bf16[768,512]{1,0:T(8,128)...) custom-call(bf16[768,2048]{1,0:T(8,128)(2,1)} %refs_0_.5, ...), custom_call_target="tpu_custom_call" | custom-call | flops 20000000000 | bytes 1000 | tf_op jit(solution)/shard_map/states_second/pallas_call | solution.py:238
  10.8 0.1 collective-permute-start.1
  10.8 1.9 %within.5 = (bf16[768,512]{1,0:T(8,128)(2,1)S(1)}, bf16[768,512]{1,0:T(8,128)(2,1)S(1)}, bf16[768,512]{1,0:T(8,128)(2,1)S(1)}) custom-call(bf16[768,512]{1,0:T(8,128)(2,1)S(1)} %get-tuple-element.82.refs_0_, bf16[768,512]{1,0:T(8,128)(2,1)S(1)} %get-tuple-element.79.refs_1_.refs_0_, bf16[768,512]{1,0:T(8,128)(2,1)S(1)} %get-tuple-element.80.refs_2_.refs_1_, ...), custom_call_target="tpu_custom_call" | custom-call | flops 20000000000 | bytes 1000 | tf_op jit(solution)/shard_map/within/pallas_call | solution.py:292
  12.8 0.0 collective-permute-done.1.rest_in
  12.8 0.2 collective-permute-start.5
  13.0 1.0 %within.6 = (bf16[768,512]{1,0:T(8,128)(2,1)S(1)}, bf16[768,512]{1,0:T(8,128)(2,1)S(1)}, bf16[768,512]{1,0:T(8,128)(2,1)S(1)}) custom-call(bf16[768,512]{1,0:T(8,128)(2,1)S(1)} %get-tuple-element.96.refs_0_, bf16[768,512]{1,0:T(8,128)(2,1)S(1)} %get-tuple-element.97.refs_1_.refs_0_, bf16[768,512]{1,0:T(8,128)(2,1)S(1)} %get-tuple-element.98.refs_2_.refs_1_, ...), custom_call_target="tpu_custom_call" | custom-call | flops 20000000000 | bytes 1000 | tf_op jit(solution)/shard_map/within/pallas_call | solution.py:292
  14.1 0.0 collective-permute-done.2.from_row.row_first
  14.1 0.1 column_first_kernel.1
  14.2 1.9 %collective-permute-start.4 = (f32[4,128,128]{2,1,0:T(8,128)S(1)}, f32[4,128,128]{2,1,0:T(8,128)S(1)}, u32[]{:S(2)}, u32[]{:S(2)}) collective-permute-start(f32[4,128,128]{2,1,0:T(8,128)S(1)} %get-tuple-element.102.refs_17_), channel_id=1, source_target_pairs={{0,4},{1,5},{2,6},{3,7},{4,0},{5,1},{6,2},{7,3},{8,12},{9,13},{10,... | collective-permute-start | bytes 786440 | tf_op jit(solution)/shard_map/ppermute | solution.py:521
  16.0 2.5 %states_other.1 = (bf16[768,512]{1,0:T(8,128)(2,1)S(1)}, bf16[768,512]{1,0:T(8,128)(2,1)S(1)}, bf16[768,512]{1,0:T(8,128)(2,1)S(1)}, bf16[768,512]{1,0:T(8,128)(...) custom-call(bf16[768,2048]{1,0:T(8,128)(2,1)} %refs_0_.5, ...), custom_call_target="tpu_custom_call", output_to_operand_aliasing={{0}: (4, {}), {1}: (5, {}), {2}: (6, {}), {3}: (7, {}), {4}... | custom-call | flops 20000000000 | bytes 1000 | tf_op jit(solution)/shard_map/states_other/pallas_call | solution.py:272
  18.6 0.1 collective-permute-start.3
  18.7 1.0 %within.7 = (bf16[768,512]{1,0:T(8,128)(2,1)S(1)}, bf16[768,512]{1,0:T(8,128)(2,1)S(1)}, bf16[768,512]{1,0:T(8,128)(2,1)S(1)}) custom-call(bf16[768,512]{1,0:T(8,128)(2,1)S(1)} %get-tuple-element.96.refs_0_, bf16[768,512]{1,0:T(8,128)(2,1)S(1)} %get-tuple-element.97.refs_1_.refs_0_, ...), custom_call_target="tpu_custom_call", output_to_operand_aliasing={{0}: (4, {}), {1}: (5, {}), {2}: (6, {})} | custom-call | flops 20000000000 | bytes 1000 | tf_op jit(solution)/shard_map/within/pallas_call | solution.py:292
  19.7 1.9 %within.8 = (bf16[768,512]{1,0:T(8,128)(2,1)S(1)}, bf16[768,512]{1,0:T(8,128)(2,1)S(1)}, bf16[768,512]{1,0:T(8,128)(2,1)S(1)}) custom-call(bf16[768,512]{1,0:T(8,128)(2,1)S(1)} %get-tuple-element.105.refs_0_, bf16[768,512]{1,0:T(8,128)(2,1)S(1)} %get-tuple-element.106.refs_1_.refs_9_, bf16[768,512]{1,0:T(8,128)(2,1)S(1)} %get-tuple-element.107.refs_2_.refs_10_, ...), custom_call_target="tpu_custom_call" | custom-call | flops 20000000000 | bytes 1000 | tf_op jit(solution)/shard_map/within/pallas_call | solution.py:292
  21.6 0.0 collective-permute-done.5.from_row.row_second
  21.7 1.4 %collective-permute-start.7 = (f32[4,128,128]{2,1,0:T(8,128)S(1)}, f32[4,128,128]{2,1,0:T(8,128)S(1)}, u32[]{:S(2)}, u32[]{:S(2)}) collective-permute-start(f32[4,128,128]{2,1,0:T(8,128)S(1)} %column_second_kernel.1.refs_0_), channel_id=1, source_target_pairs={{0,4},{1,5},{2,6},{3,7},{4,0},{5,1},{6,2},{7,3},{8,12},{9,13},{10,... | collective-permute-start | bytes 786440 | tf_op jit(solution)/shard_map/ppermute | solution.py:521
  23.1 0.0 collective-permute-done.4.from_column.column_first
  23.1 0.0 collective-permute-done.3.later_in.refs_24_
  23.1 1.6 %collective-permute-start.6 = (f32[4,128,128]{2,1,0:T(8,128)S(1)}, f32[4,128,128]{2,1,0:T(8,128)S(1)}, u32[]{:S(2)}, u32[]{:S(2)}) collective-permute-start(f32[4,128,128]{2,1,0:T(8,128)S(1)} %row_third_kernel.1.refs_0_), channel_id=1, source_target_pairs={{0,2},{1,3},{2,0},{3,1},{4,6},{5,7},{6,4},{7,5},{8,10},{9,11},{10,... | collective-permute-start | bytes 786440 | tf_op jit(solution)/shard_map/ppermute | solution.py:521
  24.7 0.2 first_states_kernel.1
  24.9 0.1 collective-permute-start.8
  24.9 1.9 %within.9 = (bf16[768,512]{1,0:T(8,128)(2,1)S(1)}, bf16[768,512]{1,0:T(8,128)(2,1)S(1)}, bf16[768,512]{1,0:T(8,128)(2,1)S(1)}) custom-call(bf16[768,512]{1,0:T(8,128)(2,1)S(1)} %get-tuple-element.116.refs_0_, bf16[768,512]{1,0:T(8,128)(2,1)S(1)} %get-tuple-element.113.refs_1_.refs_0_, bf16[768,512]{1,0:T(8,128)(2,1)S(1)} %get-tuple-element.114.refs_2_.refs_1_, ...), custom_call_target="tpu_custom_call" | custom-call | flops 20000000000 | bytes 1000 | tf_op jit(solution)/shard_map/within/pallas_call | solution.py:292
  26.9 0.0 collective-permute-done.8.refs_15_
  26.9 3.5 %finish.3 = (bf16[768,2048]{1,0:T(8,128)(2,1)}, bf16[768,2048]{1,0:T(8,128)(2,1)}, bf16[768,2048]{1,0:T(8,128)(2,1)}) custom-call(bf16[768,512]{1,0:T(8,128)(2,1)S(1)} %get-tuple-element.113.refs_1_.refs_0_, bf16[768,512]{1,0:T(8,128)(2,1)S(1)} %get-tuple-element.114.refs_2_.refs_1_, bf16[768,512]{1,0:T(8,128)(2,1)S(1)} %get-tuple-element.115.refs_3_.refs_2_, ...), custom_call_target="tpu_custom_call" | custom-call | flops 20000000000 | bytes 1000 | tf_op jit(solution)/shard_map/finish/pallas_call | solution.py:498
  30.4 0.0 collective-permute-done.7.column_second
  30.5 0.3 collective-permute-done.6.row_third
  30.8 0.2 second_states_kernel.1
  31.0 0.2 collective-permute-start.9
  31.2 1.6 %finish.4 = (bf16[768,2048]{1,0:T(8,128)(2,1)}, bf16[768,2048]{1,0:T(8,128)(2,1)}, bf16[768,2048]{1,0:T(8,128)(2,1)}) custom-call(bf16[768,512]{1,0:T(8,128)(2,1)S(1)} %get-tuple-element.97.refs_1_.refs_0_, bf16[768,512]{1,0:T(8,128)(2,1)S(1)} %get-tuple-element.98.refs_2_.refs_1_, ...), custom_call_target="tpu_custom_call", output_to_operand_aliasing={{0}: (9, {}), {1}: (10, {}), {2}: (11, {})} | custom-call | flops 20000000000 | bytes 1000 | tf_op jit(solution)/shard_map/finish/pallas_call | solution.py:498
  32.8 0.2 collective-permute-done.9.refs_6_
  33.0 1.6 %finish.5 = (bf16[768,2048]{1,0:T(8,128)(2,1)}, bf16[768,2048]{1,0:T(8,128)(2,1)}, bf16[768,2048]{1,0:T(8,128)(2,1)}) custom-call(bf16[768,512]{1,0:T(8,128)(2,1)S(1)} %get-tuple-element.79.refs_1_.refs_0_, bf16[768,512]{1,0:T(8,128)(2,1)S(1)} %get-tuple-element.80.refs_2_.refs_1_, ...), custom_call_target="tpu_custom_call", output_to_operand_aliasing={{0}: (9, {}), {1}: (10, {}), {2}: (11, {})} | custom-call | flops 20000000000 | bytes 1000 | tf_op jit(solution)/shard_map/finish/pallas_call | solution.py:498
  (4 shorter events, 0.2 us)
Async XLA Ops:
  2.7 1.7 %collective-permute-start = (f32[4,128,128]{2,1,0:T(8,128)S(1)}, f32[4,128,128]{2,1,0:T(8,128)S(1)}, u32[]{:S(2)}, u32[]{:S(2)}) collective-permute-start(f32[4,128,128]{2,1,0:T(8,128)S(1)} %get-tuple-element.77.refs_4_), channel_id=1, source_target_pairs={{0,1},{1,0},{2,3},{3,2},{4,5},{5,4},{6,7},{7,6},{8,9},{9,8},{10,11... | collective-permute-start | bytes 786440 | tf_op jit(solution)/shard_map/ppermute | solution.py:521
  4.4 9.7 %collective-permute-start.2 = (f32[4,128,128]{2,1,0:T(8,128)S(1)}, f32[4,128,128]{2,1,0:T(8,128)S(1)}, u32[]{:S(2)}, u32[]{:S(2)}) collective-permute-start(f32[4,128,128]{2,1,0:T(8,128)S(1)} %row_first_kernel.1.refs_4_), channel_id=1, source_target_pairs={{0,2},{1,3},{2,0},{3,1},{4,6},{5,7},{6,4},{7,5},{8,10},{9,11},{10,... | collective-permute-start | bytes 786440 | tf_op jit(solution)/shard_map/ppermute | solution.py:521
  10.8 2.0 %collective-permute-start.1 = (f32[2,4,128,128]{3,2,1,0:T(8,128)S(1)}, f32[2,4,128,128]{3,2,1,0:T(8,128)S(1)}, u32[]{:S(2)}, u32[]{:S(2)}) collective-permute-start(f32[2,4,128,128]{3,2,1,0:T(8,128)S(1)} %get-tuple-element.83.refs_4_), channel_id=1, source_target_pairs={{0,1},{1,0},{2,3},{3,2},{4,5},{5,4},{6,7},{7,6},{8,9},{9,8},{10,11... | collective-permute-start | bytes 1572872 | tf_op jit(solution)/shard_map/ppermute | solution.py:521
  12.8 8.8 %collective-permute-start.5 = (f32[4,128,128]{2,1,0:T(8,128)S(1)}, f32[4,128,128]{2,1,0:T(8,128)S(1)}, u32[]{:S(2)}, u32[]{:S(2)}) collective-permute-start(f32[4,128,128]{2,1,0:T(8,128)S(1)} %row_second_kernel.1.refs_4_), channel_id=1, source_target_pairs={{0,2},{1,3},{2,0},{3,1},{4,6},{5,7},{6,4},{7,5},{8,10},{9,11},{10,... | collective-permute-start | bytes 786440 | tf_op jit(solution)/shard_map/ppermute | solution.py:521
  14.2 8.9 %collective-permute-start.4 = (f32[4,128,128]{2,1,0:T(8,128)S(1)}, f32[4,128,128]{2,1,0:T(8,128)S(1)}, u32[]{:S(2)}, u32[]{:S(2)}) collective-permute-start(f32[4,128,128]{2,1,0:T(8,128)S(1)} %get-tuple-element.102.refs_17_), channel_id=1, source_target_pairs={{0,4},{1,5},{2,6},{3,7},{4,0},{5,1},{6,2},{7,3},{8,12},{9,13},{10,... | collective-permute-start | bytes 786440 | tf_op jit(solution)/shard_map/ppermute | solution.py:521
  18.6 4.5 %collective-permute-start.3 = (f32[2,4,128,128]{3,2,1,0:T(8,128)S(1)}, f32[2,4,128,128]{3,2,1,0:T(8,128)S(1)}, u32[]{:S(2)}, u32[]{:S(2)}) collective-permute-start(f32[2,4,128,128]{3,2,1,0:T(8,128)S(1)} %get-tuple-element.104.refs_7_), channel_id=1, source_target_pairs={{0,1},{1,0},{2,3},{3,2},{4,5},{5,4},{6,7},{7,6},{8,9},{9,8},{10,11... | collective-permute-start | bytes 1572872 | tf_op jit(solution)/shard_map/ppermute | solution.py:521
  21.7 8.8 %collective-permute-start.7 = (f32[4,128,128]{2,1,0:T(8,128)S(1)}, f32[4,128,128]{2,1,0:T(8,128)S(1)}, u32[]{:S(2)}, u32[]{:S(2)}) collective-permute-start(f32[4,128,128]{2,1,0:T(8,128)S(1)} %column_second_kernel.1.refs_0_), channel_id=1, source_target_pairs={{0,4},{1,5},{2,6},{3,7},{4,0},{5,1},{6,2},{7,3},{8,12},{9,13},{10,... | collective-permute-start | bytes 786440 | tf_op jit(solution)/shard_map/ppermute | solution.py:521
  23.1 7.7 %collective-permute-start.6 = (f32[4,128,128]{2,1,0:T(8,128)S(1)}, f32[4,128,128]{2,1,0:T(8,128)S(1)}, u32[]{:S(2)}, u32[]{:S(2)}) collective-permute-start(f32[4,128,128]{2,1,0:T(8,128)S(1)} %row_third_kernel.1.refs_0_), channel_id=1, source_target_pairs={{0,2},{1,3},{2,0},{3,1},{4,6},{5,7},{6,4},{7,5},{8,10},{9,11},{10,... | collective-permute-start | bytes 786440 | tf_op jit(solution)/shard_map/ppermute | solution.py:521
  24.9 2.0 %collective-permute-start.8 = (f32[2,4,128,128]{3,2,1,0:T(8,128)S(1)}, f32[2,4,128,128]{3,2,1,0:T(8,128)S(1)}, u32[]{:S(2)}, u32[]{:S(2)}) collective-permute-start(f32[2,4,128,128]{3,2,1,0:T(8,128)S(1)} %get-tuple-element.125), channel_id=1, source_target_pairs={{0,1},{1,0},{2,3},{3,2},{4,5},{5,4},{6,7},{7,6},{8,9},{9,8},{10,11... | collective-permute-start | bytes 1572872 | tf_op jit(solution)/shard_map/ppermute | solution.py:521
  31.0 2.0 %collective-permute-start.9 = (f32[2,4,128,128]{3,2,1,0:T(8,128)S(1)}, f32[2,4,128,128]{3,2,1,0:T(8,128)S(1)}, u32[]{:S(2)}, u32[]{:S(2)}) collective-permute-start(f32[2,4,128,128]{3,2,1,0:T(8,128)S(1)} %get-tuple-element.132), channel_id=1, source_target_pairs={{0,1},{1,0},{2,3},{3,2},{4,5},{5,4},{6,7},{7,6},{8,9},{9,8},{10,11... | collective-permute-start | bytes 1572872 | tf_op jit(solution)/shard_map/ppermute | solution.py:521

commit v9 on v8

--- a/solution.py
+++ b/solution.py
@@ -447,6 +447,18 @@
         return [copies_of(i, number, which, 2 * which, 2) for which in range(GROUP // 2)]
 
     sometimes, always = [], []
+    rest = refs[9 * len(halves) :]
+    for n in range(ahead):
+        number = len(halves) + n
+        o, dq, prefix, early = rest[4 * n : 4 * n + 4]
+        prefix = prefix if n == 0 else prefix.at[1]
+        query = pieces(0, number)
+        sometimes += query
+
+        @pl.when(row == 0)
+        def _():
+            run(0, number, query, dq, o, prefix, early, QUERY)
+
     for number in range(len(halves)):
         k, v, o, dq, dk, dv, state, early, late = refs[9 * number : 9 * number + 9]
         query = pieces(0, number)
@@ -463,18 +475,6 @@
             copies = pieces(i, number)
             always += copies
             run(i, number, copies, *arguments)
-    rest = refs[9 * len(halves) :]
-    for n in range(ahead):
-        number = len(halves) + n
-        o, dq, prefix, early = rest[4 * n : 4 * n + 4]
-        prefix = prefix if n == 0 else prefix.at[1]
-        query = pieces(0, number)
-        sometimes += query
-
-        @pl.when(row == 0)
-        def _():
-            run(0, number, query, dq, o, prefix, early, QUERY)
-
     for copy in always:
         copy.wait()
     if sometimes:

time: 34.8 us -> 34.8 us (level)
  transfers between devices with their start and end apart: 10 -> 10, of which waited for: 3 -> 2; matrix products, arithmetic and copies ran while one was open for 0% -> 0% of each run, Pallas kernels for 57% -> 57%
where the time goes in v9:
time: 34.8 us; the launch traced here: 34.7 us
  Pallas kernels  23.6 us (68%)
  starting transfers between devices  9.01 us (26%)
  waiting for transfers between devices  1.07 us (3%)
  between operations  0.98 us (3%)
    ppermute x10, starting transfers between devices, trade(): return lax.ppermute(value, 'seq', [(i, i ^ distance) for i in range(count)])  9.01 us
    pallas_call x5, Pallas kernels, within(): pl.pallas_call(functools.partial(within_kernel, scale, tuple(pairs)), out...  7.81 us
    pallas_call x3, Pallas kernels, finish(): pl.pallas_call(functools.partial(finish_kernel, scale, square, group, hal...  6.85 us
    pallas_call x1, Pallas kernels, states_second(): pl.pallas_call(functools.partial(states_second_kernel, square), out_shape...  3.39 us
    pallas_call x1, Pallas kernels, states_other(): pl.pallas_call(functools.partial(states_other_kernel, square), out_shape=...  2.54 us
    pallas_call x1, Pallas kernels, states_first(): pl.pallas_call(functools.partial(states_first_kernel, square), out_shape=...  2.06 us
    ppermute x10, waiting for transfers between devices, trade(): return lax.ppermute(value, 'seq', [(i, i ^ distance) for i in range(count)])  1.07 us
    pallas_call x8, Pallas kernels, call(): pl.pallas_call(kernel, out_shape=out, in_specs=[IN_VMEM] * len(operands)...  1 us
  transfers between devices with their start and end apart: 10, of which 2 were waited for; matrix products, arithmetic and copies ran while one was open for 0% of the time, Pallas kernels for 57%

profile of v9, /device:TPU:0, one launch (start us, length us, event | category | flops | bytes accessed | tf_op | source)
XLA Modules:
  0.0 34.7 jit_solution(5218848613490800235)
XLA Ops:
  0.6 2.1 %states_first.1 = (bf16[768,512]{1,0:T(8,128)(2,1)S(1)}, bf16[768,512]{1,0:T(8,128)(2,1)S(1)}, bf16[768,512]{1,0:T(8,128)(2,1)S(1)}, bf16[768,512]{1,0:T(8,128)(...) custom-call(bf16[768,2048]{1,0:T(8,128)(2,1)} %refs_0_.5, ...), custom_call_target="tpu_custom_call" | custom-call | flops 20000000000 | bytes 1000 | tf_op jit(solution)/shard_map/states_first/pallas_call | solution.py:193
  2.7 0.5 %collective-permute-start = (f32[4,128,128]{2,1,0:T(8,128)S(1)}, f32[4,128,128]{2,1,0:T(8,128)S(1)}, u32[]{:S(2)}, u32[]{:S(2)}) collective-permute-start(f32[4,128,128]{2,1,0:T(8,128)S(1)} %get-tuple-element.77.refs_4_), channel_id=1, source_target_pairs={{0,1},{1,0},{2,3},{3,2},{4,5},{5,4},{6,7},{7,6},{8,9},{9,8},{10,11... | collective-permute-start | bytes 786440 | tf_op jit(solution)/shard_map/ppermute | solution.py:521
  3.2 0.4 %states_mine.1 = (f32[4,2,128,128]{3,2,1,0:T(8,128)S(1)}, f32[4,2,128,128]{3,2,1,0:T(8,128)S(1)}, f32[4,128,128]{2,1,0:T(8,128)S(1)}) custom-call(bf16[768,512]{1,0:T(8,128)(2,1)S(1)} %get-tuple-element.73.refs_0_.refs_10_, bf16[768,512]{1,0:T(8,128)(2,1)S(1)} %get-tuple-element.74.refs_1_.refs_11_, bf16[768,512]{1,0:T(8,128)(2,1)S(1)} %get-tuple-element.75.refs_2_.refs_12_, ...), custom_call_target="tpu_custom_call" | custom-call | flops 20000000000 | bytes 1000 | tf_op jit(solution)/shard_map/states_mine/pallas_call | solution.py:65
  3.6 0.7 %collective-permute-done.start_in = f32[4,128,128]{2,1,0:T(8,128)S(1)} collective-permute-done((f32[4,128,128]{2,1,0:T(8,128)S(1)}, f32[4,128,128]{2,1,0:T(8,128)S(1)}, u32[]{:S(2)}, u32[]{:S(2)}) %collective-permute-start) | collective-permute-done | bytes 262176 | tf_op jit(solution)/shard_map/ppermute | solution.py:521
  4.4 3.0 %collective-permute-start.2 = (f32[4,128,128]{2,1,0:T(8,128)S(1)}, f32[4,128,128]{2,1,0:T(8,128)S(1)}, u32[]{:S(2)}, u32[]{:S(2)}) collective-permute-start(f32[4,128,128]{2,1,0:T(8,128)S(1)} %row_first_kernel.1.refs_4_), channel_id=1, source_target_pairs={{0,2},{1,3},{2,0},{3,1},{4,6},{5,7},{6,4},{7,5},{8,10},{9,11},{10,... | collective-permute-start | bytes 786440 | tf_op jit(solution)/shard_map/ppermute | solution.py:521
  7.4 3.4 %states_second.1 = (bf16[768,512]{1,0:T(8,128)(2,1)S(1)}, bf16[768,512]{1,0:T(8,128)(2,1)S(1)}, bf16[768,512]{1,0:T(8,128)(2,1)S(1)}, bf16[768,512]{1,0:T(8,128)...) custom-call(bf16[768,2048]{1,0:T(8,128)(2,1)} %refs_0_.5, ...), custom_call_target="tpu_custom_call" | custom-call | flops 20000000000 | bytes 1000 | tf_op jit(solution)/shard_map/states_second/pallas_call | solution.py:238
  10.8 0.1 collective-permute-start.1
  10.8 1.9 %within.5 = (bf16[768,512]{1,0:T(8,128)(2,1)S(1)}, bf16[768,512]{1,0:T(8,128)(2,1)S(1)}, bf16[768,512]{1,0:T(8,128)(2,1)S(1)}) custom-call(bf16[768,512]{1,0:T(8,128)(2,1)S(1)} %get-tuple-element.82.refs_0_, bf16[768,512]{1,0:T(8,128)(2,1)S(1)} %get-tuple-element.79.refs_1_.refs_0_, bf16[768,512]{1,0:T(8,128)(2,1)S(1)} %get-tuple-element.80.refs_2_.refs_1_, ...), custom_call_target="tpu_custom_call" | custom-call | flops 20000000000 | bytes 1000 | tf_op jit(solution)/shard_map/within/pallas_call | solution.py:292
  12.8 0.0 collective-permute-done.1.rest_in
  12.8 0.2 collective-permute-start.5
  13.0 1.0 %within.6 = (bf16[768,512]{1,0:T(8,128)(2,1)S(1)}, bf16[768,512]{1,0:T(8,128)(2,1)S(1)}, bf16[768,512]{1,0:T(8,128)(2,1)S(1)}) custom-call(bf16[768,512]{1,0:T(8,128)(2,1)S(1)} %get-tuple-element.96.refs_0_, bf16[768,512]{1,0:T(8,128)(2,1)S(1)} %get-tuple-element.97.refs_1_.refs_0_, bf16[768,512]{1,0:T(8,128)(2,1)S(1)} %get-tuple-element.98.refs_2_.refs_1_, ...), custom_call_target="tpu_custom_call" | custom-call | flops 20000000000 | bytes 1000 | tf_op jit(solution)/shard_map/within/pallas_call | solution.py:292
  14.1 0.0 collective-permute-done.2.from_row.row_first
  14.1 0.1 column_first_kernel.1
  14.2 1.9 %collective-permute-start.4 = (f32[4,128,128]{2,1,0:T(8,128)S(1)}, f32[4,128,128]{2,1,0:T(8,128)S(1)}, u32[]{:S(2)}, u32[]{:S(2)}) collective-permute-start(f32[4,128,128]{2,1,0:T(8,128)S(1)} %get-tuple-element.102.refs_17_), channel_id=1, source_target_pairs={{0,4},{1,5},{2,6},{3,7},{4,0},{5,1},{6,2},{7,3},{8,12},{9,13},{10,... | collective-permute-start | bytes 786440 | tf_op jit(solution)/shard_map/ppermute | solution.py:521
  16.0 2.5 %states_other.1 = (bf16[768,512]{1,0:T(8,128)(2,1)S(1)}, bf16[768,512]{1,0:T(8,128)(2,1)S(1)}, bf16[768,512]{1,0:T(8,128)(2,1)S(1)}, bf16[768,512]{1,0:T(8,128)(...) custom-call(bf16[768,2048]{1,0:T(8,128)(2,1)} %refs_0_.5, ...), custom_call_target="tpu_custom_call", output_to_operand_aliasing={{0}: (4, {}), {1}: (5, {}), {2}: (6, {}), {3}: (7, {}), {4}... | custom-call | flops 20000000000 | bytes 1000 | tf_op jit(solution)/shard_map/states_other/pallas_call | solution.py:272
  18.6 0.1 collective-permute-start.3
  18.7 1.0 %within.7 = (bf16[768,512]{1,0:T(8,128)(2,1)S(1)}, bf16[768,512]{1,0:T(8,128)(2,1)S(1)}, bf16[768,512]{1,0:T(8,128)(2,1)S(1)}) custom-call(bf16[768,512]{1,0:T(8,128)(2,1)S(1)} %get-tuple-element.96.refs_0_, bf16[768,512]{1,0:T(8,128)(2,1)S(1)} %get-tuple-element.97.refs_1_.refs_0_, ...), custom_call_target="tpu_custom_call", output_to_operand_aliasing={{0}: (4, {}), {1}: (5, {}), {2}: (6, {})} | custom-call | flops 20000000000 | bytes 1000 | tf_op jit(solution)/shard_map/within/pallas_call | solution.py:292
  19.7 1.9 %within.8 = (bf16[768,512]{1,0:T(8,128)(2,1)S(1)}, bf16[768,512]{1,0:T(8,128)(2,1)S(1)}, bf16[768,512]{1,0:T(8,128)(2,1)S(1)}) custom-call(bf16[768,512]{1,0:T(8,128)(2,1)S(1)} %get-tuple-element.105.refs_0_, bf16[768,512]{1,0:T(8,128)(2,1)S(1)} %get-tuple-element.106.refs_1_.refs_9_, bf16[768,512]{1,0:T(8,128)(2,1)S(1)} %get-tuple-element.107.refs_2_.refs_10_, ...), custom_call_target="tpu_custom_call" | custom-call | flops 20000000000 | bytes 1000 | tf_op jit(solution)/shard_map/within/pallas_call | solution.py:292
  21.6 0.0 collective-permute-done.5.from_row.row_second
  21.7 1.4 %collective-permute-start.7 = (f32[4,128,128]{2,1,0:T(8,128)S(1)}, f32[4,128,128]{2,1,0:T(8,128)S(1)}, u32[]{:S(2)}, u32[]{:S(2)}) collective-permute-start(f32[4,128,128]{2,1,0:T(8,128)S(1)} %column_second_kernel.1.refs_0_), channel_id=1, source_target_pairs={{0,4},{1,5},{2,6},{3,7},{4,0},{5,1},{6,2},{7,3},{8,12},{9,13},{10,... | collective-permute-start | bytes 786440 | tf_op jit(solution)/shard_map/ppermute | solution.py:521
  23.1 0.0 collective-permute-done.4.from_column.column_first
  23.1 0.0 collective-permute-done.3.later_in.refs_24_
  23.1 1.6 %collective-permute-start.6 = (f32[4,128,128]{2,1,0:T(8,128)S(1)}, f32[4,128,128]{2,1,0:T(8,128)S(1)}, u32[]{:S(2)}, u32[]{:S(2)}) collective-permute-start(f32[4,128,128]{2,1,0:T(8,128)S(1)} %row_third_kernel.1.refs_0_), channel_id=1, source_target_pairs={{0,2},{1,3},{2,0},{3,1},{4,6},{5,7},{6,4},{7,5},{8,10},{9,11},{10,... | collective-permute-start | bytes 786440 | tf_op jit(solution)/shard_map/ppermute | solution.py:521
  24.7 0.2 first_states_kernel.1
  24.9 0.1 collective-permute-start.8
  24.9 1.9 %within.9 = (bf16[768,512]{1,0:T(8,128)(2,1)S(1)}, bf16[768,512]{1,0:T(8,128)(2,1)S(1)}, bf16[768,512]{1,0:T(8,128)(2,1)S(1)}) custom-call(bf16[768,512]{1,0:T(8,128)(2,1)S(1)} %get-tuple-element.116.refs_0_, bf16[768,512]{1,0:T(8,128)(2,1)S(1)} %get-tuple-element.113.refs_1_.refs_0_, bf16[768,512]{1,0:T(8,128)(2,1)S(1)} %get-tuple-element.114.refs_2_.refs_1_, ...), custom_call_target="tpu_custom_call" | custom-call | flops 20000000000 | bytes 1000 | tf_op jit(solution)/shard_map/within/pallas_call | solution.py:292
  26.9 0.0 collective-permute-done.8.refs_15_
  26.9 3.7 %finish.3 = (bf16[768,2048]{1,0:T(8,128)(2,1)}, bf16[768,2048]{1,0:T(8,128)(2,1)}, bf16[768,2048]{1,0:T(8,128)(2,1)}) custom-call(bf16[768,512]{1,0:T(8,128)(2,1)S(1)} %get-tuple-element.113.refs_1_.refs_0_, bf16[768,512]{1,0:T(8,128)(2,1)S(1)} %get-tuple-element.114.refs_2_.refs_1_, bf16[768,512]{1,0:T(8,128)(2,1)S(1)} %get-tuple-element.115.refs_3_.refs_2_, ...), custom_call_target="tpu_custom_call" | custom-call | flops 20000000000 | bytes 1000 | tf_op jit(solution)/shard_map/finish/pallas_call | solution.py:498
  30.5 0.0 collective-permute-done.7.column_second
  30.6 0.3 collective-permute-done.6.row_third
  30.8 0.2 second_states_kernel.1
  31.0 0.3 collective-permute-start.9
  31.3 1.6 %finish.4 = (bf16[768,2048]{1,0:T(8,128)(2,1)}, bf16[768,2048]{1,0:T(8,128)(2,1)}, bf16[768,2048]{1,0:T(8,128)(2,1)}) custom-call(bf16[768,512]{1,0:T(8,128)(2,1)S(1)} %get-tuple-element.97.refs_1_.refs_0_, bf16[768,512]{1,0:T(8,128)(2,1)S(1)} %get-tuple-element.98.refs_2_.refs_1_, ...), custom_call_target="tpu_custom_call", output_to_operand_aliasing={{0}: (9, {}), {1}: (10, {}), {2}: (11, {})} | custom-call | flops 20000000000 | bytes 1000 | tf_op jit(solution)/shard_map/finish/pallas_call | solution.py:498
  32.9 0.0 collective-permute-done.9.refs_6_
  33.0 1.6 %finish.5 = (bf16[768,2048]{1,0:T(8,128)(2,1)}, bf16[768,2048]{1,0:T(8,128)(2,1)}, bf16[768,2048]{1,0:T(8,128)(2,1)}) custom-call(bf16[768,512]{1,0:T(8,128)(2,1)S(1)} %get-tuple-element.79.refs_1_.refs_0_, bf16[768,512]{1,0:T(8,128)(2,1)S(1)} %get-tuple-element.80.refs_2_.refs_1_, ...), custom_call_target="tpu_custom_call", output_to_operand_aliasing={{0}: (9, {}), {1}: (10, {}), {2}: (11, {})} | custom-call | flops 20000000000 | bytes 1000 | tf_op jit(solution)/shard_map/finish/pallas_call | solution.py:498
  (4 shorter events, 0.2 us)
Async XLA Ops:
  2.7 1.7 %collective-permute-start = (f32[4,128,128]{2,1,0:T(8,128)S(1)}, f32[4,128,128]{2,1,0:T(8,128)S(1)}, u32[]{:S(2)}, u32[]{:S(2)}) collective-permute-start(f32[4,128,128]{2,1,0:T(8,128)S(1)} %get-tuple-element.77.refs_4_), channel_id=1, source_target_pairs={{0,1},{1,0},{2,3},{3,2},{4,5},{5,4},{6,7},{7,6},{8,9},{9,8},{10,11... | collective-permute-start | bytes 786440 | tf_op jit(solution)/shard_map/ppermute | solution.py:521
  4.4 9.7 %collective-permute-start.2 = (f32[4,128,128]{2,1,0:T(8,128)S(1)}, f32[4,128,128]{2,1,0:T(8,128)S(1)}, u32[]{:S(2)}, u32[]{:S(2)}) collective-permute-start(f32[4,128,128]{2,1,0:T(8,128)S(1)} %row_first_kernel.1.refs_4_), channel_id=1, source_target_pairs={{0,2},{1,3},{2,0},{3,1},{4,6},{5,7},{6,4},{7,5},{8,10},{9,11},{10,... | collective-permute-start | bytes 786440 | tf_op jit(solution)/shard_map/ppermute | solution.py:521
  10.8 2.0 %collective-permute-start.1 = (f32[2,4,128,128]{3,2,1,0:T(8,128)S(1)}, f32[2,4,128,128]{3,2,1,0:T(8,128)S(1)}, u32[]{:S(2)}, u32[]{:S(2)}) collective-permute-start(f32[2,4,128,128]{3,2,1,0:T(8,128)S(1)} %get-tuple-element.83.refs_4_), channel_id=1, source_target_pairs={{0,1},{1,0},{2,3},{3,2},{4,5},{5,4},{6,7},{7,6},{8,9},{9,8},{10,11... | collective-permute-start | bytes 1572872 | tf_op jit(solution)/shard_map/ppermute | solution.py:521
  12.8 8.8 %collective-permute-start.5 = (f32[4,128,128]{2,1,0:T(8,128)S(1)}, f32[4,128,128]{2,1,0:T(8,128)S(1)}, u32[]{:S(2)}, u32[]{:S(2)}) collective-permute-start(f32[4,128,128]{2,1,0:T(8,128)S(1)} %row_second_kernel.1.refs_4_), channel_id=1, source_target_pairs={{0,2},{1,3},{2,0},{3,1},{4,6},{5,7},{6,4},{7,5},{8,10},{9,11},{10,... | collective-permute-start | bytes 786440 | tf_op jit(solution)/shard_map/ppermute | solution.py:521
  14.2 8.9 %collective-permute-start.4 = (f32[4,128,128]{2,1,0:T(8,128)S(1)}, f32[4,128,128]{2,1,0:T(8,128)S(1)}, u32[]{:S(2)}, u32[]{:S(2)}) collective-permute-start(f32[4,128,128]{2,1,0:T(8,128)S(1)} %get-tuple-element.102.refs_17_), channel_id=1, source_target_pairs={{0,4},{1,5},{2,6},{3,7},{4,0},{5,1},{6,2},{7,3},{8,12},{9,13},{10,... | collective-permute-start | bytes 786440 | tf_op jit(solution)/shard_map/ppermute | solution.py:521
  18.6 4.5 %collective-permute-start.3 = (f32[2,4,128,128]{3,2,1,0:T(8,128)S(1)}, f32[2,4,128,128]{3,2,1,0:T(8,128)S(1)}, u32[]{:S(2)}, u32[]{:S(2)}) collective-permute-start(f32[2,4,128,128]{3,2,1,0:T(8,128)S(1)} %get-tuple-element.104.refs_7_), channel_id=1, source_target_pairs={{0,1},{1,0},{2,3},{3,2},{4,5},{5,4},{6,7},{7,6},{8,9},{9,8},{10,11... | collective-permute-start | bytes 1572872 | tf_op jit(solution)/shard_map/ppermute | solution.py:521
  21.7 8.8 %collective-permute-start.7 = (f32[4,128,128]{2,1,0:T(8,128)S(1)}, f32[4,128,128]{2,1,0:T(8,128)S(1)}, u32[]{:S(2)}, u32[]{:S(2)}) collective-permute-start(f32[4,128,128]{2,1,0:T(8,128)S(1)} %column_second_kernel.1.refs_0_), channel_id=1, source_target_pairs={{0,4},{1,5},{2,6},{3,7},{4,0},{5,1},{6,2},{7,3},{8,12},{9,13},{10,... | collective-permute-start | bytes 786440 | tf_op jit(solution)/shard_map/ppermute | solution.py:521
  23.1 7.7 %collective-permute-start.6 = (f32[4,128,128]{2,1,0:T(8,128)S(1)}, f32[4,128,128]{2,1,0:T(8,128)S(1)}, u32[]{:S(2)}, u32[]{:S(2)}) collective-permute-start(f32[4,128,128]{2,1,0:T(8,128)S(1)} %row_third_kernel.1.refs_0_), channel_id=1, source_target_pairs={{0,2},{1,3},{2,0},{3,1},{4,6},{5,7},{6,4},{7,5},{8,10},{9,11},{10,... | collective-permute-start | bytes 786440 | tf_op jit(solution)/shard_map/ppermute | solution.py:521
  24.9 2.0 %collective-permute-start.8 = (f32[2,4,128,128]{3,2,1,0:T(8,128)S(1)}, f32[2,4,128,128]{3,2,1,0:T(8,128)S(1)}, u32[]{:S(2)}, u32[]{:S(2)}) collective-permute-start(f32[2,4,128,128]{3,2,1,0:T(8,128)S(1)} %get-tuple-element.125), channel_id=1, source_target_pairs={{0,1},{1,0},{2,3},{3,2},{4,5},{5,4},{6,7},{7,6},{8,9},{9,8},{10,11... | collective-permute-start | bytes 1572872 | tf_op jit(solution)/shard_map/ppermute | solution.py:521
  31.0 2.0 %collective-permute-start.9 = (f32[2,4,128,128]{3,2,1,0:T(8,128)S(1)}, f32[2,4,128,128]{3,2,1,0:T(8,128)S(1)}, u32[]{:S(2)}, u32[]{:S(2)}) collective-permute-start(f32[2,4,128,128]{3,2,1,0:T(8,128)S(1)} %get-tuple-element.132), channel_id=1, source_target_pairs={{0,1},{1,0},{2,3},{3,2},{4,5},{5,4},{6,7},{7,6},{8,9},{9,8},{10,11... | collective-permute-start | bytes 1572872 | tf_op jit(solution)/shard_map/ppermute | solution.py:521
